TPU v7x, 32 devices: a whole 2x2x4 slice. The times are simulated.
32 devices in a mesh: ctx: 8 (over z, core), fsdp: 4 (over y, x).
Axes of the slice: x: 2, y: 2, z: 4, core: 2. Of those that a mesh axis runs over, the one named last changes fastest.
Arguments:
- hidden: bfloat16 [4, 1024, 2048], P('fsdp', 'ctx'), may hold values from -8 to 8
- ln1_gain: float32 [2048], P('fsdp'), may hold values from 0.5 to 1.5
- ln1_bias: float32 [2048], P('fsdp'), may hold values from -1.75 to 1.75
- qkv_weight: bfloat16 [2048, 6144], P('fsdp'), may hold values from -0.125 to 0.125
- qkv_bias: float32 [6144], P('fsdp'), may hold values from -1.75 to 1.75
- dense_weight: bfloat16 [2048, 2048], P('fsdp'), may hold values from -0.75 to 0.75
- dense_bias: float32 [2048], P('fsdp'), may hold values from -1.75 to 1.75
- ln2_gain: float32 [2048], P('fsdp'), may hold values from 0.5 to 1.5
- ln2_bias: float32 [2048], P('fsdp'), may hold values from -1.75 to 1.75
- fc1_weight: bfloat16 [2048, 8192], P('fsdp'), may hold values from -0.125 to 0.125
- fc1_bias: float32 [8192], P('fsdp'), may hold values from -1.75 to 1.75
- fc2_weight: bfloat16 [8192, 2048], P('fsdp'), may hold values from -0.0625 to 0.0625
- fc2_bias: float32 [2048], P('fsdp'), may hold values from -1.75 to 1.75
- segments: int32 [4, 1024], P('fsdp', 'ctx'), may hold values from 0 to 6, as said below
- out_grad: bfloat16 [4, 1024, 2048], P('fsdp', 'ctx'), may hold values from -6 to 6
Outputs:
- layer_output: bfloat16 [4, 1024, 2048], P('fsdp', 'ctx')
- input_grad: bfloat16 [4, 1024, 2048], P('fsdp', 'ctx')
- ln1_gain_grad: float32 [2048], P('fsdp')
- ln1_bias_grad: float32 [2048], P('fsdp')
- qkv_weight_grad: float32 [2048, 6144], P('fsdp')
- qkv_bias_grad: float32 [6144], P('fsdp')
- dense_weight_grad: float32 [2048, 2048], P('fsdp')
- dense_bias_grad: float32 [2048], P('fsdp')
- ln2_gain_grad: float32 [2048], P('fsdp')
- ln2_bias_grad: float32 [2048], P('fsdp')
- fc1_weight_grad: float32 [2048, 8192], P('fsdp')
- fc1_bias_grad: float32 [8192], P('fsdp')
- fc2_weight_grad: float32 [8192, 2048], P('fsdp')
- fc2_bias_grad: float32 [2048], P('fsdp')
Inputs may be any that keep to these rules, and one draw needn't show every extreme that they name: `segments`: never decreases along a sequence.
All inputs are finite; a program needn't handle non-finite values.
Results may differ from a plain program's by a relative error of at most 0.01.
Values may be sent and summed in bfloat16 or wider, within the bound.
A program may use at most 576 MiB of HBM per device.

v0:
```python
import math

import jax
import jax.numpy as jnp
from jax import lax
from jax.sharding import PartitionSpec as P

HEADS = 8
ROT = 64


def layer_norm(values, gain, shift):
    center = values - jnp.mean(values, axis=-1, keepdims=True)
    spread = jnp.mean(center * center, axis=-1, keepdims=True)
    return center * lax.rsqrt(spread + 1e-05) * gain + shift


def gelu_exact(values):
    return jax.nn.gelu(values, approximate=False)


def rotary_tables(places, width):
    half_rot = width // 2
    freqs = 10000.0 ** (-2.0 * jnp.arange(half_rot, dtype=jnp.float32) / width)
    angles = places.astype(jnp.float32)[:, None] * freqs[None, :]
    return (jnp.cos(angles), jnp.sin(angles))


def rotate(values, cosine, sine):
    half_rot = cosine.shape[-1]
    first = values[..., :half_rot]
    second = values[..., half_rot : 2 * half_rot]
    remain = values[..., 2 * half_rot :]
    cos_b = cosine[:, None, :]
    sin_b = sine[:, None, :]
    return jnp.concatenate(
        [first * cos_b - second * sin_b, second * cos_b + first * sin_b, remain], axis=-1
    )


def contract_rows(left, right):
    return lax.dot_general(
        left, right, (((0,), (0,)), ((), ())), preferred_element_type=jnp.float32
    )


def contract_cols(left, right):
    return lax.dot_general(
        left, right, (((1,), (1,)), ((), ())), preferred_element_type=jnp.float32
    )


def reorder_cols(values, shard_count, ctx_count):
    tokens = values.shape[0]
    return (
        values.reshape(tokens, shard_count, ctx_count, -1).transpose(0, 2, 1, 3).reshape(tokens, -1)
    )


def reorder_vec(values, shard_count, ctx_count):
    return values.reshape(shard_count, ctx_count, -1).transpose(1, 0, 2).reshape(-1)


def rows_product(left, weight):
    return jnp.dot(
        left, lax.all_gather(weight, "fsdp", axis=0, tiled=True), preferred_element_type=jnp.float32
    )


def cols_product(grad, weight):
    return contract_cols(grad, lax.all_gather(weight, "fsdp", axis=0, tiled=True))


def per_device(
    hidden,
    ln1_gain,
    ln1_bias,
    qkv_weight,
    qkv_bias,
    dense_weight,
    dense_bias,
    ln2_gain,
    ln2_bias,
    fc1_weight,
    fc1_bias,
    fc2_weight,
    fc2_bias,
    segments,
    out_grad,
):
    ctx_count = lax.axis_size("ctx")
    shard_count = lax.axis_size("fsdp")
    tokens = hidden.shape[1]
    width = hidden.shape[2]
    length = tokens * ctx_count
    heads = HEADS
    head_dim = width // heads
    factor = head_dim ** (-0.5)
    residual = hidden[0].astype(jnp.float32)
    small = (
        lax.all_gather(ln1_gain, "fsdp", axis=0, tiled=True),
        lax.all_gather(ln1_bias, "fsdp", axis=0, tiled=True),
        lax.all_gather(qkv_bias, "fsdp", axis=0, tiled=True),
        lax.all_gather(dense_bias, "fsdp", axis=0, tiled=True),
        lax.all_gather(ln2_gain, "fsdp", axis=0, tiled=True),
        lax.all_gather(ln2_bias, "fsdp", axis=0, tiled=True),
        lax.all_gather(fc1_bias, "fsdp", axis=0, tiled=True),
        lax.all_gather(fc2_bias, "fsdp", axis=0, tiled=True),
    )
    gain_one, shift_one, joined_shift, dense_shift, gain_two, shift_two, up_shift, down_shift = (
        small
    )
    normed_one = layer_norm(residual, gain_one, shift_one).astype(jnp.bfloat16)
    normed_two = layer_norm(residual, gain_two, shift_two).astype(jnp.bfloat16)
    pieces = (
        lax.all_gather(qkv_weight, "fsdp", axis=0, tiled=True),
        lax.all_gather(fc1_weight, "fsdp", axis=0, tiled=True),
    )
    joined_pre = jnp.dot(normed_one, pieces[0], preferred_element_type=jnp.float32)
    up_pre = jnp.dot(normed_two, pieces[1], preferred_element_type=jnp.float32)
    joined = joined_pre + joined_shift
    up_value = up_pre + up_shift
    activated = gelu_exact(up_value).astype(jnp.bfloat16)
    places = lax.axis_index("ctx") * tokens + jnp.arange(tokens, dtype=jnp.int32)
    cosine, sine = rotary_tables(places, ROT)
    queries = rotate(joined[:, :width].reshape(tokens, heads, head_dim), cosine, sine).astype(
        jnp.bfloat16
    )
    key_local = (
        rotate(joined[:, width : 2 * width].reshape(tokens, heads, head_dim), cosine, sine)
        .astype(jnp.bfloat16)
        .reshape(tokens, width)
    )
    value_local = joined[:, 2 * width :].astype(jnp.bfloat16)
    query_seg = segments[0]
    key_all, value_all, seg_all = (
        lax.all_gather(key_local, "ctx", axis=0, tiled=True),
        lax.all_gather(value_local, "ctx", axis=0, tiled=True),
        lax.all_gather(query_seg, "ctx", axis=0, tiled=True),
    )
    block_rows = math.gcd(length, 1024)
    block_count = length // block_rows
    block_steps = jnp.arange(block_count, dtype=jnp.int32)

    def block_scores(step_index, key_rows, seg_rows):
        offset = step_index * block_rows
        key_part = lax.dynamic_slice_in_dim(key_rows, offset, block_rows, 0).reshape(
            block_rows, heads, head_dim
        )
        seg_part = lax.dynamic_slice_in_dim(seg_rows, offset, block_rows, 0)
        key_place = offset + jnp.arange(block_rows, dtype=jnp.int32)
        allowed = (key_place[None, :] <= places[:, None]) & (
            seg_part[None, :] == query_seg[:, None]
        )
        scores = (
            jnp.einsum("qhd,khd->hqk", queries, key_part, preferred_element_type=jnp.float32)
            * factor
        )
        return (jnp.where(allowed[None], scores, -1e30), allowed, key_part, offset)

    def gather_stats(carry, step_index):
        top, total = carry
        scores, allowed, key_part, offset = block_scores(step_index, key_all, seg_all)
        new_top = jnp.maximum(top, jnp.max(scores, axis=-1))
        terms = jnp.where(allowed[None], jnp.exp(scores - new_top[..., None]), 0.0)
        return ((new_top, total * jnp.exp(top - new_top) + jnp.sum(terms, axis=-1)), None)

    start_stats = (
        jnp.full((heads, tokens), -1e30, jnp.float32),
        jnp.zeros((heads, tokens), jnp.float32),
    )
    (top, total), _ = lax.scan(gather_stats, start_stats, block_steps)
    log_total = top + jnp.log(total)

    def gather_values(acc, step_index):
        scores, allowed, key_part, offset = block_scores(step_index, key_all, seg_all)
        probs = jnp.exp(scores - log_total[..., None]).astype(jnp.bfloat16)
        value_part = lax.dynamic_slice_in_dim(value_all, offset, block_rows, 0).reshape(
            block_rows, heads, head_dim
        )
        return (
            acc + jnp.einsum("hqk,khd->qhd", probs, value_part, preferred_element_type=jnp.float32),
            None,
        )

    attended_f, _ = lax.scan(
        gather_values, jnp.zeros((tokens, heads, head_dim), jnp.float32), block_steps
    )
    attended = attended_f.reshape(tokens, width).astype(jnp.bfloat16)
    branch_sum = rows_product(attended, dense_weight) + rows_product(activated, fc2_weight)
    layer_output = (residual + branch_sum + dense_shift + down_shift).astype(jnp.bfloat16)
    grad_out = out_grad[0]
    d_attended = cols_product(grad_out, dense_weight).astype(jnp.bfloat16)
    d_activated = cols_product(grad_out, fc2_weight)
    _, gelu_back = jax.vjp(gelu_exact, up_value)
    d_up = gelu_back(d_activated)[0].astype(jnp.bfloat16)
    d_out_heads = d_attended.reshape(tokens, heads, head_dim)
    delta = jnp.sum(
        d_attended.astype(jnp.float32).reshape(tokens, heads, head_dim) * attended_f, axis=-1
    ).T

    def grad_block(acc, step_index):
        scores, allowed, key_part, offset = block_scores(step_index, key_all, seg_all)
        probs = jnp.exp(scores - log_total[..., None])
        value_part = lax.dynamic_slice_in_dim(value_all, offset, block_rows, 0).reshape(
            block_rows, heads, head_dim
        )
        d_probs = jnp.einsum(
            "qhd,khd->hqk", d_out_heads, value_part, preferred_element_type=jnp.float32
        )
        d_scores = (probs * (d_probs - delta[..., None])).astype(jnp.bfloat16)
        acc = (
            acc
            + jnp.einsum("hqk,khd->qhd", d_scores, key_part, preferred_element_type=jnp.float32)
            * factor
        )
        d_keys = (
            jnp.einsum("hqk,qhd->khd", d_scores, queries, preferred_element_type=jnp.float32)
            * factor
        )
        d_values = jnp.einsum(
            "hqk,qhd->khd",
            probs.astype(jnp.bfloat16),
            d_out_heads,
            preferred_element_type=jnp.float32,
        )
        return (
            acc,
            jnp.concatenate(
                [d_keys.reshape(block_rows, width), d_values.reshape(block_rows, width)], axis=1
            ),
        )

    d_queries, key_terms = lax.scan(
        grad_block, jnp.zeros((tokens, heads, head_dim), jnp.float32), block_steps
    )
    key_share = lax.psum_scatter(
        key_terms.reshape(length, 2 * width).astype(jnp.bfloat16),
        "ctx",
        scatter_dimension=0,
        tiled=True,
    ).astype(jnp.float32)
    _, unrotate = jax.vjp(
        lambda values: rotate(values, cosine, sine),
        jnp.zeros((tokens, heads, head_dim), jnp.float32),
    )
    d_query_pre = unrotate(d_queries)[0].reshape(tokens, width)
    d_key_pre = unrotate(key_share[:, :width].reshape(tokens, heads, head_dim))[0].reshape(
        tokens, width
    )
    d_joined = jnp.concatenate([d_query_pre, d_key_pre, key_share[:, width:]], axis=1).astype(
        jnp.bfloat16
    )
    pieces = lax.all_gather((qkv_weight, fc1_weight), "fsdp", axis=0, tiled=True)
    d_normed = jnp.stack([contract_cols(d_joined, pieces[0]), contract_cols(d_up, pieces[1])])
    _, norm_back_one = jax.vjp(layer_norm, residual, gain_one, shift_one)
    d_res_one, d_gain_one, d_shift_one = norm_back_one(d_normed[0])
    _, norm_back_two = jax.vjp(layer_norm, residual, gain_two, shift_two)
    d_res_two, d_gain_two, d_shift_two = norm_back_two(d_normed[1])
    input_grad = (
        (grad_out.astype(jnp.float32) + d_res_one + d_res_two)
        .astype(jnp.bfloat16)
        .reshape(1, tokens, width)
    )
    out_total = jnp.sum(grad_out, axis=0, dtype=jnp.float32)
    joined_total = jnp.sum(d_joined, axis=0, dtype=jnp.float32)
    up_total = jnp.sum(d_up, axis=0, dtype=jnp.float32)
    grad_joined = contract_rows(reorder_cols(normed_one, shard_count, ctx_count), d_joined)
    grad_dense = contract_rows(reorder_cols(attended, shard_count, ctx_count), grad_out)
    grad_up = contract_rows(reorder_cols(normed_two, shard_count, ctx_count), d_up)
    grad_down = contract_rows(reorder_cols(activated, shard_count, ctx_count), grad_out)
    shares = (
        lax.psum_scatter(
            reorder_vec(d_gain_one, shard_count, ctx_count),
            ("ctx", "fsdp"),
            scatter_dimension=0,
            tiled=True,
        ),
        lax.psum_scatter(
            reorder_vec(d_shift_one, shard_count, ctx_count),
            ("ctx", "fsdp"),
            scatter_dimension=0,
            tiled=True,
        ),
        lax.psum_scatter(grad_joined, ("ctx", "fsdp"), scatter_dimension=0, tiled=True),
        lax.psum_scatter(
            reorder_vec(joined_total, shard_count, ctx_count),
            ("ctx", "fsdp"),
            scatter_dimension=0,
            tiled=True,
        ),
        lax.psum_scatter(grad_dense, ("ctx", "fsdp"), scatter_dimension=0, tiled=True),
        lax.psum_scatter(
            reorder_vec(out_total, shard_count, ctx_count),
            ("ctx", "fsdp"),
            scatter_dimension=0,
            tiled=True,
        ),
        lax.psum_scatter(
            reorder_vec(d_gain_two, shard_count, ctx_count),
            ("ctx", "fsdp"),
            scatter_dimension=0,
            tiled=True,
        ),
        lax.psum_scatter(
            reorder_vec(d_shift_two, shard_count, ctx_count),
            ("ctx", "fsdp"),
            scatter_dimension=0,
            tiled=True,
        ),
        lax.psum_scatter(grad_up, ("ctx", "fsdp"), scatter_dimension=0, tiled=True),
        lax.psum_scatter(
            reorder_vec(up_total, shard_count, ctx_count),
            ("ctx", "fsdp"),
            scatter_dimension=0,
            tiled=True,
        ),
        lax.psum_scatter(grad_down, ("ctx", "fsdp"), scatter_dimension=0, tiled=True),
        lax.psum_scatter(
            reorder_vec(out_total, shard_count, ctx_count),
            ("ctx", "fsdp"),
            scatter_dimension=0,
            tiled=True,
        ),
    )
    totals = (
        lax.all_gather(shares[0].astype(jnp.bfloat16), "ctx", axis=0, tiled=True).astype(
            jnp.float32
        ),
        lax.all_gather(shares[1].astype(jnp.bfloat16), "ctx", axis=0, tiled=True).astype(
            jnp.float32
        ),
        lax.all_gather(shares[2].astype(jnp.bfloat16), "ctx", axis=0, tiled=True).astype(
            jnp.float32
        ),
        lax.all_gather(shares[3].astype(jnp.bfloat16), "ctx", axis=0, tiled=True).astype(
            jnp.float32
        ),
        lax.all_gather(shares[4].astype(jnp.bfloat16), "ctx", axis=0, tiled=True).astype(
            jnp.float32
        ),
        lax.all_gather(shares[5].astype(jnp.bfloat16), "ctx", axis=0, tiled=True).astype(
            jnp.float32
        ),
        lax.all_gather(shares[6].astype(jnp.bfloat16), "ctx", axis=0, tiled=True).astype(
            jnp.float32
        ),
        lax.all_gather(shares[7].astype(jnp.bfloat16), "ctx", axis=0, tiled=True).astype(
            jnp.float32
        ),
        lax.all_gather(shares[8].astype(jnp.bfloat16), "ctx", axis=0, tiled=True).astype(
            jnp.float32
        ),
        lax.all_gather(shares[9].astype(jnp.bfloat16), "ctx", axis=0, tiled=True).astype(
            jnp.float32
        ),
        lax.all_gather(shares[10].astype(jnp.bfloat16), "ctx", axis=0, tiled=True).astype(
            jnp.float32
        ),
        lax.all_gather(shares[11].astype(jnp.bfloat16), "ctx", axis=0, tiled=True).astype(
            jnp.float32
        ),
    )
    return (
        layer_output.reshape(1, tokens, width),
        input_grad,
        totals[0],
        totals[1],
        totals[2],
        totals[3],
        totals[4],
        totals[5],
        totals[6],
        totals[7],
        totals[8],
        totals[9],
        totals[10],
        totals[11],
    )


def solution(mesh):
    return jax.shard_map(
        per_device,
        mesh=mesh,
        in_specs=(
            P("fsdp", "ctx", None),
            P("fsdp"),
            P("fsdp"),
            P("fsdp", None),
            P("fsdp"),
            P("fsdp", None),
            P("fsdp"),
            P("fsdp"),
            P("fsdp"),
            P("fsdp", None),
            P("fsdp"),
            P("fsdp", None),
            P("fsdp"),
            P("fsdp", "ctx"),
            P("fsdp", "ctx", None),
        ),
        out_specs=(
            P("fsdp", "ctx", None),
            P("fsdp", "ctx", None),
            P("fsdp"),
            P("fsdp"),
            P("fsdp", None),
            P("fsdp"),
            P("fsdp", None),
            P("fsdp"),
            P("fsdp"),
            P("fsdp"),
            P("fsdp", None),
            P("fsdp"),
            P("fsdp", None),
            P("fsdp"),
        ),
        check_vma=False,
    )
```

profile of v0, /device:TPU:0, one launch (start us, length us, event | category | flops | bytes accessed | tf_op | source)
XLA Modules:
  0.0 5044.2 jit_solution(15832396943010406710)
XLA Ops:
  34.6 205.9 %all-gather.20.cloned.1.call-done = bf16[2048,6144]{1,0:T(8,128)(2,1)} async-done(((bf16[512,6144]{1,0:T(8,128)(2,1)}), bf16[2048,6144]{1,0:T(8,128)(2,1)}) %all-gather.20.cloned.1.call-update) | async-done | bytes 25165840 | tf_op jit(solution)/shard_map/all_gather | solution.py:116
  272.0 58.0 %all-gather.26.cloned.1.call-done = bf16[2048,2048]{1,0:T(8,128)(2,1)} async-done(((bf16[512,2048]{1,0:T(8,128)(2,1)}), bf16[2048,2048]{1,0:T(8,128)(2,1)}) %all-gather.26.cloned.1.call-update) | async-done | bytes 8388624 | tf_op jit(solution)/shard_map/all_gather | solution.py:66
  338.7 41.3 all-gather.24.cloned.1.call-done
  387.0 40.4 all-gather.22.cloned.1.call-done
  500.1 52.5 %reduce-scatter.16.cloned.1.call-done = bf16[128,4096]{1,0:T(8,128)(2,1)} async-done(((bf16[1024,4096]{1,0:T(8,128)(2,1)}), bf16[128,4096]{1,0:T(8,128)(2,1)}) %reduce-scatter.16.cloned.1.call-update) | async-done | bytes 1048592
  571.2 22.0 fusion.53
  603.9 246.2 %all-gather.28.cloned.1.call-done = bf16[2048,8192]{1,0:T(8,128)(2,1)} async-done(((bf16[512,8192]{1,0:T(8,128)(2,1)}), bf16[2048,8192]{1,0:T(8,128)(2,1)}) %all-gather.28.cloned.1.call-update) | async-done | bytes 33554448 | tf_op jit(solution)/shard_map/all_gather | solution.py:117
  850.2 21.9 multiply_convert_fusion.2
  872.0 277.2 %all-gather.30.cloned.1.call-done = bf16[8192,2048]{1,0:T(8,128)(2,1)} async-done(((bf16[2048,2048]{1,0:T(8,128)(2,1)}), bf16[8192,2048]{1,0:T(8,128)(2,1)}) %all-gather.30.cloned.1.call-update) | async-done | bytes 33554448 | tf_op jit(solution)/shard_map/all_gather | solution.py:66
  1149.3 26.0 convert_reduce_fusion
  1175.3 26.2 fusion.66
  1208.2 25.0 fusion.30
  1233.3 276.5 %reduce-scatter.10.cloned.1.call-done = f32[64,2048]{1,0:T(8,128)} async-done(((f32[2048,2048]{1,0:T(8,128)}), f32[64,2048]{1,0:T(8,128)}) %reduce-scatter.10.cloned.1.call-update) | async-done | bytes 524304 | tf_op jit(solution)/shard_map/reduce_scatter | solution.py:292
  1511.6 437.7 %reduce-scatter.8.cloned.1.call-done = f32[64,6144]{1,0:T(8,128)} async-done(((f32[2048,6144]{1,0:T(8,128)}), f32[64,6144]{1,0:T(8,128)}) %reduce-scatter.8.cloned.1.call-update) | async-done | bytes 1572880 | tf_op jit(solution)/shard_map/reduce_scatter | solution.py:285
  1951.8 1403.1 %reduce-scatter.12.cloned.1.call-done = f32[64,8192]{1,0:T(8,128)} async-done(((f32[2048,8192]{1,0:T(8,128)}), f32[64,8192]{1,0:T(8,128)}) %reduce-scatter.12.cloned.1.call-update) | async-done | bytes 2097168 | tf_op jit(solution)/shard_map/reduce_scatter | solution.py:311
  3357.6 1404.2 %reduce-scatter.14.cloned.1.call-done = f32[256,2048]{1,0:T(8,128)} async-done(((f32[8192,2048]{1,0:T(8,128)}), f32[256,2048]{1,0:T(8,128)}) %reduce-scatter.14.cloned.1.call-update) | async-done | bytes 2097168 | tf_op jit(solution)/shard_map/reduce_scatter | solution.py:318
  4787.7 14.4 fusion.18
  4802.2 16.6 fusion.65
  4818.9 14.2 fusion.58
  4840.7 41.7 all-reduce.19
  4884.1 16.7 all-reduce.20
  4930.1 12.8 all-gather.36.cloned.1.call-done
  4942.9 12.5 convert_element_type.195
  4955.4 69.6 %all-gather.38.cloned.1.call-done = bf16[2048,2048]{1,0:T(8,128)(2,1)} async-done(((bf16[256,2048]{1,0:T(8,128)(2,1)}), bf16[2048,2048]{1,0:T(8,128)(2,1)}) %all-gather.38.cloned.1.call-update) | async-done | bytes 8388624 | tf_op jit(solution)/shard_map/all_gather | solution.py:357
  (278 shorter events, 265.1 us)
Async XLA Ops:
  7.2 233.2 %all-gather.20.cloned.1.call-start = ((), (), s32[]{:S(2)}) async-start(), calls=%async_computation.5 | async-start | bytes 31457280 | tf_op jit(solution)/shard_map/all_gather | solution.py:116
  8.0 322.0 %all-gather.26.cloned.1.call-start = ((), (), s32[]{:S(2)}) async-start(), calls=%async_computation.8 | async-start | bytes 10485760 | tf_op jit(solution)/shard_map/all_gather | solution.py:66
  8.7 371.2 %all-gather.24.cloned.1.call-start = ((), (), s32[]{:S(2)}) async-start(), calls=%async_computation.7 | async-start | bytes 4718592 | tf_op jit(solution)/shard_map/all_gather | solution.py:137
  26.4 448.3 %copy-start.25 = (f32[4,1,512]{2,1,0:T(1,128)}, f32[4,1,512]{2,1,0:T(1,128)S(1)}, u32[]{:S(2)}) copy-start(f32[4,1,512]{2,1,0:T(1,128)S(1)} %all-gather.1) | copy-start | bytes 24580
  34.5 218.2 %copy-start.21 = (f32[128,32]{1,0:T(8,128)}, f32[128,32]{1,0:T(8,128)S(1)}, u32[]{:S(2)}) copy-start(f32[128,32]{1,0:T(8,128)S(1)} %get-tuple-element.156) | copy-start | bytes 49156
  34.5 218.2 %copy-start.23 = (f32[128,32]{1,0:T(8,128)}, f32[128,32]{1,0:T(8,128)S(1)}, u32[]{:S(2)}) copy-start(f32[128,32]{1,0:T(8,128)S(1)} %get-tuple-element.157) | copy-start | bytes 49156
  257.1 170.3 %all-gather.22.cloned.1.call-start = ((), (), s32[]{:S(2)}) async-start(), calls=%async_computation.6 | async-start | bytes 4718592 | tf_op jit(solution)/shard_map/all_gather | solution.py:138
  259.2 293.4 %reduce-scatter.16.cloned.1.call-start = ((), (), s32[]{:S(2)}) async-start(), calls=%async_computation.19 | async-start | bytes 9437184
  464.1 386.0 %all-gather.28.cloned.1.call-start = ((), (), s32[]{:S(2)}) async-start(), calls=%async_computation.9 | async-start | bytes 41943040 | tf_op jit(solution)/shard_map/all_gather | solution.py:117
  464.7 684.5 %all-gather.30.cloned.1.call-start = ((), (), s32[]{:S(2)}) async-start(), calls=%async_computation.10 | async-start | bytes 41943040 | tf_op jit(solution)/shard_map/all_gather | solution.py:66
  465.5 1044.3 %reduce-scatter.10.cloned.1.call-start = ((), (), s32[]{:S(2)}) async-start(), calls=%async_computation.13 | async-start | bytes 17301504 | tf_op jit(solution)/shard_map/reduce_scatter | solution.py:292
  474.4 1474.9 %reduce-scatter.8.cloned.1.call-start = ((), (), s32[]{:S(2)}) async-start(), calls=%async_computation.11 | async-start | bytes 51904512 | tf_op jit(solution)/shard_map/reduce_scatter | solution.py:285
  491.3 358.9 %copy-start.27 = (f32[4,1,512]{2,1,0:T(1,128)}, f32[4,1,512]{2,1,0:T(1,128)S(1)}, u32[]{:S(2)}) copy-start(f32[4,1,512]{2,1,0:T(1,128)S(1)} %all-gather.4) | copy-start | bytes 24580
  593.2 256.9 %copy-start.31 = (f32[128]{0:T(128)S(1)}, f32[128]{0:T(128)}, u32[]{:S(2)}) copy-start(f32[128]{0:T(128)} %copy-done.29) | copy-start | bytes 1540
  593.3 256.9 %copy-start.36 = (f32[128]{0:T(128)S(1)}, f32[128]{0:T(128)}, u32[]{:S(2)}) copy-start(f32[128]{0:T(128)} %copy-done.34) | copy-start | bytes 1540
  593.3 2761.6 %reduce-scatter.12.cloned.1.call-start = ((), (), s32[]{:S(2)}) async-start(), calls=%async_computation.15 | async-start | bytes 69206016 | tf_op jit(solution)/shard_map/reduce_scatter | solution.py:311
  1201.5 3560.3 %reduce-scatter.14.cloned.1.call-start = ((), (), s32[]{:S(2)}) async-start(), calls=%async_computation.17 | async-start | bytes 69206016 | tf_op jit(solution)/shard_map/reduce_scatter | solution.py:318
  1233.2 3683.5 %all-gather.34.cloned.1.call-start = ((), (), s32[]{:S(2)}) async-start(), calls=%async_computation.14 | async-start | bytes 2359296 | tf_op jit(solution)/shard_map/all_gather | solution.py:339
  1511.6 3409.3 %all-gather.32.cloned.1.call-start = ((), (), s32[]{:S(2)}) async-start(), calls=%async_computation.12 | async-start | bytes 7077888 | tf_op jit(solution)/shard_map/all_gather | solution.py:333
  1951.7 2812.9 %copy-start.51 = (u32[32]{0:T(128)S(1)}, u32[32]{0:T(128)}, u32[]{:S(2)}) copy-start(u32[32]{0:T(128)} %constant.164) | copy-start | bytes 388
  1951.7 2814.8 %copy-start.46 = (f32[512]{0:T(512)S(1)}, f32[512]{0:T(512)}, u32[]{:S(2)}) copy-start(f32[512]{0:T(512)} %param.27) | copy-start | bytes 6148
  1951.7 2821.5 %copy-start.47 = (f32[512]{0:T(512)S(1)}, f32[512]{0:T(512)}, u32[]{:S(2)}) copy-start(f32[512]{0:T(512)} %param.21) | copy-start | bytes 6148
  1951.7 2991.2 %all-gather.36.cloned.1.call-start = ((), (), s32[]{:S(2)}) async-start(), calls=%async_computation.16 | async-start | bytes 9437184 | tf_op jit(solution)/shard_map/all_gather | solution.py:351
  3357.5 1667.4 %all-gather.38.cloned.1.call-start = ((), (), s32[]{:S(2)}) async-start(), calls=%async_computation.18 | async-start | bytes 9437184 | tf_op jit(solution)/shard_map/all_gather | solution.py:357
  (43 other events, 1511.5 us)
Sparse Core Ops, SparseCore 0:
  9.9 230.4 all-gather.19
  242.3 87.5 all-gather.25
  332.1 47.7 all-gather.23
  382.0 45.3 all-gather.21
  464.3 88.3 reduce-scatter.15
  554.3 295.8 all-gather.27
  852.0 297.2 all-gather.29
  1152.1 357.5 reduce-scatter.9
  1516.2 433.0 reduce-scatter.7
  1951.5 1403.3 reduce-scatter.11
  3357.2 1404.5 reduce-scatter.13
  4763.3 29.2 all-gather.33
  4794.8 64.2 all-gather.31
  4861.1 81.7 all-gather.35
  4944.3 80.5 all-gather.37
where the time goes:
time: 5060 us; the launch traced here: 5040 us
  waiting for transfers between devices  4530 us (90%)
  matrix products  223 us (4%)
  blocking collectives  148 us (3%)
  other arithmetic  78.7 us (2%)
    reduce_scatter x1, waiting for transfers between devices, per_device(): lax.psum_scatter(grad_down, ('ctx', 'fsdp'), scatter_dimension=0, tiled=T...  1400 us
    reduce_scatter x1, waiting for transfers between devices, per_device(): lax.psum_scatter(grad_up, ('ctx', 'fsdp'), scatter_dimension=0, tiled=True)  1400 us
    reduce_scatter x1, waiting for transfers between devices, per_device(): lax.psum_scatter(grad_joined, ('ctx', 'fsdp'), scatter_dimension=0, tiled...  438 us
    all_gather x2, waiting for transfers between devices, rows_product(): lax.all_gather(weight, 'fsdp', axis=0, tiled=True)  335 us
    reduce_scatter x1, waiting for transfers between devices, per_device(): lax.psum_scatter(grad_dense, ('ctx', 'fsdp'), scatter_dimension=0, tiled=...  277 us
    all_gather x1, waiting for transfers between devices, per_device(): lax.all_gather(fc1_weight, 'fsdp', axis=0, tiled=True)  246 us
    all_gather x1, waiting for transfers between devices, per_device(): lax.all_gather(qkv_weight, 'fsdp', axis=0, tiled=True)  206 us
  transfers between devices with their start and end apart: 15, of which 13 were waited for; matrix products, arithmetic and copies ran while one was open for 6% of the time, Pallas kernels for 0%

commit v1 on v0

v1 whole, which is shorter than its diff:
```python
import jax
import jax.numpy as jnp
from jax import lax
from jax.sharding import PartitionSpec as P

HEADS = 8
ROT = 64
CORES = 2


def dot(left, right):
    return jnp.dot(left, right, preferred_element_type=jnp.float32)


def dot_rows(left, right):
    return lax.dot_general(
        left, right, (((0,), (0,)), ((), ())), preferred_element_type=jnp.float32
    )


def dot_cols(left, right):
    return lax.dot_general(
        left, right, (((1,), (1,)), ((), ())), preferred_element_type=jnp.float32
    )


def gelu_and_slope(values):
    cdf = 0.5 * (1.0 + lax.erf(values * (0.5**0.5)))
    density = jnp.exp(-0.5 * values * values) * ((2.0 * jnp.pi) ** -0.5)
    return values * cdf, cdf + values * density


def rotary_tables(places, width):
    half_rot = width // 2
    freqs = 10000.0 ** (-2.0 * jnp.arange(half_rot, dtype=jnp.float32) / width)
    angles = places.astype(jnp.float32)[:, None] * freqs[None, :]
    return (jnp.cos(angles), jnp.sin(angles))


def rotate(values, cosine, sine):
    half = cosine.shape[-1]
    first, second, remain = values[:, :half], values[:, half : 2 * half], values[:, 2 * half :]
    return jnp.concatenate(
        [first * cosine - second * sine, second * cosine + first * sine, remain], axis=1
    )


def line_gather(block):
    count = lax.axis_size("ctx")
    chips = count // CORES
    ctx = lax.axis_index("ctx")
    place, core = ctx // CORES, ctx % CORES
    up = down = block
    ups, downs = [], []
    for hop in range(1, chips):
        up = lax.ppermute(
            up,
            "ctx",
            [
                (i * CORES + k, (i + 1) * CORES + k)
                for i in range(hop - 1, chips - 1)
                for k in range(CORES)
            ],
        )
        down = lax.ppermute(
            down,
            "ctx",
            [
                (i * CORES + k, (i - 1) * CORES + k)
                for i in range(1, chips - hop + 1)
                for k in range(CORES)
            ],
        )
        ups.append(up)
        downs.append(down)
    around = jnp.stack(ups[::-1] + [block] + downs)
    mine = lax.dynamic_slice_in_dim(around, chips - 1 - place, chips, 0)
    other = lax.ppermute(mine, "ctx", [(i, i ^ 1) for i in range(count)])
    is_mine = (jnp.arange(CORES) == core).reshape((1, CORES) + (1,) * block.ndim)
    return jnp.where(is_mine, mine[:, None], other[:, None]).reshape((count,) + block.shape)


def gather_fsdp(values, axis=0):
    return lax.all_gather(values, "fsdp", axis=axis, tiled=True)


def scatter_fsdp(values):
    return lax.psum_scatter(values, "fsdp", scatter_dimension=0, tiled=True)


def per_device(
    hidden,
    ln1_gain,
    ln1_bias,
    qkv_weight,
    qkv_bias,
    dense_weight,
    dense_bias,
    ln2_gain,
    ln2_bias,
    fc1_weight,
    fc1_bias,
    fc2_weight,
    fc2_bias,
    segments,
    out_grad,
):
    ctx_count = lax.axis_size("ctx")
    shards = lax.axis_size("fsdp")
    ctx = lax.axis_index("ctx")
    tokens, width = hidden.shape[1], hidden.shape[2]
    length = tokens * ctx_count
    head_dim = width // HEADS
    repeat = ctx_count // HEADS
    head = ctx // repeat
    factor = head_dim ** (-0.5)
    rows = width // shards
    ff = fc1_weight.shape[1]
    units = ff // shards // ctx_count
    bf16, f32 = jnp.bfloat16, jnp.float32

    vectors = [
        ln1_gain, ln1_bias, dense_bias, ln2_gain, ln2_bias, fc2_bias, qkv_bias, fc1_bias
    ]
    packed = lax.all_gather(jnp.concatenate(vectors), "fsdp", axis=0)
    split, at = [], 0
    for vector in vectors:
        split.append(packed[:, at : at + vector.shape[0]].reshape(-1))
        at += vector.shape[0]
    gain_one, shift_one, dense_shift, gain_two, shift_two, down_shift, qkv_shift, up_shift = split
    query_seg = lax.all_gather(segments[0], "ctx", axis=0, tiled=True)

    up_part = lax.dynamic_index_in_dim(
        fc1_weight.reshape(rows, shards, ctx_count, units), ctx, 2, keepdims=False
    ).reshape(rows, shards * units)
    down_part = lax.dynamic_slice_in_dim(fc2_weight, ctx * units, units, 0)
    qkv_part = lax.dynamic_index_in_dim(
        qkv_weight.reshape(rows, 3, HEADS, head_dim), head, 2, keepdims=False
    ).reshape(rows, 3 * head_dim)
    dense_cols = lax.all_to_all(
        dense_weight, "fsdp", split_axis=1, concat_axis=0, tiled=True
    )
    dense_part = lax.dynamic_slice_in_dim(dense_cols, head * head_dim, head_dim, 0)
    up_w = gather_fsdp(up_part)
    down_w = gather_fsdp(down_part)
    qkv_w = gather_fsdp(qkv_part)
    dense_w = gather_fsdp(dense_part, axis=1)

    hidden_all = line_gather(hidden[0]).reshape(length, width)
    grad_all = line_gather(out_grad[0]).reshape(length, width)

    residual = hidden_all.astype(f32)
    center = residual - jnp.mean(residual, axis=-1, keepdims=True)
    spread = lax.rsqrt(jnp.mean(center * center, axis=-1, keepdims=True) + 1e-05)
    scaled = center * spread
    normed_one = (scaled * gain_one + shift_one).astype(bf16)
    normed_two = (scaled * gain_two + shift_two).astype(bf16)

    up_shift_part = lax.dynamic_index_in_dim(
        up_shift.reshape(shards, ctx_count, units), ctx, 1, keepdims=False
    ).reshape(-1)
    up_value = dot(normed_two, up_w) + up_shift_part
    act_f, slope = gelu_and_slope(up_value)
    act = act_f.astype(bf16)
    down_grad = scatter_fsdp(dot_rows(act, grad_all).astype(bf16))
    d_up_f = dot_cols(grad_all, down_w) * slope
    d_up = d_up_f.astype(bf16)
    up_grad = scatter_fsdp(dot_rows(normed_two, d_up).astype(bf16))

    qkv_shift_part = lax.dynamic_index_in_dim(
        qkv_shift.reshape(3, HEADS, head_dim), head, 1, keepdims=False
    ).reshape(-1)
    joined = dot(normed_one, qkv_w) + qkv_shift_part
    places = jnp.arange(length, dtype=jnp.int32)
    cosine, sine = rotary_tables(places, ROT)
    queries = rotate(joined[:, :head_dim], cosine, sine).astype(bf16)
    keys = rotate(joined[:, head_dim : 2 * head_dim], cosine, sine).astype(bf16)
    values = joined[:, 2 * head_dim :].astype(bf16)
    allowed = (places[None, :] <= places[:, None]) & (query_seg[None, :] == query_seg[:, None])
    if repeat > 1:
        allowed = allowed & (places // (length // repeat) == ctx % repeat)[:, None]
    scores = jnp.where(allowed, dot_cols(queries, keys) * factor, -1e30)
    top = jnp.max(scores, axis=-1, keepdims=True)
    terms = jnp.where(allowed, jnp.exp(scores - top), 0.0)
    total = jnp.sum(terms, axis=-1, keepdims=True)
    probs = terms * jnp.where(total > 0.0, 1.0 / total, 0.0)
    probs_low = probs.astype(bf16)
    att_f = dot(probs_low, values)
    att = att_f.astype(bf16)
    partial = dot(att, dense_w) + dot(act, down_w)
    branch = lax.psum_scatter(partial.astype(bf16), "ctx", scatter_dimension=0, tiled=True)
    own = hidden[0].astype(f32)
    layer_output = (own + branch.astype(f32) + dense_shift + down_shift).astype(bf16)

    d_att = dot_cols(grad_all, dense_w).astype(bf16)
    delta = jnp.sum(d_att.astype(f32) * att_f, axis=-1, keepdims=True)
    dense_grad = dot_rows(att, grad_all).astype(bf16)
    d_scores = (probs * (dot_cols(d_att, values) - delta)).astype(bf16)
    d_queries = rotate(dot(d_scores, keys) * factor, cosine, -sine)
    d_keys = rotate(dot_rows(d_scores, queries) * factor, cosine, -sine)
    d_values = dot_rows(probs_low, d_att)
    d_joined = jnp.concatenate([d_queries, d_keys, d_values], axis=1).astype(bf16)
    qkv_grad = dot_rows(normed_one, d_joined).astype(bf16)

    d_one = dot_cols(d_joined, qkv_w)
    d_two = dot_cols(d_up, up_w)
    both = (d_one * gain_one + d_two * gain_two).astype(bf16)
    back = lax.psum_scatter(both, "ctx", scatter_dimension=0, tiled=True).astype(f32)
    own_center = own - jnp.mean(own, axis=-1, keepdims=True)
    own_spread = lax.rsqrt(jnp.mean(own_center * own_center, axis=-1, keepdims=True) + 1e-05)
    own_scaled = own_center * own_spread
    input_part = own_spread * (
        back
        - jnp.mean(back, axis=-1, keepdims=True)
        - own_scaled * jnp.mean(back * own_scaled, axis=-1, keepdims=True)
    )
    input_grad = (out_grad[0].astype(f32) + input_part).astype(bf16)

    first = (ctx == 0).astype(f32)
    columns = jnp.sum(grad_all.astype(f32), axis=0) * first
    joined_sum = jnp.sum(d_joined.astype(f32), axis=0).reshape(3, 1, head_dim)
    joined_full = jnp.where((jnp.arange(HEADS) == head)[None, :, None], joined_sum, 0.0)
    up_sum = jnp.sum(d_up.astype(f32), axis=0).reshape(shards, 1, units)
    up_full = jnp.where((jnp.arange(ctx_count) == ctx)[None, :, None], up_sum, 0.0)
    small = [
        jnp.sum(d_one * scaled, axis=0),
        jnp.sum(d_one, axis=0),
        columns,
        jnp.sum(d_two * scaled, axis=0),
        jnp.sum(d_two, axis=0),
        joined_full,
        up_full,
    ]
    small = jnp.concatenate([piece.reshape(shards, -1) for piece in small], axis=1).astype(bf16)
    small_size = small.shape[1]
    small_rows = -(-small_size // (3 * head_dim * 16)) * 16
    small = jnp.pad(small, ((0, 0), (0, small_rows * 3 * head_dim - small_size)))
    last_grad = scatter_fsdp(
        jnp.concatenate(
            [
                qkv_grad.reshape(shards, rows, 3 * head_dim),
                small.reshape(shards, small_rows, 3 * head_dim),
            ],
            axis=1,
        ).reshape(-1, 3 * head_dim)
    )
    dense_share = scatter_fsdp(
        dense_grad.reshape(head_dim, shards, rows).transpose(1, 0, 2).reshape(-1, rows)
    )

    down_all = line_gather(down_grad).astype(f32).reshape(ctx_count * units, width)
    up_all = (
        line_gather(up_grad)
        .astype(f32)
        .reshape(ctx_count, rows, shards, units)
        .transpose(1, 2, 0, 3)
        .reshape(rows, ff)
    )
    dense_cols_all = line_gather(dense_share)
    if repeat > 1:
        dense_cols_all = jnp.sum(
            dense_cols_all.astype(f32).reshape(HEADS, repeat, head_dim, rows), axis=1
        ).astype(bf16)
    dense_all = lax.all_to_all(
        dense_cols_all.reshape(width, rows), "fsdp", split_axis=0, concat_axis=1, tiled=True
    ).astype(f32)
    last_all = line_gather(last_grad)
    qkv_all = last_all[:, :rows].astype(f32)
    if repeat > 1:
        qkv_all = jnp.sum(qkv_all.reshape(HEADS, repeat, rows, 3 * head_dim), axis=1)
    qkv_all = (
        qkv_all.reshape(HEADS, rows, 3, head_dim).transpose(1, 2, 0, 3).reshape(rows, 3 * width)
    )
    small_all = jnp.sum(last_all[:, rows:].astype(f32), axis=0).reshape(-1)
    sizes = [rows] * 5 + [3 * rows, ff // shards]
    parts, at = [], 0
    for size in sizes:
        parts.append(small_all[at : at + size])
        at += size
    gain_one_grad, shift_one_grad, columns_grad, gain_two_grad, shift_two_grad, joined_grad, up_b_grad = parts
    return (
        layer_output[None],
        input_grad[None],
        gain_one_grad,
        shift_one_grad,
        qkv_all,
        joined_grad,
        dense_all,
        columns_grad,
        gain_two_grad,
        shift_two_grad,
        up_all,
        up_b_grad,
        down_all,
        columns_grad,
    )


def solution(mesh):
    vec, mat, act = P("fsdp"), P("fsdp", None), P("fsdp", "ctx", None)
    return jax.shard_map(
        per_device,
        mesh=mesh,
        in_specs=(
            act, vec, vec, mat, vec, mat, vec, vec, vec, mat, vec, mat, vec, P("fsdp", "ctx"), act
        ),
        out_specs=(act, act, vec, vec, mat, vec, mat, vec, vec, vec, mat, vec, mat, vec),
        check_vma=False,
    )
```

time: 5060 us -> 806 us (0.16)
  waiting for transfers between devices: 4530 us -> 341 us
  blocking collectives: 148 us -> 17.4 us
  local copies, waits for them, and re-layouts: 49.6 us -> 170 us
  matrix products: 223 us -> 105 us
  starting transfers between devices: 0.61 us -> 73.3 us
    reduce_scatter x4 -> x6, waiting for transfers between devices: 3520 us -> 69 us  [the longest x4 69 us: scatter_fsdp(): return lax.psum_scatter(values, 'fsdp', scatter_dimension=0, tiled=True)]
    all_gather x10 -> x4, waiting for transfers between devices: 951 us -> 0.01 us  [gather_fsdp(): return lax.all_gather(values, 'fsdp', axis=axis, tiled=True)]
    ppermute x0 -> x42, waiting for transfers between devices: none -> 246 us  [the longest x18 198 us: line_gather(): lax.ppermute(down, 'ctx', [(i * CORES + k, (i - 1) * CORES + k) for i in...]
    dot_general x18, matrix products: 223 us -> 105 us  [the longest x6 38.4 us: dot(): return jnp.dot(left, right, preferred_element_type=jnp.float32)]
    all_gather x10 -> x2, blocking collectives: 89.2 us -> 17.4 us  [the longest x1 9.03 us: per_device(): packed = lax.all_gather(jnp.concatenate(vectors), 'fsdp', axis=0)]
    ppermute x0 -> x42, starting transfers between devices: none -> 62.5 us  [the longest x18 38.5 us: line_gather(): lax.ppermute(up, 'ctx', [(i * CORES + k, (i + 1) * CORES + k) for i in ra...]
    unnamed x2 -> x0, blocking collectives: 58.4 us -> none
    unnamed x138 -> x125, local copies, waits for them, and re-layouts: 27.5 us -> 84.9 us
  transfers between devices with their start and end apart: 15 -> 54, of which waited for: 13 -> 20; matrix products, arithmetic and copies ran while one was open for 6% -> 41% of each run, Pallas kernels for 0% -> 0%
where the time goes in v1:
time: 806 us; the launch traced here: 797 us
  waiting for transfers between devices  341 us (42%)
  local copies, waits for them, and re-layouts  170 us (21%)
  matrix products  105 us (13%)
  other arithmetic  73.7 us (9%)
  starting transfers between devices  73.3 us (9%)
  blocking collectives  17.4 us (2%)
  between operations  15.8 us (2%)
    ppermute x18, waiting for transfers between devices, line_gather(): lax.ppermute(down, 'ctx', [(i * CORES + k, (i - 1) * CORES + k) for i in...  198 us
    unnamed x125, local copies, waits for them, and re-layouts  84.9 us
    reduce_scatter x4, waiting for transfers between devices, scatter_fsdp(): return lax.psum_scatter(values, 'fsdp', scatter_dimension=0, tiled=True)  69 us
    ppermute x18, waiting for transfers between devices, line_gather(): lax.ppermute(up, 'ctx', [(i * CORES + k, (i + 1) * CORES + k) for i in ra...  48.3 us
    ppermute x18, starting transfers between devices, line_gather(): lax.ppermute(up, 'ctx', [(i * CORES + k, (i + 1) * CORES + k) for i in ra...  38.5 us
    dot_general x6, matrix products, dot(): return jnp.dot(left, right, preferred_element_type=jnp.float32)  38.4 us
    dot_general x6, matrix products, dot_cols(): lax.dot_general(left, right, (((1,), (1,)), ((), ())), preferred_element_...  38.3 us
    dot_general x6, matrix products, dot_rows(): lax.dot_general(left, right, (((0,), (0,)), ((), ())), preferred_element_...  28.6 us
  transfers between devices with their start and end apart: 54, of which 20 were waited for; matrix products, arithmetic and copies ran while one was open for 41% of the time, Pallas kernels for 0%

profile of v1, /device:TPU:0, one launch (start us, length us, event | category | flops | bytes accessed | tf_op | source)
XLA Modules:
  0.0 797.0 jit_solution(13358752330918374183)
XLA Ops:
  16.3 24.9 %all-to-all-done = bf16[512,4,512]{0,2,1:T(8,128)(2,1)S(1)} async-done(((bf16[512,4,512]{0,2,1:T(8,128)(2,1)}), bf16[512,4,512]{0,2,1:T(8,128)(2,1)S(1)}, u32[]{:S(2)}, u32[]{:S(2)}) %all-to-all-start) | async-done | bytes 2097184 | tf_op jit(solution)/shard_map/all_to_all | solution.py:140
  56.1 12.0 %copy.77 = bf16[512,8192]{0,1:T(8,128)(2,1)} copy(bf16[512,8192]{1,0:T(8,128)(2,1)} %param.24) | data formatting | bytes 16777216 | tf_op args[9]
  109.1 10.3 %collective-permute-done.11 = bf16[128,2048]{1,0:T(8,128)(2,1)} collective-permute-done((bf16[128,2048]{1,0:T(8,128)(2,1)S(1)}, bf16[128,2048]{1,0:T(8,128)(2,1)}, u32[]{:S(2)}, u32[]{:S(2)}) %collective-permute-start.11) | collective-permute-done | bytes 524320 | tf_op jit(solution)/shard_map/ppermute | solution.py:65
  120.7 9.6 %collective-permute-done.4 = bf16[128,2048]{1,0:T(8,128)(2,1)} collective-permute-done((bf16[128,2048]{1,0:T(8,128)(2,1)S(1)}, bf16[128,2048]{1,0:T(8,128)(2,1)}, u32[]{:S(2)}, u32[]{:S(2)}) %collective-permute-start.4) | collective-permute-done | bytes 524320 | tf_op jit(solution)/shard_map/ppermute | solution.py:65
  136.2 11.8 %collective-permute-done.5 = bf16[128,2048]{1,0:T(8,128)(2,1)S(1)} collective-permute-done((bf16[128,2048]{1,0:T(8,128)(2,1)}, bf16[128,2048]{1,0:T(8,128)(2,1)S(1)}, u32[]{:S(2)}, u32[]{:S(2)}) %collective-permute-start.5) | collective-permute-done | bytes 524320 | tf_op jit(solution)/shard_map/ppermute | solution.py:65
  226.6 9.2 %fusion.77 = f32[1024,2048]{1,0:T(8,128)} fusion(bf16[1024,768]{0,1:T(8,128)(2,1)} %copy-done.8, bf16[2048,768]{0,1:T(8,128)(2,1)} %all-gather.8.cloned.1.call-done), kind=kOutput, calls=%fused_computation.226 | convolution fusion | flops 3221225472 | bytes 13107200 | tf_op jit(solution)/shard_map/dot_general | solution.py:22
  235.8 11.1 %multiply_convert_fusion.1 = (bf16[1024,1024]{1,0:T(8,128)(2,1)}, f32[1024,1024]{1,0:T(8,128)}) fusion(f32[1024]{0:T(1024)S(1)} %bitcast.269, bf16[1024,2048]{1,0:T(8,128)(2,1)} %get-tuple-element.68, bf16[2048,1024]{0,1:T(8,128)(2,1)} %all-gather.12.cloned.1.call-done), kind=kOutput, calls=%fused_computation.28 | convolution fusion | flops 4301258752 | bytes 14684160 | tf_op jit(solution)/shard_map/dot_general | solution.py:12
  247.0 9.7 %convert_reduce_fusion.2 = (bf16[1024]{0:T(1024)(128)(2,1)S(1)}, bf16[1024,1024]{1,0:T(8,128)(2,1)S(1)}) fusion(f32[1024,1024]{1,0:T(8,128)} %get-tuple-element.95, f32[1024]{0:T(1024)S(1)} %bitcast.270, bf16[1024,2048]{1,0:T(8,128)(2,1)} %bitcast_select_fusion.2, bf16[1024,2048]{1,0:T(8,128)(2,1)} %all-gather.14.cloned.1.call-done), kind=kOutput, calls=%fused_computation.26 | convolution fusion | flops 4308597760 | bytes 14686208 | tf_op jit(solution)/shard_map/dot_general | solution.py:22
  256.7 10.8 %fusion.71 = (bf16[2048]{0:T(1024)(128)(2,1)S(1)}, bf16[2048]{0:T(1024)(128)(2,1)S(1)}, bf16[1024,2048]{1,0:T(8,128)(2,1)}, bf16[2048]{0:T(1024)(128)(2,1)S(1)}, bf16[2048]{0:T(1024)(128)(2,1)S(1)}) fusion(f32[1024]{0:T(1024)S(1)} %bitcast.264, f32[1024]{0:T(1024)S(1)} %bitcast.256, bf16[4,128,2048]{2,1,0:T(8,128)(2,1)} %collective-permute-done.6, ...), kind=kOutput, calls=%fused_computation.220 | convolution fusion | flops 4324319232 | bytes 23110656 | tf_op jit(solution)/shard_map/dot_general | solution.py:22
  324.5 12.9 %collective-permute-done.14 = bf16[528,768]{1,0:T(8,128)(2,1)} collective-permute-done((bf16[528,768]{1,0:T(8,128)(2,1)}, bf16[528,768]{1,0:T(8,128)(2,1)}, u32[]{:S(2)}, u32[]{:S(2)}) %collective-permute-start.14) | collective-permute-done | bytes 811040 | tf_op jit(solution)/shard_map/ppermute | solution.py:56
  339.2 32.5 %reduce-scatter.15.cloned.1.call-done = bf16[512,1024]{1,0:T(8,128)(2,1)} async-done(((bf16[2048,1024]{1,0:T(8,128)(2,1)}), bf16[512,1024]{1,0:T(8,128)(2,1)}) %reduce-scatter.15.cloned.1.call-update) | async-done | bytes 1048592 | tf_op jit(solution)/shard_map/reduce_scatter | solution.py:88
  379.4 11.0 %fusion.76 = f32[1024,2048]{1,0:T(8,128)} fusion(bf16[1024,1024]{1,0:T(8,128)(2,1)} %get-tuple-element.94, bf16[1024,2048]{1,0:T(8,128)(2,1)} %all-gather.14.cloned.1.call-done), kind=kOutput, calls=%fused_computation.225 | convolution fusion | flops 4294967296 | bytes 14680064 | tf_op jit(solution)/shard_map/dot_general | solution.py:12
  391.6 36.4 %reduce-scatter.17.cloned.1.call-done = bf16[256,2048]{1,0:T(8,128)(2,1)} async-done(((bf16[1024,2048]{1,0:T(8,128)(2,1)}), bf16[256,2048]{1,0:T(8,128)(2,1)}) %reduce-scatter.17.cloned.1.call-update) | async-done | bytes 1048592 | tf_op jit(solution)/shard_map/reduce_scatter | solution.py:88
  456.3 16.1 %collective-permute-done.35 = bf16[256,2048]{1,0:T(8,128)(2,1)} collective-permute-done((bf16[256,2048]{1,0:T(8,128)(2,1)}, bf16[256,2048]{1,0:T(8,128)(2,1)}, u32[]{:S(2)}, u32[]{:S(2)}) %collective-permute-start.35) | collective-permute-done | bytes 1048608 | tf_op jit(solution)/shard_map/ppermute | solution.py:56
  487.0 29.8 %collective-permute-done.19 = bf16[528,768]{1,0:T(8,128)(2,1)S(1)} collective-permute-done((bf16[528,768]{1,0:T(8,128)(2,1)}, bf16[528,768]{1,0:T(8,128)(2,1)S(1)}, u32[]{:S(2)}, u32[]{:S(2)}) %collective-permute-start.19) | collective-permute-done | bytes 811040 | tf_op jit(solution)/shard_map/ppermute | solution.py:65
  518.8 34.2 %collective-permute-done.32 = bf16[512,1024]{1,0:T(8,128)(2,1)S(1)} collective-permute-done((bf16[512,1024]{1,0:T(8,128)(2,1)}, bf16[512,1024]{1,0:T(8,128)(2,1)S(1)}, u32[]{:S(2)}, u32[]{:S(2)}) %collective-permute-start.32) | collective-permute-done | bytes 1048608 | tf_op jit(solution)/shard_map/ppermute | solution.py:65
  555.0 42.9 %collective-permute-done.39 = bf16[256,2048]{1,0:T(8,128)(2,1)S(1)} collective-permute-done((bf16[256,2048]{1,0:T(8,128)(2,1)}, bf16[256,2048]{1,0:T(8,128)(2,1)S(1)}, u32[]{:S(2)}, u32[]{:S(2)}) %collective-permute-start.39) | collective-permute-done | bytes 1048608 | tf_op jit(solution)/shard_map/ppermute | solution.py:65
  604.6 19.4 %collective-permute-done.33 = bf16[512,1024]{1,0:T(8,128)(2,1)S(1)} collective-permute-done((bf16[512,1024]{1,0:T(8,128)(2,1)S(1)}, bf16[512,1024]{1,0:T(8,128)(2,1)S(1)}, u32[]{:S(2)}, u32[]{:S(2)}) %collective-permute-start.33) | collective-permute-done | bytes 1048608 | tf_op jit(solution)/shard_map/ppermute | solution.py:65
  629.7 15.4 %collective-permute-done.40 = bf16[256,2048]{1,0:T(8,128)(2,1)S(1)} collective-permute-done((bf16[256,2048]{1,0:T(8,128)(2,1)S(1)}, bf16[256,2048]{1,0:T(8,128)(2,1)S(1)}, u32[]{:S(2)}, u32[]{:S(2)}) %collective-permute-start.40) | collective-permute-done | bytes 1048608 | tf_op jit(solution)/shard_map/ppermute | solution.py:65
  696.9 9.3 %convert_bitcast_fusion.1 = f32[512,3,8,256]{0,3,1,2:T(8,128)} fusion(bf16[8,512,3,256]{1,3,2,0:T(8,128)(2,1)} %bitcast.227), kind=kLoop, calls=%fused_computation.1 | loop fusion | flops 3145728 | bytes 18874368 | tf_op jit(solution)/shard_map/reshape | solution.py:272
  706.2 11.6 %copy.82 = f32[512,3,8,256]{0,3,2,1:T(8,128)} copy(f32[512,3,8,256]{0,3,1,2:T(8,128)} %convert_bitcast_fusion.1) | data formatting | bytes 25165824 | tf_op jit(solution)/shard_map/reshape | solution.py:272
  717.8 12.6 %copy.88 = f32[512,6144]{1,0:T(8,128)} copy(f32[512,6144]{0,1:T(8,128)} %bitcast.224) | data formatting | bytes 25165824
  762.1 17.4 %copy.90 = f32[512,8192]{1,0:T(8,128)} copy(f32[512,8192]{0,1:T(8,128)} %bitcast.223) | data formatting | bytes 33554432
  779.5 9.8 %fusion.2 = f32[2048,2048]{1,0:T(8,128)} fusion(pred[2048]{0:T(1024)(128)(4,1)S(1)} %broadcast_in_dim.316, bf16[4,256,2048]{2,1,0:T(8,128)(2,1)} %collective-permute-done.41, bf16[4,256,2048]{2,1,0:T(8,128)(2,1)} %constant_dynamic-slice_fusion), kind=kLoop, calls=%fused_computation.7 | loop fusion | flops 8388608 | bytes 25167872 | tf_op jit(solution)/shard_map/convert_element_type | solution.py:251
  (336 shorter events, 360.3 us)
Async XLA Ops:
  16.3 165.3 %all-gather.10.cloned.1.call-start = ((), (), s32[]{:S(2)}) async-start(), calls=%async_computation.9 | async-start | bytes 1310720 | tf_op jit(solution)/shard_map/all_gather | solution.py:84
  45.2 149.2 %all-gather.8.cloned.1.call-start = ((), (), s32[]{:S(2)}) async-start(), calls=%async_computation.8 | async-start | bytes 3932160 | tf_op jit(solution)/shard_map/all_gather | solution.py:84
  56.0 179.8 %all-gather.12.cloned.1.call-start = ((), (), s32[]{:S(2)}) async-start(), calls=%async_computation.10 | async-start | bytes 5242880 | tf_op jit(solution)/shard_map/all_gather | solution.py:84
  70.4 176.5 %all-gather.14.cloned.1.call-start = ((), (), s32[]{:S(2)}) async-start(), calls=%async_computation.11 | async-start | bytes 5242880 | tf_op jit(solution)/shard_map/all_gather | solution.py:84
  108.2 183.2 %reduce-scatter.13.cloned.1.call-start = ((), (), s32[]{:S(2)}) async-start(), calls=%async_computation.15 | async-start | bytes 1310720 | tf_op jit(solution)/shard_map/reduce_scatter | solution.py:88
  226.3 90.3 %reduce-scatter.11.cloned.1.call-start = ((), (), s32[]{:S(2)}) async-start(), calls=%async_computation.14 | async-start | bytes 4055040 | tf_op jit(solution)/shard_map/reduce_scatter | solution.py:88
  271.7 100.1 %reduce-scatter.15.cloned.1.call-start = ((), (), s32[]{:S(2)}) async-start(), calls=%async_computation.16 | async-start | bytes 5242880 | tf_op jit(solution)/shard_map/reduce_scatter | solution.py:88
  280.6 147.5 %reduce-scatter.17.cloned.1.call-start = ((), (), s32[]{:S(2)}) async-start(), calls=%async_computation.17 | async-start | bytes 5242880 | tf_op jit(solution)/shard_map/reduce_scatter | solution.py:88
  290.6 368.1 %reduce-scatter.9.cloned.1.call-start = ((), (), s32[]{:S(2)}) async-start(), calls=%async_computation.13 | async-start | bytes 4718592 | tf_op jit(solution)/shard_map/reduce_scatter | solution.py:208
  291.4 368.9 %reduce-scatter.7.cloned.1.call-start = ((), (), s32[]{:S(2)}) async-start(), calls=%async_computation.12 | async-start | bytes 4718592 | tf_op jit(solution)/shard_map/reduce_scatter | solution.py:191
  371.8 61.9 %collective-permute-start.28 = (bf16[512,1024]{1,0:T(8,128)(2,1)}, bf16[512,1024]{1,0:T(8,128)(2,1)}, u32[]{:S(2)}, u32[]{:S(2)}) collective-permute-start(bf16[512,1024]{1,0:T(8,128)(2,1)} %reduce-scatter.15.cloned.1.call-done), channel_id=1, source_target_pairs={{0,8},{4,12},{8,16},{12,20},{16,24},{20,28},{1,9},{5,13},{9,17},{1... | collective-permute-start | bytes 3145736 | tf_op jit(solution)/shard_map/ppermute | solution.py:56
  377.8 72.3 %collective-permute-start.16 = (bf16[528,768]{1,0:T(8,128)(2,1)}, bf16[528,768]{1,0:T(8,128)(2,1)}, u32[]{:S(2)}, u32[]{:S(2)}) collective-permute-start(bf16[528,768]{1,0:T(8,128)(2,1)} %collective-permute-done.15), channel_id=1, source_target_pairs={{16,24},{20,28},{17,25},{21,29},{18,26},{22,30},{19,27},{23,31}} | collective-permute-start | bytes 2433032 | tf_op jit(solution)/shard_map/ppermute | solution.py:56
  390.3 64.7 %collective-permute-start.31 = (bf16[512,1024]{1,0:T(8,128)(2,1)}, bf16[512,1024]{1,0:T(8,128)(2,1)}, u32[]{:S(2)}, u32[]{:S(2)}) collective-permute-start(bf16[512,1024]{1,0:T(8,128)(2,1)} %reduce-scatter.15.cloned.1.call-done), channel_id=1, source_target_pairs={{8,0},{12,4},{16,8},{20,12},{24,16},{28,20},{9,1},{13,5},{17,9},{2... | collective-permute-start | bytes 3145736 | tf_op jit(solution)/shard_map/ppermute | solution.py:65
  445.4 202.6 %all-to-all-start.1 = ((bf16[4,512,512]{2,1,0:T(8,128)(2,1)}), bf16[4,512,512]{2,1,0:T(8,128)(2,1)}, u32[]{:S(2)}, u32[]{:S(2)}) async-start(bf16[4,512,512]{2,1,0:T(8,128)(2,1)} %bitcast_select_fusion.4), calls=%async_computation.5 | async-start | bytes 4194304 | tf_op jit(solution)/shard_map/all_to_all | solution.py:264
  450.1 66.8 %collective-permute-start.19 = (bf16[528,768]{1,0:T(8,128)(2,1)}, bf16[528,768]{1,0:T(8,128)(2,1)S(1)}, u32[]{:S(2)}, u32[]{:S(2)}) collective-permute-start(bf16[528,768]{1,0:T(8,128)(2,1)} %collective-permute-done.18), channel_id=1, source_target_pairs={{8,0},{12,4},{9,1},{13,5},{10,2},{14,6},{11,3},{15,7}} | collective-permute-start | bytes 2433032 | tf_op jit(solution)/shard_map/ppermute | solution.py:65
  455.0 98.0 %collective-permute-start.32 = (bf16[512,1024]{1,0:T(8,128)(2,1)}, bf16[512,1024]{1,0:T(8,128)(2,1)S(1)}, u32[]{:S(2)}, u32[]{:S(2)}) collective-permute-start(bf16[512,1024]{1,0:T(8,128)(2,1)} %collective-permute-done.31), channel_id=1, source_target_pairs={{8,0},{12,4},{16,8},{20,12},{9,1},{13,5},{17,9},{21,13},{10,2},{14... | collective-permute-start | bytes 3145736 | tf_op jit(solution)/shard_map/ppermute | solution.py:65
  472.4 81.9 %collective-permute-start.36 = (bf16[256,2048]{1,0:T(8,128)(2,1)}, bf16[256,2048]{1,0:T(8,128)(2,1)S(1)}, u32[]{:S(2)}, u32[]{:S(2)}) collective-permute-start(bf16[256,2048]{1,0:T(8,128)(2,1)} %collective-permute-done.35), channel_id=1, source_target_pairs={{8,16},{12,20},{16,24},{20,28},{9,17},{13,21},{17,25},{21,29},{10,... | collective-permute-start | bytes 3145736 | tf_op jit(solution)/shard_map/ppermute | solution.py:56
  482.3 115.6 %collective-permute-start.39 = (bf16[256,2048]{1,0:T(8,128)(2,1)}, bf16[256,2048]{1,0:T(8,128)(2,1)S(1)}, u32[]{:S(2)}, u32[]{:S(2)}) collective-permute-start(bf16[256,2048]{1,0:T(8,128)(2,1)} %collective-permute-done.38), channel_id=1, source_target_pairs={{8,0},{12,4},{16,8},{20,12},{9,1},{13,5},{17,9},{21,13},{10,2},{14... | collective-permute-start | bytes 3145736 | tf_op jit(solution)/shard_map/ppermute | solution.py:65
  483.8 115.4 %collective-permute-start.30 = (bf16[512,1024]{1,0:T(8,128)(2,1)}, bf16[512,1024]{1,0:T(8,128)(2,1)S(1)}, u32[]{:S(2)}, u32[]{:S(2)}) collective-permute-start(bf16[512,1024]{1,0:T(8,128)(2,1)} %collective-permute-done.29), channel_id=1, source_target_pairs={{16,24},{20,28},{17,25},{21,29},{18,26},{22,30},{19,27},{23,31}} | collective-permute-start | bytes 3145736 | tf_op jit(solution)/shard_map/ppermute | solution.py:56
  518.8 156.1 %collective-permute-start.20 = (bf16[4,528,768]{2,1,0:T(8,128)(2,1)}, bf16[4,528,768]{2,1,0:T(8,128)(2,1)}, u32[]{:S(2)}, u32[]{:S(2)}) collective-permute-start(bf16[4,528,768]{2,1,0:T(8,128)(2,1)} %constant_dynamic-slice_fusion.3), channel_id=1, source_target_pairs={{0,4},{4,0},{8,12},{12,8},{16,20},{20,16},{24,28},{28,24},{1,5},{5... | collective-permute-start | bytes 9732104 | tf_op jit(solution)/shard_map/ppermute | solution.py:78
  553.0 71.1 %collective-permute-start.33 = (bf16[512,1024]{1,0:T(8,128)(2,1)S(1)}, bf16[512,1024]{1,0:T(8,128)(2,1)S(1)}, u32[]{:S(2)}, u32[]{:S(2)}) collective-permute-start(bf16[512,1024]{1,0:T(8,128)(2,1)S(1)} %collective-permute-done.32), channel_id=1, source_target_pairs={{8,0},{12,4},{9,1},{13,5},{10,2},{14,6},{11,3},{15,7}} | collective-permute-start | bytes 3145736 | tf_op jit(solution)/shard_map/ppermute | solution.py:65
  554.3 72.3 %collective-permute-start.37 = (bf16[256,2048]{1,0:T(8,128)(2,1)S(1)}, bf16[256,2048]{1,0:T(8,128)(2,1)S(1)}, u32[]{:S(2)}, u32[]{:S(2)}) collective-permute-start(bf16[256,2048]{1,0:T(8,128)(2,1)S(1)} %collective-permute-done.36), channel_id=1, source_target_pairs={{16,24},{20,28},{17,25},{21,29},{18,26},{22,30},{19,27},{23,31}} | collective-permute-start | bytes 3145736 | tf_op jit(solution)/shard_map/ppermute | solution.py:56
  626.6 104.4 %collective-permute-start.34 = (bf16[4,512,1024]{2,1,0:T(8,128)(2,1)}, bf16[4,512,1024]{2,1,0:T(8,128)(2,1)}, u32[]{:S(2)}, u32[]{:S(2)}) collective-permute-start(bf16[4,512,1024]{2,1,0:T(8,128)(2,1)} %constant_dynamic-slice_fusion.1), channel_id=1, source_target_pairs={{0,4},{4,0},{8,12},{12,8},{16,20},{20,16},{24,28},{28,24},{1,5},{5... | collective-permute-start | bytes 12582920 | tf_op jit(solution)/shard_map/ppermute | solution.py:78
  647.5 132.0 %collective-permute-start.41 = (bf16[4,256,2048]{2,1,0:T(8,128)(2,1)}, bf16[4,256,2048]{2,1,0:T(8,128)(2,1)}, u32[]{:S(2)}, u32[]{:S(2)}) collective-permute-start(bf16[4,256,2048]{2,1,0:T(8,128)(2,1)} %constant_dynamic-slice_fusion), channel_id=1, source_target_pairs={{0,4},{4,0},{8,12},{12,8},{16,20},{20,16},{24,28},{28,24},{1,5},{5... | collective-permute-start | bytes 12582920 | tf_op jit(solution)/shard_map/ppermute | solution.py:78
  (57 other events, 1232.7 us)
Sparse Core Ops, SparseCore 0:
  45.3 26.8 all-gather.9
  74.6 43.8 all-gather.7
  120.4 53.4 all-gather.11
  175.5 52.6 all-gather.13
  231.0 27.7 reduce-scatter.12
  271.8 43.3 reduce-scatter.10
  319.1 52.6 reduce-scatter.14
  375.3 52.6 reduce-scatter.16
  431.0 80.6 reduce-scatter.8
  514.6 87.8 reduce-scatter.6

commit v2 on v1

--- a/solution.py
+++ b/solution.py
@@ -1,6 +1,11 @@
+import functools
+import math
+
 import jax
 import jax.numpy as jnp
 from jax import lax
+from jax.experimental import pallas as pl
+from jax.experimental.pallas import tpu as pltpu
 from jax.sharding import PartitionSpec as P
 
 HEADS = 8
@@ -28,6 +33,13 @@
     cdf = 0.5 * (1.0 + lax.erf(values * (0.5**0.5)))
     density = jnp.exp(-0.5 * values * values) * ((2.0 * jnp.pi) ** -0.5)
     return values * cdf, cdf + values * density
+
+
+def centred(values):
+    values = values.astype(jnp.float32)
+    center = values - jnp.mean(values, axis=-1, keepdims=True)
+    spread = lax.rsqrt(jnp.mean(center * center, axis=-1, keepdims=True) + 1e-05)
+    return center * spread, spread
 
 
 def rotary_tables(places, width):
@@ -88,6 +100,507 @@
     return lax.psum_scatter(values, "fsdp", scatter_dimension=0, tiled=True)
 
 
+def remote(src, dst, sems, slot, device):
+    return pltpu.make_async_remote_copy(
+        src_ref=src,
+        dst_ref=dst,
+        send_sem=sems[0].at[slot],
+        recv_sem=sems[1].at[slot],
+        device_id=device,
+        device_id_type=pl.DeviceIdType.MESH,
+    )
+
+
+class Line:
+    def __init__(self, source, blocks, sems, base, place, chips):
+        self.source, self.sems, self.base, self.chips = source, sems, base, chips
+        self.ctx, self.shard = place
+        self.chip = self.ctx // CORES
+        rows = source.shape[0]
+        self.block = lambda index: blocks.at[pl.ds(pl.multiple_of(index * rows, rows), rows)]
+        self.swap_base = base + 2 * (chips - 1)
+        self.own_slot = base + 4 * (chips - 1)
+
+    @staticmethod
+    def slots(chips):
+        return 4 * (chips - 1) + 2
+
+    def hop(self, up, number):
+        step = 1 if up else -1
+        slot = (0 if up else self.chips - 1) + number - 1
+        origin = self.ctx - step * (number - 1) * CORES
+        if up:
+            sends = (self.chip >= number - 1) & (self.chip < self.chips - 1)
+            gets = self.chip >= number
+        else:
+            sends = (self.chip <= self.chips - number) & (self.chip > 0)
+            gets = self.chip <= self.chips - 1 - number
+        return slot, step, origin, sends, gets
+
+    def send(self, up, number):
+        slot, step, origin, sends, _ = self.hop(up, number)
+
+        @pl.when(sends)
+        def _():
+            remote(
+                self.source if number == 1 else self.block(origin),
+                self.block(origin),
+                self.sems,
+                self.base + slot,
+                (self.ctx + step * CORES, self.shard),
+            ).start()
+
+    def start(self):
+        self.send(True, 1)
+        self.send(False, 1)
+        remote(
+            self.source, self.block(self.ctx), self.sems, self.own_slot, (self.ctx ^ 1, self.shard)
+        ).start()
+        self.local = pltpu.make_async_copy(
+            self.source, self.block(self.ctx), self.sems[0].at[self.own_slot + 1]
+        )
+        self.local.start()
+
+    def land(self, number):
+        for up in (True, False):
+            slot, step, origin, _, gets = self.hop(up, number)
+            block = self.block(origin - step * CORES)
+
+            @pl.when(gets)
+            def _(block=block, slot=slot):
+                remote(
+                    block, block, self.sems, self.base + slot, (self.ctx ^ 1, self.shard)
+                ).wait_recv()
+
+            if number < self.chips - 1:
+                self.send(up, number + 1)
+
+            @pl.when(gets)
+            def _(block=block, slot=slot):
+                remote(
+                    block, block, self.sems, self.swap_base + slot, (self.ctx ^ 1, self.shard)
+                ).start()
+
+    def arrived(self):
+        other = self.block(self.ctx ^ 1)
+        remote(other, other, self.sems, self.own_slot, (self.ctx ^ 1, self.shard)).wait_recv()
+        self.local.wait()
+        for up in (True, False):
+            for number in range(1, self.chips):
+                slot, step, origin, _, gets = self.hop(up, number)
+                block = self.block((origin - step * CORES) ^ 1)
+
+                @pl.when(gets)
+                def _(block=block, slot=slot):
+                    remote(
+                        block, block, self.sems, self.swap_base + slot, (self.ctx ^ 1, self.shard)
+                    ).wait_recv()
+
+    def sent(self):
+        source = self.source
+        peer = (self.ctx ^ 1, self.shard)
+        remote(source, source, self.sems, self.own_slot, peer).wait_send()
+        for up in (True, False):
+            for number in range(1, self.chips):
+                slot, _, _, sends, gets = self.hop(up, number)
+
+                @pl.when(sends)
+                def _(slot=slot):
+                    remote(source, source, self.sems, self.base + slot, peer).wait_send()
+
+                @pl.when(gets)
+                def _(slot=slot):
+                    remote(source, source, self.sems, self.swap_base + slot, peer).wait_send()
+
+
+class Square:
+    SLOTS = 8
+
+    def __init__(self, pieces, blocks, sems, base, place):
+        self.pieces, self.sems, self.base = pieces, sems, base
+        self.ctx, self.shard = place
+        half = blocks.shape[0] // 8
+
+        def part(owner, which, columns=slice(None)):
+            start = pl.multiple_of((2 * owner + which) * half, half)
+            return blocks.at[pl.ds(start, half), columns]
+
+        self.part = part
+
+    def to(self, bit):
+        return (self.ctx, self.shard ^ bit)
+
+    def own(self, bit, which):
+        for source, columns in self.pieces(which):
+            remote(
+                source,
+                self.part(self.shard, which, columns),
+                self.sems,
+                self.base + 2 * (bit - 1) + which,
+                self.to(bit),
+            ).start()
+
+    def start(self):
+        self.own(1, 0)
+        self.own(2, 1)
+        self.own(1, 1)
+        self.own(2, 0)
+        for which in (0, 1):
+            for source, columns in self.pieces(which):
+                pltpu.make_async_copy(
+                    source,
+                    self.part(self.shard, which, columns),
+                    self.sems[0].at[self.base + 6 + which],
+                ).start()
+
+    def wait(self, owner, which, slot, bit):
+        part = self.part(owner, which)
+        remote(part, part, self.sems, self.base + slot, self.to(bit)).wait_recv()
+
+    def forward(self):
+        for bit in (1, 2):
+            which = bit - 1
+            owner = self.shard ^ bit
+            self.wait(owner, which, 2 * (bit - 1) + which, bit)
+            part = self.part(owner, which)
+            remote(part, part, self.sems, self.base + 4 + which, self.to(3 - bit)).start()
+
+    def arrived(self):
+        self.wait(self.shard ^ 1, 1, 1, 1)
+        self.wait(self.shard ^ 2, 0, 2, 2)
+        self.wait(self.shard ^ 3, 0, 4, 2)
+        self.wait(self.shard ^ 3, 1, 5, 1)
+        for which in (0, 1):
+            part = self.part(self.shard, which)
+            pltpu.make_async_copy(part, part, self.sems[0].at[self.base + 6 + which]).wait()
+
+    def sent(self):
+        for slot in range(6):
+            part = self.part(self.shard, 0)
+            remote(part, part, self.sems, self.base + slot, self.to(1)).wait_send()
+
+
+class Tree:
+    SLOTS = 8
+
+    def __init__(self, source, block, sems, base, place, owner):
+        self.source, self.block, self.sems, self.base = source, block, sems, base
+        self.ctx, self.shard = place
+        self.turn = self.shard ^ owner
+        self.half = block.shape[0] // 2
+
+    def rows(self, ref, which):
+        return ref.at[pl.ds(which * self.half, self.half)]
+
+    def copy(self, ref, which, slot, bit):
+        return remote(
+            self.rows(ref, which),
+            self.rows(self.block, which),
+            self.sems,
+            self.base + slot,
+            (self.ctx, self.shard ^ bit),
+        )
+
+    def start(self):
+        @pl.when(self.turn == 0)
+        def _():
+            self.copy(self.source, 0, 0, 1).start()
+            self.copy(self.source, 1, 3, 2).start()
+            self.copy(self.source, 1, 1, 1).start()
+            self.copy(self.source, 0, 2, 2).start()
+            pltpu.make_async_copy(self.source, self.block, self.sems[0].at[self.base + 6]).start()
+
+    def forward(self):
+        for bit in (1, 2):
+            which = bit - 1
+
+            @pl.when(self.turn == bit)
+            def _(bit=bit, which=which):
+                self.copy(self.block, which, 2 * (bit - 1) + which, bit).wait_recv()
+                self.copy(self.block, which, 4 + which, 3 - bit).start()
+
+    def arrived(self):
+        @pl.when(self.turn == 0)
+        def _():
+            pltpu.make_async_copy(self.source, self.block, self.sems[0].at[self.base + 6]).wait()
+
+        for bit in (1, 2):
+
+            @pl.when(self.turn == bit)
+            def _(bit=bit):
+                which = 2 - bit
+                self.copy(self.block, which, 2 * (bit - 1) + which, bit).wait_recv()
+
+        @pl.when(self.turn == 3)
+        def _():
+            self.copy(self.block, 0, 4, 2).wait_recv()
+            self.copy(self.block, 1, 5, 1).wait_recv()
+
+    def sent(self):
+        @pl.when(self.turn == 0)
+        def _():
+            for slot in range(4):
+                self.copy(self.block, 0, slot, 1).wait_send()
+
+        for bit in (1, 2):
+
+            @pl.when(self.turn == bit)
+            def _(bit=bit):
+                self.copy(self.block, bit - 1, 3 + bit, 3 - bit).wait_send()
+
+
+TILE = 256
+
+
+def gather_kernel(
+    sizes,
+    hidden, grad, fc1, fc2, qkv, dense, vectors, segs,
+    hidden_out, n1_out, grad_out, qkv_out, dense_out, vec_out, seg_out,
+    down_grad_out, up_grad_out, ff_out, e_out, sums_out,
+    hid, gra, n1, n2, w_up, w_down, vec, act, slope, d_up, down_grad, up_grad, ff, e_two, sums,
+    send_sems, recv_sems, out_sems,
+):
+    chips, shards, units = sizes
+    place = ctx, shard = lax.axis_index("ctx"), lax.axis_index("fsdp")
+    chip, core = ctx // CORES, ctx % CORES
+    sems = (send_sems, recv_sems)
+    width = hidden.shape[1]
+    length = hid.shape[0]
+    ff_units = w_down.shape[0]
+    tiles = length // TILE
+    f32, bf16 = jnp.float32, jnp.bfloat16
+
+    barrier = pltpu.get_barrier_semaphore()
+    peers = [(ctx, shard ^ bit) for bit in (1, 2, 3)]
+    peers += [(lax.rem(ctx + step, CORES * chips), shard) for step in range(1, CORES * chips)]
+    for peer in peers:
+        pl.semaphore_signal(barrier, inc=1, device_id=peer, device_id_type=pl.DeviceIdType.MESH)
+    pl.semaphore_wait(barrier, len(peers))
+
+    base = 0
+    lines = []
+    for source, blocks in ((hidden, hid), (grad, gra)):
+        lines.append(Line(source, blocks, sems, base, place, chips))
+        base += Line.slots(chips)
+    hid_line, gra_line = lines
+    columns = units // shards
+
+    def halves(ref, which, start, size):
+        half = ref.shape[0] // 2
+        return ref.at[pl.ds(which * half, half), pl.ds(pl.multiple_of(start, size), size)]
+
+    def up_pieces(which):
+        stride = fc1.shape[1] // shards
+        return [
+            (
+                halves(fc1, which, index * stride + ctx * columns, columns),
+                pl.ds(index * columns, columns),
+            )
+            for index in range(shards)
+        ]
+
+    def down_pieces(which):
+        half = columns // 2
+        start = pl.multiple_of(ctx * columns + which * half, half)
+        return [(fc2.at[pl.ds(start, half)], slice(None))]
+
+    head_dim = qkv_out.shape[1] // 3
+
+    def qkv_pieces(which):
+        return [
+            (
+                halves(qkv, which, index * width + ctx * head_dim, head_dim),
+                pl.ds(index * head_dim, head_dim),
+            )
+            for index in range(3)
+        ]
+
+    squares = []
+    for pieces, blocks in ((up_pieces, w_up), (down_pieces, w_down), (qkv_pieces, qkv_out)):
+        squares.append(Square(pieces, blocks, sems, base, place))
+        base += Square.SLOTS
+    up_square, down_square, qkv_square = squares
+    heads_here = dense.shape[0] // head_dim
+    dense_rows = dense.at[
+        pl.ds(pl.multiple_of(lax.rem(ctx, heads_here) * head_dim, head_dim), head_dim)
+    ]
+    tree = Tree(dense_rows, dense_out, sems, base, place, ctx // heads_here)
+    base += Tree.SLOTS
+
+    small = []
+    for bit in (1, 2, 3):
+        small.append((remote(vectors, vec.at[shard], sems, base, (ctx, shard ^ bit)), vec.at[shard ^ bit]))
+        base += 1
+    seg_rows = segs.shape[0]
+
+    def seg_block(index):
+        return seg_out.at[pl.ds(pl.multiple_of(index * seg_rows, seg_rows), seg_rows)]
+
+    for step in range(1, CORES * chips):
+        peer = lax.rem(ctx + step, CORES * chips)
+        origin = lax.rem(ctx + CORES * chips - step, CORES * chips)
+        small.append((remote(segs, seg_block(ctx), sems, base, (peer, shard)), seg_block(origin)))
+        base += 1
+    for copy, _ in small:
+        copy.start()
+    own_vec = pltpu.make_async_copy(vectors, vec.at[shard], out_sems.at[0])
+    own_seg = pltpu.make_async_copy(segs, seg_block(ctx), out_sems.at[1])
+    own_vec.start()
+    own_seg.start()
+
+    hid_line.start()
+    up_square.start()
+    hid_line.land(1)
+    up_square.forward()
+    down_square.start()
+    hid_line.land(2)
+    gra_line.start()
+    hid_line.land(3)
+    for slot, (copy, landing) in enumerate(small):
+        remote(landing, landing, sems, base - len(small) + slot, (ctx ^ 1, shard)).wait_recv()
+    own_vec.wait()
+    own_seg.wait()
+    hid_line.arrived()
+
+    def vector(row):
+        return jnp.concatenate([vec[index, row : row + 1] for index in range(shards)], axis=1)
+
+    def rows_of(index):
+        return pl.ds(pl.multiple_of(index * TILE, TILE), TILE)
+
+    def centred(rows):
+        values = hid[rows].astype(f32)
+        center = values - jnp.mean(values, axis=-1, keepdims=True)
+        return center * lax.rsqrt(jnp.mean(center * center, axis=-1, keepdims=True) + 1e-05)
+
+    def loop(body):
+        lax.fori_loop(0, tiles, lambda index, carry: (body(rows_of(index)), carry)[1], 0)
+
+    def norms(rows):
+        scaled = centred(rows)
+        n1[rows] = (scaled * vector(0) + vector(1)).astype(bf16)
+        n2[rows] = (scaled * vector(2) + vector(3)).astype(bf16)
+
+    loop(norms)
+    up_square.arrived()
+    down_square.forward()
+    qkv_square.start()
+    gra_line.land(1)
+
+    row_size = vec.shape[2]
+    bias_start = ctx * columns
+    bias_row = 9 + bias_start // row_size
+    bias_column = pl.multiple_of(lax.rem(bias_start, row_size), columns)
+    bias = jnp.concatenate(
+        [vec[index, pl.ds(bias_row, 1), pl.ds(bias_column, columns)] for index in range(shards)],
+        axis=1,
+    )
+
+    def forward(rows):
+        value = dot(n2[rows], w_up[...]) + bias
+        cdf = 0.5 * (1.0 + lax.erf(value * (0.5**0.5)))
+        density = jnp.exp(-0.5 * value * value) * ((2.0 * math.pi) ** -0.5)
+        act[rows] = (value * cdf).astype(bf16)
+        slope[rows] = cdf + value * density
+
+    loop(forward)
+    gra_line.land(2)
+    down_square.arrived()
+    qkv_square.forward()
+    tree.start()
+
+    def output(rows):
+        ff[rows] = dot(act[rows], w_down[...]).astype(bf16)
+
+    loop(output)
+    gra_line.land(3)
+    gra_line.arrived()
+
+    def backward(rows):
+        d_up[rows] = (dot_cols(gra[rows], w_down[...]) * slope[rows]).astype(bf16)
+
+    loop(backward)
+    tree.forward()
+
+    def fc2_grad(rows):
+        down_grad[rows] = dot_rows(act[:, rows], gra[...]).astype(bf16)
+
+    lax.fori_loop(
+        0, ff_units // TILE, lambda index, carry: (fc2_grad(rows_of(index)), carry)[1], 0
+    )
+
+    def fc1_grad(rows):
+        up_grad[rows] = dot_rows(n2[:, rows], d_up[...]).astype(bf16)
+
+    lax.fori_loop(0, width // TILE, lambda index, carry: (fc1_grad(rows_of(index)), carry)[1], 0)
+    sums[...] = jnp.zeros_like(sums)
+
+    def inputs(rows):
+        d_two = dot_cols(d_up[rows], w_up[...])
+        sums[0:1] += jnp.sum(d_two * centred(rows), axis=0, keepdims=True)
+        sums[1:2] += jnp.sum(d_two, axis=0, keepdims=True)
+        sums[2:3] += jnp.sum(gra[rows].astype(f32), axis=0, keepdims=True)
+        sums[3:4, :ff_units] += jnp.sum(d_up[rows].astype(f32), axis=0, keepdims=True)
+        e_two[rows] = (d_two * vector(2)).astype(bf16)
+
+    loop(inputs)
+
+    pairs = (
+        (hid, hidden_out), (n1, n1_out), (gra, grad_out), (vec, vec_out), (down_grad, down_grad_out),
+        (up_grad, up_grad_out), (ff, ff_out), (e_two, e_out), (sums, sums_out),
+    )
+    writes = [
+        pltpu.make_async_copy(src, dst, out_sems.at[index]) for index, (src, dst) in enumerate(pairs)
+    ]
+    for write in writes:
+        write.start()
+    qkv_square.arrived()
+    tree.arrived()
+    for item in lines + squares + [tree]:
+        item.sent()
+    for copy, _ in small:
+        copy.wait_send()
+    for write in writes:
+        write.wait()
+
+
+def gather_and_feed_forward(hidden, grad, fc1, fc2, qkv, dense, vectors, segs):
+    chips, shards = lax.axis_size("ctx") // CORES, lax.axis_size("fsdp")
+    tokens, width = hidden.shape
+    length = tokens * chips * CORES
+    units = fc1.shape[1] // (chips * CORES)
+    head_dim = width // HEADS
+    bf16, f32 = jnp.bfloat16, jnp.float32
+    wide = (length, width)
+    shapes = [
+        (wide, bf16), (wide, bf16), (wide, bf16), ((width, 3 * head_dim), bf16), ((head_dim, width), bf16),
+        ((shards,) + vectors.shape, f32), ((segs.shape[0] * chips * CORES, segs.shape[1]), segs.dtype),
+        ((units, width), bf16), ((width, units), bf16), (wide, bf16), (wide, bf16), ((8, width), f32),
+    ]
+    scratch = [
+        (wide, bf16), (wide, bf16), (wide, bf16), (wide, bf16), ((width, units), bf16), ((units, width), bf16),
+        ((shards,) + vectors.shape, f32), ((length, units), bf16), ((length, units), f32), ((length, units), bf16),
+        ((units, width), bf16), ((width, units), bf16), (wide, bf16), (wide, bf16), ((8, width), f32),
+    ]
+    count = 2 * Line.slots(chips) + 3 * Square.SLOTS + Tree.SLOTS + 3 + CORES * chips - 1
+    return pl.pallas_call(
+        functools.partial(gather_kernel, (chips, shards, units)),
+        out_shape=[jax.ShapeDtypeStruct(shape, kind) for shape, kind in shapes],
+        in_specs=[pl.BlockSpec(memory_space=pl.ANY)] * 8,
+        out_specs=[pl.BlockSpec(memory_space=pl.ANY)] * len(shapes),
+        scratch_shapes=[pltpu.VMEM(shape, kind) for shape, kind in scratch]
+        + [
+            pltpu.SemaphoreType.DMA((count,)),
+            pltpu.SemaphoreType.DMA((count,)),
+            pltpu.SemaphoreType.DMA((9,)),
+        ],
+        compiler_params=pltpu.CompilerParams(
+            collective_id=0, has_side_effects=True, vmem_limit_bytes=60 * 2**20
+        ),
+        name="gather_and_feed_forward",
+    )(hidden, grad, fc1, fc2, qkv, dense, vectors, segs)
+
+
 def per_device(
     hidden,
     ln1_gain,
@@ -119,53 +632,64 @@
     units = ff // shards // ctx_count
     bf16, f32 = jnp.bfloat16, jnp.float32
 
-    vectors = [
-        ln1_gain, ln1_bias, dense_bias, ln2_gain, ln2_bias, fc2_bias, qkv_bias, fc1_bias
-    ]
-    packed = lax.all_gather(jnp.concatenate(vectors), "fsdp", axis=0)
-    split, at = [], 0
-    for vector in vectors:
-        split.append(packed[:, at : at + vector.shape[0]].reshape(-1))
-        at += vector.shape[0]
-    gain_one, shift_one, dense_shift, gain_two, shift_two, down_shift, qkv_shift, up_shift = split
-    query_seg = lax.all_gather(segments[0], "ctx", axis=0, tiled=True)
-
-    up_part = lax.dynamic_index_in_dim(
-        fc1_weight.reshape(rows, shards, ctx_count, units), ctx, 2, keepdims=False
-    ).reshape(rows, shards * units)
-    down_part = lax.dynamic_slice_in_dim(fc2_weight, ctx * units, units, 0)
-    qkv_part = lax.dynamic_index_in_dim(
-        qkv_weight.reshape(rows, 3, HEADS, head_dim), head, 2, keepdims=False
-    ).reshape(rows, 3 * head_dim)
-    dense_cols = lax.all_to_all(
-        dense_weight, "fsdp", split_axis=1, concat_axis=0, tiled=True
-    )
-    dense_part = lax.dynamic_slice_in_dim(dense_cols, head * head_dim, head_dim, 0)
-    up_w = gather_fsdp(up_part)
-    down_w = gather_fsdp(down_part)
-    qkv_w = gather_fsdp(qkv_part)
-    dense_w = gather_fsdp(dense_part, axis=1)
-
-    hidden_all = line_gather(hidden[0]).reshape(length, width)
-    grad_all = line_gather(out_grad[0]).reshape(length, width)
-
-    residual = hidden_all.astype(f32)
-    center = residual - jnp.mean(residual, axis=-1, keepdims=True)
-    spread = lax.rsqrt(jnp.mean(center * center, axis=-1, keepdims=True) + 1e-05)
-    scaled = center * spread
-    normed_one = (scaled * gain_one + shift_one).astype(bf16)
-    normed_two = (scaled * gain_two + shift_two).astype(bf16)
-
-    up_shift_part = lax.dynamic_index_in_dim(
-        up_shift.reshape(shards, ctx_count, units), ctx, 1, keepdims=False
-    ).reshape(-1)
-    up_value = dot(normed_two, up_w) + up_shift_part
-    act_f, slope = gelu_and_slope(up_value)
-    act = act_f.astype(bf16)
-    down_grad = scatter_fsdp(dot_rows(act, grad_all).astype(bf16))
-    d_up_f = dot_cols(grad_all, down_w) * slope
-    d_up = d_up_f.astype(bf16)
-    up_grad = scatter_fsdp(dot_rows(normed_two, d_up).astype(bf16))
+    vectors = jnp.concatenate(
+        [ln1_gain, ln1_bias, ln2_gain, ln2_bias, dense_bias, fc2_bias, qkv_bias, fc1_bias]
+    ).reshape(-1, rows)
+    vectors = jnp.pad(vectors, ((0, -vectors.shape[0] % 8), (0, 0)))
+    if ctx_count == HEADS and shards == 4:
+        (
+            hidden_all, normed_one, grad_all, qkv_w, dense_w, vec, seg_all,
+            down_part_grad, up_part_grad, ff_part, e_two, sums,
+        ) = gather_and_feed_forward(
+            hidden[0], out_grad[0], fc1_weight, fc2_weight, qkv_weight, dense_weight, vectors,
+            jnp.broadcast_to(segments, (8, tokens)),
+        )
+        query_seg = seg_all.reshape(ctx_count, 8, tokens)[:, 0].reshape(-1)
+        gain_two_sum, shift_two_sum, columns = sums[0], sums[1], sums[2]
+        up_sum = sums[3, : shards * units]
+    else:
+        vec = lax.all_gather(vectors, "fsdp", axis=0)
+        query_seg = lax.all_gather(segments[0], "ctx", axis=0, tiled=True)
+        up_part = lax.dynamic_index_in_dim(
+            fc1_weight.reshape(rows, shards, ctx_count, units), ctx, 2, keepdims=False
+        ).reshape(rows, shards * units)
+        down_part = lax.dynamic_slice_in_dim(fc2_weight, ctx * units, units, 0)
+        qkv_part = lax.dynamic_index_in_dim(
+            qkv_weight.reshape(rows, 3, HEADS, head_dim), head, 2, keepdims=False
+        ).reshape(rows, 3 * head_dim)
+        dense_cols = lax.all_to_all(
+            dense_weight, "fsdp", split_axis=1, concat_axis=0, tiled=True
+        )
+        dense_part = lax.dynamic_slice_in_dim(dense_cols, head * head_dim, head_dim, 0)
+        up_w = gather_fsdp(up_part)
+        down_w = gather_fsdp(down_part)
+        qkv_w = gather_fsdp(qkv_part)
+        dense_w = gather_fsdp(dense_part, axis=1)
+        hidden_all = line_gather(hidden[0]).reshape(length, width)
+        grad_all = line_gather(out_grad[0]).reshape(length, width)
+        normed_one = (centred(hidden_all)[0] * vec[:, 0].reshape(-1) + vec[:, 1].reshape(-1)).astype(bf16)
+        scaled = centred(hidden_all)[0]
+        gain_two = vec[:, 2].reshape(-1)
+        normed_two = (scaled * gain_two + vec[:, 3].reshape(-1)).astype(bf16)
+        up_shift = lax.dynamic_index_in_dim(
+            vec[:, 9 : 9 + ff // width].reshape(shards, ctx_count, units), ctx, 1, keepdims=False
+        ).reshape(-1)
+        act_f, slope = gelu_and_slope(dot(normed_two, up_w) + up_shift)
+        act = act_f.astype(bf16)
+        d_up = (dot_cols(grad_all, down_w) * slope).astype(bf16)
+        down_part_grad = dot_rows(act, grad_all).astype(bf16)
+        up_part_grad = dot_rows(normed_two, d_up).astype(bf16)
+        ff_part = dot(act, down_w).astype(bf16)
+        d_two = dot_cols(d_up, up_w)
+        e_two = (d_two * gain_two).astype(bf16)
+        gain_two_sum, shift_two_sum = jnp.sum(d_two * scaled, axis=0), jnp.sum(d_two, axis=0)
+        columns = jnp.sum(grad_all.astype(f32), axis=0)
+        up_sum = jnp.sum(d_up.astype(f32), axis=0)
+    gain_one = vec[:, 0].reshape(-1)
+    dense_shift, down_shift = vec[:, 4].reshape(-1), vec[:, 5].reshape(-1)
+    qkv_shift = vec[:, 6:9].reshape(-1)
+    down_grad = scatter_fsdp(down_part_grad)
+    up_grad = scatter_fsdp(up_part_grad)
 
     qkv_shift_part = lax.dynamic_index_in_dim(
         qkv_shift.reshape(3, HEADS, head_dim), head, 1, keepdims=False
@@ -187,7 +711,7 @@
     probs_low = probs.astype(bf16)
     att_f = dot(probs_low, values)
     att = att_f.astype(bf16)
-    partial = dot(att, dense_w) + dot(act, down_w)
+    partial = dot(att, dense_w) + ff_part.astype(f32)
     branch = lax.psum_scatter(partial.astype(bf16), "ctx", scatter_dimension=0, tiled=True)
     own = hidden[0].astype(f32)
     layer_output = (own + branch.astype(f32) + dense_shift + down_shift).astype(bf16)
@@ -203,12 +727,9 @@
     qkv_grad = dot_rows(normed_one, d_joined).astype(bf16)
 
     d_one = dot_cols(d_joined, qkv_w)
-    d_two = dot_cols(d_up, up_w)
-    both = (d_one * gain_one + d_two * gain_two).astype(bf16)
+    both = (d_one * gain_one + e_two.astype(f32)).astype(bf16)
     back = lax.psum_scatter(both, "ctx", scatter_dimension=0, tiled=True).astype(f32)
-    own_center = own - jnp.mean(own, axis=-1, keepdims=True)
-    own_spread = lax.rsqrt(jnp.mean(own_center * own_center, axis=-1, keepdims=True) + 1e-05)
-    own_scaled = own_center * own_spread
+    own_scaled, own_spread = centred(own)
     input_part = own_spread * (
         back
         - jnp.mean(back, axis=-1, keepdims=True)
@@ -217,17 +738,16 @@
     input_grad = (out_grad[0].astype(f32) + input_part).astype(bf16)
 
     first = (ctx == 0).astype(f32)
-    columns = jnp.sum(grad_all.astype(f32), axis=0) * first
     joined_sum = jnp.sum(d_joined.astype(f32), axis=0).reshape(3, 1, head_dim)
     joined_full = jnp.where((jnp.arange(HEADS) == head)[None, :, None], joined_sum, 0.0)
-    up_sum = jnp.sum(d_up.astype(f32), axis=0).reshape(shards, 1, units)
+    up_sum = up_sum.reshape(shards, 1, units)
     up_full = jnp.where((jnp.arange(ctx_count) == ctx)[None, :, None], up_sum, 0.0)
     small = [
-        jnp.sum(d_one * scaled, axis=0),
+        jnp.sum(d_one * centred(hidden_all)[0], axis=0),
         jnp.sum(d_one, axis=0),
-        columns,
-        jnp.sum(d_two * scaled, axis=0),
-        jnp.sum(d_two, axis=0),
+        columns * first,
+        gain_two_sum,
+        shift_two_sum,
         joined_full,
         up_full,
     ]

time: 806 us -> 758 us (0.940)
  Pallas kernels: 0 us -> 125 us
  matrix products: 105 us -> 40.3 us
  waiting for transfers between devices: 341 us -> 303 us
  local copies, waits for them, and re-layouts: 170 us -> 143 us
  blocking collectives: 17.4 us -> 0 us
  starting transfers between devices: 73.3 us -> 56.8 us
    pallas_call x0 -> x1, Pallas kernels: none -> 125 us  [gather_and_feed_forward(): pl.pallas_call(functools.partial(gather_kernel, (chips, shards, units)),...]
    reduce_scatter x4, waiting for transfers between devices: 69 us -> 112 us  [scatter_fsdp(): return lax.psum_scatter(values, 'fsdp', scatter_dimension=0, tiled=True)]
    ppermute x18 -> x12, waiting for transfers between devices: 198 us -> 169 us  [line_gather(): lax.ppermute(down, 'ctx', [(i * CORES + k, (i - 1) * CORES + k) for i in...]
    ppermute x18 -> x12, waiting for transfers between devices: 48.3 us -> 20.4 us  [line_gather(): lax.ppermute(up, 'ctx', [(i * CORES + k, (i + 1) * CORES + k) for i in ra...]
    dot_general x6 -> x4, matrix products: 38.3 us -> 13.4 us  [dot_cols(): lax.dot_general(left, right, (((1,), (1,)), ((), ())), preferred_element_...]
    all_to_all x1 -> x0, waiting for transfers between devices: 24.9 us -> none  [per_device(): lax.all_to_all(dense_weight, 'fsdp', split_axis=1, concat_axis=0, tiled=T...]
    unnamed x125 -> x120, local copies, waits for them, and re-layouts: 84.9 us -> 62 us
    dot_general x6 -> x4, matrix products: 38.4 us -> 15.8 us  [dot(): return jnp.dot(left, right, preferred_element_type=jnp.float32)]
  transfers between devices with their start and end apart: 54 -> 35, of which waited for: 20 -> 14; matrix products, arithmetic and copies ran while one was open for 41% -> 27% of each run, Pallas kernels for 0% -> 0%
where the time goes in v2:
time: 758 us; the launch traced here: 751 us
  waiting for transfers between devices  303 us (40%)
  local copies, waits for them, and re-layouts  143 us (19%)
  Pallas kernels  125 us (16%)
  other arithmetic  67.9 us (9%)
  starting transfers between devices  56.8 us (7%)
  matrix products  40.3 us (5%)
  between operations  15.4 us (2%)
    ppermute x12, waiting for transfers between devices, line_gather(): lax.ppermute(down, 'ctx', [(i * CORES + k, (i - 1) * CORES + k) for i in...  169 us
    pallas_call x1, Pallas kernels, gather_and_feed_forward(): pl.pallas_call(functools.partial(gather_kernel, (chips, shards, units)),...  125 us
    reduce_scatter x4, waiting for transfers between devices, scatter_fsdp(): return lax.psum_scatter(values, 'fsdp', scatter_dimension=0, tiled=True)  112 us
    unnamed x120, local copies, waits for them, and re-layouts  62 us
    ppermute x12, starting transfers between devices, line_gather(): lax.ppermute(up, 'ctx', [(i * CORES + k, (i + 1) * CORES + k) for i in ra...  36.4 us
    ppermute x12, waiting for transfers between devices, line_gather(): lax.ppermute(up, 'ctx', [(i * CORES + k, (i + 1) * CORES + k) for i in ra...  20.4 us
    dynamic_slice x6, local copies, waits for them, and re-layouts, line_gather(): mine = lax.dynamic_slice_in_dim(around, chips - 1 - place, chips, 0)  19.8 us
    dot_general x4, matrix products, dot(): return jnp.dot(left, right, preferred_element_type=jnp.float32)  15.8 us
  transfers between devices with their start and end apart: 35, of which 14 were waited for; matrix products, arithmetic and copies ran while one was open for 27% of the time, Pallas kernels for 0%

profile of v2, /device:TPU:0, one launch (start us, length us, event | category | flops | bytes accessed | tf_op | source)
XLA Modules:
  0.0 751.4 jit_solution(15430355585056042927)
XLA Ops:
  14.7 125.1 %gather_and_feed_forward.1 = (bf16[1024,2048]{1,0:T(8,128)(2,1)}, bf16[1024,2048]{1,0:T(8,128)(2,1)}, bf16[1024,2048]{1,0:T(8,128)(2,1)}, bf16[2048,768]{1,0:T(8...) custom-call(bf16[128,2048]{1,0:T(8,128)(2,1)} %bitcast.139, ...), custom_call_target="tpu_custom_call" | custom-call | tf_op jit(solution)/shard_map/gather_and_feed_forward/pallas_call | solution.py:586
  150.1 12.6 %fusion.67 = f32[1024]{0:T(1024)S(1)} fusion(f32[1024]{0:T(1024)S(1)} %get-tuple-element.105, f32[1024,1024]{0,1:T(8,128)S(1)} %get-tuple-element.106, s32[1024]{0:T(1024)S(1)} %bitcast.149), kind=kLoop, calls=%fused_computation.176 | loop fusion | flops 8387584 | bytes 4206592 | tf_op jit(solution)/shard_map/reduce_sum | solution.py:709
  187.9 7.0 fusion.68
  210.9 15.1 %collective-permute-start.7 = (bf16[256,512]{1,0:T(8,128)(2,1)}, bf16[256,512]{1,0:T(8,128)(2,1)S(1)}, u32[]{:S(2)}, u32[]{:S(2)}) collective-permute-start(bf16[256,512]{1,0:T(8,128)(2,1)} %reduce-scatter.13.cloned.1.call-done), channel_id=1, source_target_pairs={{0,8},{4,12},{8,16},{12,20},{16,24},{20,28},{1,9},{5,13},{9,17},{1... | collective-permute-start | bytes 786440 | tf_op jit(solution)/shard_map/ppermute | solution.py:68
  248.6 15.2 %reduce-scatter.11.cloned.1.call-done = bf16[528,768]{1,0:T(8,128)(2,1)} async-done(((bf16[2112,768]{1,0:T(8,128)(2,1)}), bf16[528,768]{1,0:T(8,128)(2,1)}) %reduce-scatter.11.cloned.1.call-update) | async-done | bytes 811024 | tf_op jit(solution)/shard_map/reduce_scatter | solution.py:100
  273.0 46.9 %reduce-scatter.15.cloned.1.call-done = bf16[512,1024]{1,0:T(8,128)(2,1)} async-done(((bf16[2048,1024]{1,0:T(8,128)(2,1)}), bf16[512,1024]{1,0:T(8,128)(2,1)}) %reduce-scatter.15.cloned.1.call-update) | async-done | bytes 1048592 | tf_op jit(solution)/shard_map/reduce_scatter | solution.py:100
  329.9 45.4 %reduce-scatter.17.cloned.1.call-done = bf16[256,2048]{1,0:T(8,128)(2,1)} async-done(((bf16[1024,2048]{1,0:T(8,128)(2,1)}), bf16[256,2048]{1,0:T(8,128)(2,1)}) %reduce-scatter.17.cloned.1.call-update) | async-done | bytes 1048592 | tf_op jit(solution)/shard_map/reduce_scatter | solution.py:100
  403.4 16.5 %collective-permute-done.21 = bf16[256,2048]{1,0:T(8,128)(2,1)} collective-permute-done((bf16[256,2048]{1,0:T(8,128)(2,1)}, bf16[256,2048]{1,0:T(8,128)(2,1)}, u32[]{:S(2)}, u32[]{:S(2)}) %collective-permute-start.21) | collective-permute-done | bytes 1048608 | tf_op jit(solution)/shard_map/ppermute | solution.py:68
  420.6 22.4 %collective-permute-done.24 = bf16[256,2048]{1,0:T(8,128)(2,1)} collective-permute-done((bf16[256,2048]{1,0:T(8,128)(2,1)}, bf16[256,2048]{1,0:T(8,128)(2,1)}, u32[]{:S(2)}, u32[]{:S(2)}) %collective-permute-start.24) | collective-permute-done | bytes 1048608 | tf_op jit(solution)/shard_map/ppermute | solution.py:77
  447.5 24.3 %collective-permute-done.5 = bf16[528,768]{1,0:T(8,128)(2,1)S(1)} collective-permute-done((bf16[528,768]{1,0:T(8,128)(2,1)}, bf16[528,768]{1,0:T(8,128)(2,1)S(1)}, u32[]{:S(2)}, u32[]{:S(2)}) %collective-permute-start.5) | collective-permute-done | bytes 811040 | tf_op jit(solution)/shard_map/ppermute | solution.py:77
  473.7 41.5 %collective-permute-done.18 = bf16[512,1024]{1,0:T(8,128)(2,1)S(1)} collective-permute-done((bf16[512,1024]{1,0:T(8,128)(2,1)}, bf16[512,1024]{1,0:T(8,128)(2,1)S(1)}, u32[]{:S(2)}, u32[]{:S(2)}) %collective-permute-start.18) | collective-permute-done | bytes 1048608 | tf_op jit(solution)/shard_map/ppermute | solution.py:77
  517.3 38.7 %collective-permute-done.25 = bf16[256,2048]{1,0:T(8,128)(2,1)S(1)} collective-permute-done((bf16[256,2048]{1,0:T(8,128)(2,1)}, bf16[256,2048]{1,0:T(8,128)(2,1)S(1)}, u32[]{:S(2)}, u32[]{:S(2)}) %collective-permute-start.25) | collective-permute-done | bytes 1048608 | tf_op jit(solution)/shard_map/ppermute | solution.py:77
  561.4 17.1 %collective-permute-done.19 = bf16[512,1024]{1,0:T(8,128)(2,1)S(1)} collective-permute-done((bf16[512,1024]{1,0:T(8,128)(2,1)S(1)}, bf16[512,1024]{1,0:T(8,128)(2,1)S(1)}, u32[]{:S(2)}, u32[]{:S(2)}) %collective-permute-start.19) | collective-permute-done | bytes 1048608 | tf_op jit(solution)/shard_map/ppermute | solution.py:77
  584.1 15.0 %collective-permute-done.26 = bf16[256,2048]{1,0:T(8,128)(2,1)S(1)} collective-permute-done((bf16[256,2048]{1,0:T(8,128)(2,1)S(1)}, bf16[256,2048]{1,0:T(8,128)(2,1)S(1)}, u32[]{:S(2)}, u32[]{:S(2)}) %collective-permute-start.26) | collective-permute-done | bytes 1048608 | tf_op jit(solution)/shard_map/ppermute | solution.py:77
  634.8 7.4 bitcast_select_fusion.1
  651.2 9.3 %convert_bitcast_fusion.1 = f32[512,3,8,256]{0,3,1,2:T(8,128)} fusion(bf16[8,512,3,256]{1,3,2,0:T(8,128)(2,1)} %bitcast.137), kind=kLoop, calls=%fused_computation.1 | loop fusion | flops 3145728 | bytes 18874368 | tf_op jit(solution)/shard_map/reshape | solution.py:792
  660.5 11.6 %copy.70 = f32[512,3,8,256]{0,3,2,1:T(8,128)} copy(f32[512,3,8,256]{0,3,1,2:T(8,128)} %convert_bitcast_fusion.1) | data formatting | bytes 25165824 | tf_op jit(solution)/shard_map/reshape | solution.py:792
  672.1 12.6 %copy.76 = f32[512,6144]{1,0:T(8,128)} copy(f32[512,6144]{0,1:T(8,128)} %bitcast.134) | data formatting | bytes 25165824
  685.3 6.3 copy.74
  691.6 6.5 broadcast_in_dim.251
  702.3 6.6 convert_bitcast_fusion
  709.0 7.5 %copy.75 = f32[512,4,8,256]{0,3,2,1:T(8,128)} copy(f32[512,4,8,256]{0,3,1,2:T(8,128)S(1)} %convert_bitcast_fusion) | data formatting | bytes 33554432 | tf_op jit(solution)/shard_map/reshape | solution.py:777
  716.5 17.4 %copy.78 = f32[512,8192]{1,0:T(8,128)} copy(f32[512,8192]{0,1:T(8,128)} %bitcast.133) | data formatting | bytes 33554432
  733.9 9.8 %fusion.5 = f32[2048,2048]{1,0:T(8,128)} fusion(pred[2048]{0:T(1024)(128)(4,1)S(1)} %broadcast_in_dim.256, bf16[4,256,2048]{2,1,0:T(8,128)(2,1)} %collective-permute-done.27, bf16[4,256,2048]{2,1,0:T(8,128)(2,1)} %constant_dynamic-slice_fusion), kind=kLoop, calls=%fused_computation.10 | loop fusion | flops 8388608 | bytes 25167872 | tf_op jit(solution)/shard_map/convert_element_type | solution.py:771
  (275 shorter events, 198.2 us)
Async XLA Ops:
  7.2 203.8 %reduce-scatter.13.cloned.1.call-start = ((), (), s32[]{:S(2)}) async-start(), calls=%async_computation.10 | async-start | bytes 1310720 | tf_op jit(solution)/shard_map/reduce_scatter | solution.py:100
  168.5 95.4 %reduce-scatter.11.cloned.1.call-start = ((), (), s32[]{:S(2)}) async-start(), calls=%async_computation.9 | async-start | bytes 4055040 | tf_op jit(solution)/shard_map/reduce_scatter | solution.py:100
  204.1 115.7 %reduce-scatter.15.cloned.1.call-start = ((), (), s32[]{:S(2)}) async-start(), calls=%async_computation.11 | async-start | bytes 5242880 | tf_op jit(solution)/shard_map/reduce_scatter | solution.py:100
  204.9 170.5 %reduce-scatter.17.cloned.1.call-start = ((), (), s32[]{:S(2)}) async-start(), calls=%async_computation.12 | async-start | bytes 5242880 | tf_op jit(solution)/shard_map/reduce_scatter | solution.py:100
  205.4 407.6 %reduce-scatter.9.cloned.1.call-start = ((), (), s32[]{:S(2)}) async-start(), calls=%async_computation.8 | async-start | bytes 4718592 | tf_op jit(solution)/shard_map/reduce_scatter | solution.py:731
  206.0 408.5 %reduce-scatter.7.cloned.1.call-start = ((), (), s32[]{:S(2)}) async-start(), calls=%async_computation.7 | async-start | bytes 4718592 | tf_op jit(solution)/shard_map/reduce_scatter | solution.py:715
  263.8 60.4 %collective-permute-start = (bf16[528,768]{1,0:T(8,128)(2,1)}, bf16[528,768]{1,0:T(8,128)(2,1)}, u32[]{:S(2)}, u32[]{:S(2)}) collective-permute-start(bf16[528,768]{1,0:T(8,128)(2,1)} %reduce-scatter.11.cloned.1.call-done), channel_id=1, source_target_pairs={{0,8},{4,12},{8,16},{12,20},{16,24},{20,28},{1,9},{5,13},{9,17},{1... | collective-permute-start | bytes 2433032 | tf_op jit(solution)/shard_map/ppermute | solution.py:68
  272.9 57.0 %collective-permute-start.13 = (bf16[4,256,512]{2,1,0:T(8,128)(2,1)S(1)}, bf16[4,256,512]{2,1,0:T(8,128)(2,1)}, u32[]{:S(2)}, u32[]{:S(2)}) collective-permute-start(bf16[4,256,512]{2,1,0:T(8,128)(2,1)S(1)} %constant_dynamic-slice_fusion.2), channel_id=1, source_target_pairs={{0,4},{4,0},{8,12},{12,8},{16,20},{20,16},{24,28},{28,24},{1,5},{5... | collective-permute-start | bytes 3145736 | tf_op jit(solution)/shard_map/ppermute | solution.py:90
  319.8 61.2 %collective-permute-start.14 = (bf16[512,1024]{1,0:T(8,128)(2,1)}, bf16[512,1024]{1,0:T(8,128)(2,1)}, u32[]{:S(2)}, u32[]{:S(2)}) collective-permute-start(bf16[512,1024]{1,0:T(8,128)(2,1)} %reduce-scatter.15.cloned.1.call-done), channel_id=1, source_target_pairs={{0,8},{4,12},{8,16},{12,20},{16,24},{20,28},{1,9},{5,13},{9,17},{1... | collective-permute-start | bytes 3145736 | tf_op jit(solution)/shard_map/ppermute | solution.py:68
  327.1 70.1 %collective-permute-start.2 = (bf16[528,768]{1,0:T(8,128)(2,1)}, bf16[528,768]{1,0:T(8,128)(2,1)}, u32[]{:S(2)}, u32[]{:S(2)}) collective-permute-start(bf16[528,768]{1,0:T(8,128)(2,1)} %collective-permute-done.1), channel_id=1, source_target_pairs={{16,24},{20,28},{17,25},{21,29},{18,26},{22,30},{19,27},{23,31}} | collective-permute-start | bytes 2433032 | tf_op jit(solution)/shard_map/ppermute | solution.py:68
  328.6 73.4 %collective-permute-start.17 = (bf16[512,1024]{1,0:T(8,128)(2,1)}, bf16[512,1024]{1,0:T(8,128)(2,1)}, u32[]{:S(2)}, u32[]{:S(2)}) collective-permute-start(bf16[512,1024]{1,0:T(8,128)(2,1)} %reduce-scatter.15.cloned.1.call-done), channel_id=1, source_target_pairs={{8,0},{12,4},{16,8},{20,12},{24,16},{28,20},{9,1},{13,5},{17,9},{2... | collective-permute-start | bytes 3145736 | tf_op jit(solution)/shard_map/ppermute | solution.py:77
  379.7 63.2 %collective-permute-start.24 = (bf16[256,2048]{1,0:T(8,128)(2,1)}, bf16[256,2048]{1,0:T(8,128)(2,1)}, u32[]{:S(2)}, u32[]{:S(2)}) collective-permute-start(bf16[256,2048]{1,0:T(8,128)(2,1)} %reduce-scatter.17.cloned.1.call-done), channel_id=1, source_target_pairs={{8,0},{12,4},{16,8},{20,12},{24,16},{28,20},{9,1},{13,5},{17,9},{2... | collective-permute-start | bytes 3145736 | tf_op jit(solution)/shard_map/ppermute | solution.py:77
  381.0 63.2 %collective-permute-start.15 = (bf16[512,1024]{1,0:T(8,128)(2,1)}, bf16[512,1024]{1,0:T(8,128)(2,1)}, u32[]{:S(2)}, u32[]{:S(2)}) collective-permute-start(bf16[512,1024]{1,0:T(8,128)(2,1)} %collective-permute-done.14), channel_id=1, source_target_pairs={{8,16},{12,20},{16,24},{20,28},{9,17},{13,21},{17,25},{21,29},{10,... | collective-permute-start | bytes 3145736 | tf_op jit(solution)/shard_map/ppermute | solution.py:68
  392.6 209.5 %all-to-all-start = ((bf16[4,512,512]{2,1,0:T(8,128)(2,1)}), bf16[4,512,512]{2,1,0:T(8,128)(2,1)}, u32[]{:S(2)}, u32[]{:S(2)}) async-start(bf16[4,512,512]{2,1,0:T(8,128)(2,1)} %bitcast_select_fusion.2), calls=%async_computation.4 | async-start | bytes 4194304 | tf_op jit(solution)/shard_map/all_to_all | solution.py:784
  397.2 74.5 %collective-permute-start.5 = (bf16[528,768]{1,0:T(8,128)(2,1)}, bf16[528,768]{1,0:T(8,128)(2,1)S(1)}, u32[]{:S(2)}, u32[]{:S(2)}) collective-permute-start(bf16[528,768]{1,0:T(8,128)(2,1)} %collective-permute-done.4), channel_id=1, source_target_pairs={{8,0},{12,4},{9,1},{13,5},{10,2},{14,6},{11,3},{15,7}} | collective-permute-start | bytes 2433032 | tf_op jit(solution)/shard_map/ppermute | solution.py:77
  402.1 113.1 %collective-permute-start.18 = (bf16[512,1024]{1,0:T(8,128)(2,1)}, bf16[512,1024]{1,0:T(8,128)(2,1)S(1)}, u32[]{:S(2)}, u32[]{:S(2)}) collective-permute-start(bf16[512,1024]{1,0:T(8,128)(2,1)} %collective-permute-done.17), channel_id=1, source_target_pairs={{8,0},{12,4},{16,8},{20,12},{9,1},{13,5},{17,9},{21,13},{10,2},{14... | collective-permute-start | bytes 3145736 | tf_op jit(solution)/shard_map/ppermute | solution.py:77
  419.9 96.7 %collective-permute-start.22 = (bf16[256,2048]{1,0:T(8,128)(2,1)}, bf16[256,2048]{1,0:T(8,128)(2,1)S(1)}, u32[]{:S(2)}, u32[]{:S(2)}) collective-permute-start(bf16[256,2048]{1,0:T(8,128)(2,1)} %collective-permute-done.21), channel_id=1, source_target_pairs={{8,16},{12,20},{16,24},{20,28},{9,17},{13,21},{17,25},{21,29},{10,... | collective-permute-start | bytes 3145736 | tf_op jit(solution)/shard_map/ppermute | solution.py:68
  442.9 113.0 %collective-permute-start.25 = (bf16[256,2048]{1,0:T(8,128)(2,1)}, bf16[256,2048]{1,0:T(8,128)(2,1)S(1)}, u32[]{:S(2)}, u32[]{:S(2)}) collective-permute-start(bf16[256,2048]{1,0:T(8,128)(2,1)} %collective-permute-done.24), channel_id=1, source_target_pairs={{8,0},{12,4},{16,8},{20,12},{9,1},{13,5},{17,9},{21,13},{10,2},{14... | collective-permute-start | bytes 3145736 | tf_op jit(solution)/shard_map/ppermute | solution.py:77
  444.2 113.0 %collective-permute-start.16 = (bf16[512,1024]{1,0:T(8,128)(2,1)}, bf16[512,1024]{1,0:T(8,128)(2,1)S(1)}, u32[]{:S(2)}, u32[]{:S(2)}) collective-permute-start(bf16[512,1024]{1,0:T(8,128)(2,1)} %collective-permute-done.15), channel_id=1, source_target_pairs={{16,24},{20,28},{17,25},{21,29},{18,26},{22,30},{19,27},{23,31}} | collective-permute-start | bytes 3145736 | tf_op jit(solution)/shard_map/ppermute | solution.py:68
  473.7 155.5 %collective-permute-start.6 = (bf16[4,528,768]{2,1,0:T(8,128)(2,1)}, bf16[4,528,768]{2,1,0:T(8,128)(2,1)}, u32[]{:S(2)}, u32[]{:S(2)}) collective-permute-start(bf16[4,528,768]{2,1,0:T(8,128)(2,1)} %constant_dynamic-slice_fusion.3), channel_id=1, source_target_pairs={{0,4},{4,0},{8,12},{12,8},{16,20},{20,16},{24,28},{28,24},{1,5},{5... | collective-permute-start | bytes 9732104 | tf_op jit(solution)/shard_map/ppermute | solution.py:90
  515.2 63.2 %collective-permute-start.19 = (bf16[512,1024]{1,0:T(8,128)(2,1)S(1)}, bf16[512,1024]{1,0:T(8,128)(2,1)S(1)}, u32[]{:S(2)}, u32[]{:S(2)}) collective-permute-start(bf16[512,1024]{1,0:T(8,128)(2,1)S(1)} %collective-permute-done.18), channel_id=1, source_target_pairs={{8,0},{12,4},{9,1},{13,5},{10,2},{14,6},{11,3},{15,7}} | collective-permute-start | bytes 3145736 | tf_op jit(solution)/shard_map/ppermute | solution.py:77
  516.5 64.5 %collective-permute-start.23 = (bf16[256,2048]{1,0:T(8,128)(2,1)S(1)}, bf16[256,2048]{1,0:T(8,128)(2,1)S(1)}, u32[]{:S(2)}, u32[]{:S(2)}) collective-permute-start(bf16[256,2048]{1,0:T(8,128)(2,1)S(1)} %collective-permute-done.22), channel_id=1, source_target_pairs={{16,24},{20,28},{17,25},{21,29},{18,26},{22,30},{19,27},{23,31}} | collective-permute-start | bytes 3145736 | tf_op jit(solution)/shard_map/ppermute | solution.py:68
  581.0 104.3 %collective-permute-start.20 = (bf16[4,512,1024]{2,1,0:T(8,128)(2,1)}, bf16[4,512,1024]{2,1,0:T(8,128)(2,1)}, u32[]{:S(2)}, u32[]{:S(2)}) collective-permute-start(bf16[4,512,1024]{2,1,0:T(8,128)(2,1)} %constant_dynamic-slice_fusion.1), channel_id=1, source_target_pairs={{0,4},{4,0},{8,12},{12,8},{16,20},{20,16},{24,28},{28,24},{1,5},{5... | collective-permute-start | bytes 12582920 | tf_op jit(solution)/shard_map/ppermute | solution.py:90
  601.6 132.4 %collective-permute-start.27 = (bf16[4,256,2048]{2,1,0:T(8,128)(2,1)}, bf16[4,256,2048]{2,1,0:T(8,128)(2,1)}, u32[]{:S(2)}, u32[]{:S(2)}) collective-permute-start(bf16[4,256,2048]{2,1,0:T(8,128)(2,1)} %constant_dynamic-slice_fusion), channel_id=1, source_target_pairs={{0,4},{4,0},{8,12},{12,8},{16,20},{20,16},{24,28},{28,24},{1,5},{5... | collective-permute-start | bytes 12582920 | tf_op jit(solution)/shard_map/ppermute | solution.py:90
  (48 other events, 768.0 us)
Sparse Core Ops, SparseCore 0:
  168.6 42.3 reduce-scatter.12
  214.8 48.9 reduce-scatter.10
  267.1 52.6 reduce-scatter.14
  322.7 52.6 reduce-scatter.16
  378.2 80.7 reduce-scatter.8
  461.8 87.7 reduce-scatter.6

commit v3 on v2

--- a/solution.py
+++ b/solution.py
@@ -3,6 +3,7 @@
 
 import jax
 import jax.numpy as jnp
+import numpy as np
 from jax import lax
 from jax.experimental import pallas as pl
 from jax.experimental.pallas import tpu as pltpu
@@ -112,12 +113,13 @@
 
 
 class Line:
-    def __init__(self, source, blocks, sems, base, place, chips):
+    def __init__(self, source, blocks, sems, base, place, chips, stride=None, offset=0):
         self.source, self.sems, self.base, self.chips = source, sems, base, chips
         self.ctx, self.shard = place
         self.chip = self.ctx // CORES
         rows = source.shape[0]
-        self.block = lambda index: blocks.at[pl.ds(pl.multiple_of(index * rows, rows), rows)]
+        stride = stride or rows
+        self.block = lambda index: blocks.at[pl.ds(pl.multiple_of(index * stride + offset, rows), rows)]
         self.swap_base = base + 2 * (chips - 1)
         self.own_slot = base + 4 * (chips - 1)
 
@@ -349,41 +351,282 @@
                 self.copy(self.block, bit - 1, 3 + bit, 3 - bit).wait_send()
 
 
+def add_rows(dst, sources):
+    step = 32
+
+    def body(index, carry):
+        rows = pl.ds(pl.multiple_of(index * step, step), step)
+        total = sources[0][rows].astype(jnp.float32)
+        for source in sources[1:]:
+            total += source[rows].astype(jnp.float32)
+        dst[rows] = total.astype(dst.dtype)
+        return carry
+
+    lax.fori_loop(0, dst.shape[0] // step, body, 0)
+
+
+class Fold:
+    SLOTS = 6
+
+    def __init__(self, parts, landing, stage, carry, final, sems, local, base, place):
+        self.parts, self.landing, self.stage, self.carry, self.final = parts, landing, stage, carry, final
+        self.sems, self.local, self.base = sems, local, base
+        self.ctx, self.shard = place
+        self.half = final.shape[0] // 2
+
+    def part(self, owner, which):
+        start = pl.multiple_of((2 * owner + which) * self.half, self.half)
+        return self.parts.at[pl.ds(start, self.half)]
+
+    def landed(self, slot):
+        return self.landing.at[pl.ds(slot * self.half, self.half)]
+
+    def copy(self, src, slot, bit):
+        return remote(
+            src, self.landed(slot), self.sems, self.base + slot, (self.ctx, self.shard ^ bit)
+        )
+
+    def send(self, slot):
+        bit, which = (1, 0) if slot < 2 else (2, 1)
+        owner = self.shard ^ (3 if slot % 2 else bit)
+        self.copy(self.part(owner, which), slot, bit).start()
+
+    def add(self, dst, sources):
+        copies = []
+        for index, source in enumerate(sources):
+            copies.append(
+                pltpu.make_async_copy(source, self.stage.at[index], self.local.at[index])
+            )
+            copies[-1].start()
+        for copy in copies:
+            copy.wait()
+        add_rows(dst, [self.stage.at[index] for index in range(len(sources))])
+
+    def wait(self, slot, bit):
+        self.copy(self.landed(slot), slot, bit).wait_recv()
+
+    def middle(self, which):
+        first, second = (1, 2) if which == 0 else (2, 1)
+        slot = 1 + 2 * which
+        self.wait(slot, first)
+        carry = self.carry.at[which]
+        self.add(carry, [self.part(self.shard ^ second, which), self.landed(slot)])
+        self.copy(carry, 4 + which, second).start()
+
+    def finish(self, which):
+        first, second = (1, 2) if which == 0 else (2, 1)
+        self.wait(2 * which, first)
+        self.wait(4 + which, second)
+        self.add(
+            self.final.at[pl.ds(which * self.half, self.half)],
+            [self.part(self.shard, which), self.landed(2 * which), self.landed(4 + which)],
+        )
+
+    def sent(self):
+        for slot in range(6):
+            self.copy(self.part(self.shard, 0), slot, 1).wait_send()
+
+
+class Sink:
+    def __init__(self, parts, swapped, landing, stage, carry, final, sems, local, base, place, chips):
+        self.parts, self.swapped, self.landing, self.stage = parts, swapped, landing, stage
+        self.carry, self.final, self.sems, self.local, self.base = carry, final, sems, local, base
+        self.ctx, self.shard = place
+        self.chip, self.core, self.chips = self.ctx // CORES, self.ctx % CORES, chips
+        self.rows = final.shape[0]
+
+    @staticmethod
+    def slots(chips):
+        return 2 * (chips - 1) + 1
+
+    def block(self, ref, index):
+        return ref.at[pl.ds(pl.multiple_of(index * self.rows, self.rows), self.rows)]
+
+    def start(self):
+        for chip in range(self.chips):
+            remote(
+                self.block(self.parts, CORES * chip + (self.core ^ 1)),
+                self.block(self.swapped, chip),
+                self.sems,
+                self.base,
+                (self.ctx ^ 1, self.shard),
+            ).start()
+
+    def swap(self):
+        swapped = self.swapped
+        remote(swapped, swapped, self.sems, self.base, (self.ctx ^ 1, self.shard)).wait_recv()
+
+    def hop(self, up, step):
+        place = self.chip if up else self.chips - 1 - self.chip
+        target = place + self.chips - step
+        target = target if up else self.chips - 1 - target
+        slot = (0 if up else self.chips - 1) + step - 1
+        sends = (place + 1 <= step) & (place < self.chips - 1)
+        gets = (place <= step) & (place > 0)
+        return slot, target, sends, gets, place > 0
+
+    def landed(self, slot):
+        return self.landing.at[pl.ds(slot * self.rows, self.rows)]
+
+    def copy(self, up, slot):
+        way = CORES if up else -CORES
+        return remote(
+            self.carry.at[0 if up else 1],
+            self.landed(slot),
+            self.sems,
+            self.base + 1 + slot,
+            (self.ctx + way, self.shard),
+        )
+
+    def load(self, index, source):
+        return pltpu.make_async_copy(source, self.stage.at[index], self.local.at[index])
+
+    def own(self, target):
+        return [
+            self.load(0, self.block(self.parts, CORES * target + self.core)),
+            self.load(1, self.block(self.swapped, target)),
+        ]
+
+    def step(self, number):
+        for up in (True, False):
+            slot, target, sends, _, passes = self.hop(up, number)
+            if number > 1:
+                before, _, sent, gets, _ = self.hop(up, number - 1)
+
+                @pl.when(gets)
+                def _(before=before, up=up):
+                    remote(
+                        self.landed(before), self.landed(before), self.sems, self.base + 1 + before,
+                        (self.ctx ^ 1, self.shard),
+                    ).wait_recv()
+
+                @pl.when(sent)
+                def _(before=before, up=up):
+                    self.copy(up, before).wait_send()
+
+            @pl.when(sends)
+            def _(up=up, slot=slot, target=target, passes=passes):
+                loads = self.own(target)
+                for load in loads:
+                    load.start()
+                carry = self.carry.at[0 if up else 1]
+                stage = self.stage
+                if number > 1:
+
+                    @pl.when(passes)
+                    def _():
+                        more = self.load(2, self.landed(slot - 1))
+                        more.start()
+                        for load in loads + [more]:
+                            load.wait()
+                        add_rows(carry, [stage.at[0], stage.at[1], stage.at[2]])
+
+                    @pl.when(jnp.logical_not(passes))
+                    def _():
+                        for load in loads:
+                            load.wait()
+                        add_rows(carry, [stage.at[0], stage.at[1]])
+                else:
+                    for load in loads:
+                        load.wait()
+                    add_rows(carry, [stage.at[0], stage.at[1]])
+                self.copy(up, slot).start()
+
+    def finish(self, dst, sem):
+        loads = self.own(self.chip)
+        for load in loads:
+            load.start()
+        for load in loads:
+            load.wait()
+        add_rows(self.final, [self.stage.at[0], self.stage.at[1]])
+        for up in (True, False):
+            slot, _, sends, gets, _ = self.hop(up, self.chips - 1)
+
+            @pl.when(gets)
+            def _(slot=slot):
+                landed = self.landed(slot)
+                remote(
+                    landed, landed, self.sems, self.base + 1 + slot, (self.ctx ^ 1, self.shard)
+                ).wait_recv()
+                load = self.load(2, landed)
+                load.start()
+                load.wait()
+                add_rows(self.final, [self.final, self.stage.at[2]])
+
+            @pl.when(sends)
+            def _(up=up, slot=slot):
+                self.copy(up, slot).wait_send()
+
+        swapped = self.swapped
+        remote(swapped, swapped, self.sems, self.base, (self.ctx ^ 1, self.shard)).wait_send()
+        copy = pltpu.make_async_copy(self.final, dst, sem)
+        copy.start()
+        copy.wait()
+
+
 TILE = 256
 
 
-def gather_kernel(
+def block_kernel(
     sizes,
-    hidden, grad, fc1, fc2, qkv, dense, vectors, segs,
-    hidden_out, n1_out, grad_out, qkv_out, dense_out, vec_out, seg_out,
-    down_grad_out, up_grad_out, ff_out, e_out, sums_out,
-    hid, gra, n1, n2, w_up, w_down, vec, act, slope, d_up, down_grad, up_grad, ff, e_two, sums,
-    send_sems, recv_sems, out_sems,
+    hidden, grad, fc1, fc2, qkv, dense, vectors, segs, tables,
+    vec_out, output_out, input_out, down_all, up_all, qkv_all, dense_all, sums_all,
+    down_parts, up_parts, qkv_parts, dense_parts, down_land, up_land, qkv_land, dense_land,
+    out_parts, out_swap, out_land, in_parts, in_swap, in_land, dense_lines,
+    hid, gra, norm, w_up, w_down, w_qkv, w_dense, vec, seg, seg_col, table,
+    act, wide_f, d_up, queries, keys, values, att_f, att, d_keys, d_values, d_joined, sums, sums_got, sums_tot,
+    stage, down_stage, up_stage,
+    down_carry, up_carry, qkv_carry, dense_carry, down_final, up_final, qkv_final, dense_final,
+    out_carry, in_carry, sink_final,
+    send_sems, recv_sems, local_sems,
 ):
-    chips, shards, units = sizes
+    chips, shards, columns = sizes
     place = ctx, shard = lax.axis_index("ctx"), lax.axis_index("fsdp")
     chip, core = ctx // CORES, ctx % CORES
+    count = CORES * chips
     sems = (send_sems, recv_sems)
-    width = hidden.shape[1]
-    length = hid.shape[0]
+    width, length = hidden.shape[1], hid.shape[0]
     ff_units = w_down.shape[0]
+    head_dim = w_dense.shape[0]
+    row_size = vec.shape[2]
     tiles = length // TILE
     f32, bf16 = jnp.float32, jnp.bfloat16
+    factor = head_dim ** (-0.5)
 
     barrier = pltpu.get_barrier_semaphore()
     peers = [(ctx, shard ^ bit) for bit in (1, 2, 3)]
-    peers += [(lax.rem(ctx + step, CORES * chips), shard) for step in range(1, CORES * chips)]
+    peers += [(lax.rem(ctx + step, count), shard) for step in range(1, count)]
     for peer in peers:
         pl.semaphore_signal(barrier, inc=1, device_id=peer, device_id_type=pl.DeviceIdType.MESH)
     pl.semaphore_wait(barrier, len(peers))
 
     base = 0
-    lines = []
-    for source, blocks in ((hidden, hid), (grad, gra)):
-        lines.append(Line(source, blocks, sems, base, place, chips))
-        base += Line.slots(chips)
-    hid_line, gra_line = lines
-    columns = units // shards
+
+    def take(slots):
+        nonlocal base
+        base += slots
+        return base - slots
+
+    def line(source, blocks, stride=None, offset=0):
+        return Line(source, blocks, sems, take(Line.slots(chips)), place, chips, stride, offset)
+
+    def line_pair(final, blocks):
+        half = final.shape[0] // 2
+        return [
+            line(final.at[pl.ds(which * half, half)], blocks, final.shape[0], which * half)
+            for which in (0, 1)
+        ]
+
+    def fold(parts, landing, stage, carry, final):
+        return Fold(
+            parts, landing, stage, carry, final, sems, local_sems.at[pl.ds(4, 4)], take(Fold.SLOTS), place
+        )
+
+    def sink(parts, swapped, landing, carry):
+        return Sink(
+            parts, swapped, landing, down_stage, carry, sink_final, sems, local_sems.at[pl.ds(4, 4)],
+            take(Sink.slots(chips)), place, chips,
+        )
 
     def halves(ref, which, start, size):
         half = ref.shape[0] // 2
@@ -404,8 +647,6 @@
         start = pl.multiple_of(ctx * columns + which * half, half)
         return [(fc2.at[pl.ds(start, half)], slice(None))]
 
-    head_dim = qkv_out.shape[1] // 3
-
     def qkv_pieces(which):
         return [
             (
@@ -415,38 +656,61 @@
             for index in range(3)
         ]
 
-    squares = []
-    for pieces, blocks in ((up_pieces, w_up), (down_pieces, w_down), (qkv_pieces, qkv_out)):
-        squares.append(Square(pieces, blocks, sems, base, place))
-        base += Square.SLOTS
+    hid_line, gra_line = line(hidden, hid), line(grad, gra)
+    squares = [
+        Square(pieces, blocks, sems, take(Square.SLOTS), place)
+        for pieces, blocks in ((up_pieces, w_up), (down_pieces, w_down), (qkv_pieces, w_qkv))
+    ]
     up_square, down_square, qkv_square = squares
     heads_here = dense.shape[0] // head_dim
     dense_rows = dense.at[
         pl.ds(pl.multiple_of(lax.rem(ctx, heads_here) * head_dim, head_dim), head_dim)
     ]
-    tree = Tree(dense_rows, dense_out, sems, base, place, ctx // heads_here)
-    base += Tree.SLOTS
+    tree = Tree(dense_rows, w_dense, sems, take(Tree.SLOTS), place, ctx // heads_here)
+    down_fold = fold(down_parts, down_land, down_stage, down_carry, down_final)
+    up_fold = fold(up_parts, up_land, up_stage, up_carry, up_final)
+    qkv_fold = fold(
+        qkv_parts, qkv_land, up_stage.at[:, :, : 3 * head_dim], qkv_carry, qkv_final
+    )
+    dense_fold = fold(
+        dense_parts, dense_land, down_stage.at[:, :, : width // shards], dense_carry, dense_final
+    )
+    down_lines = line_pair(down_final, down_all)
+    up_lines = line_pair(up_final, up_all)
+    qkv_lines = line_pair(qkv_final, qkv_all)
+    dense_line = line(dense_final, dense_lines)
+    sums_line = line(sums_tot, sums_all)
+    out_sink = sink(out_parts, out_swap, out_land, out_carry)
+    in_sink = sink(in_parts, in_swap, in_land, in_carry)
 
     small = []
+
+    def send_small(src, dst, landing, device):
+        slot = take(1)
+        small.append((remote(src, dst, sems, slot, device), landing, slot))
+
+    seg_rows = segs.shape[0]
+
+    def seg_block(index):
+        return seg.at[pl.ds(pl.multiple_of(index * seg_rows, seg_rows), seg_rows)]
+
     for bit in (1, 2, 3):
-        small.append((remote(vectors, vec.at[shard], sems, base, (ctx, shard ^ bit)), vec.at[shard ^ bit]))
-        base += 1
-    seg_rows = segs.shape[0]
-
-    def seg_block(index):
-        return seg_out.at[pl.ds(pl.multiple_of(index * seg_rows, seg_rows), seg_rows)]
-
-    for step in range(1, CORES * chips):
-        peer = lax.rem(ctx + step, CORES * chips)
-        origin = lax.rem(ctx + CORES * chips - step, CORES * chips)
-        small.append((remote(segs, seg_block(ctx), sems, base, (peer, shard)), seg_block(origin)))
-        base += 1
-    for copy, _ in small:
+        send_small(vectors, vec.at[shard], vec.at[shard ^ bit], (ctx, shard ^ bit))
+    for step in range(1, count):
+        send_small(
+            segs, seg_block(ctx), seg_block(lax.rem(ctx + count - step, count)),
+            (lax.rem(ctx + step, count), shard),
+        )
+    for copy, _, _ in small:
         copy.start()
-    own_vec = pltpu.make_async_copy(vectors, vec.at[shard], out_sems.at[0])
-    own_seg = pltpu.make_async_copy(segs, seg_block(ctx), out_sems.at[1])
-    own_vec.start()
-    own_seg.start()
+    locals_in = [
+        pltpu.make_async_copy(src, dst, local_sems.at[8 + index])
+        for index, (src, dst) in enumerate(
+            ((vectors, vec.at[shard]), (segs, seg_block(ctx)), (tables, table))
+        )
+    ]
+    for copy in locals_in:
+        copy.start()
 
     hid_line.start()
     up_square.start()
@@ -456,10 +720,10 @@
     hid_line.land(2)
     gra_line.start()
     hid_line.land(3)
-    for slot, (copy, landing) in enumerate(small):
-        remote(landing, landing, sems, base - len(small) + slot, (ctx ^ 1, shard)).wait_recv()
-    own_vec.wait()
-    own_seg.wait()
+    for _, landing, slot in small:
+        remote(landing, landing, sems, slot, (ctx ^ 1, shard)).wait_recv()
+    for copy in locals_in:
+        copy.wait()
     hid_line.arrived()
 
     def vector(row):
@@ -468,137 +732,486 @@
     def rows_of(index):
         return pl.ds(pl.multiple_of(index * TILE, TILE), TILE)
 
-    def centred(rows):
-        values = hid[rows].astype(f32)
-        center = values - jnp.mean(values, axis=-1, keepdims=True)
-        return center * lax.rsqrt(jnp.mean(center * center, axis=-1, keepdims=True) + 1e-05)
-
-    def loop(body):
-        lax.fori_loop(0, tiles, lambda index, carry: (body(rows_of(index)), carry)[1], 0)
-
-    def norms(rows):
-        scaled = centred(rows)
-        n1[rows] = (scaled * vector(0) + vector(1)).astype(bf16)
-        n2[rows] = (scaled * vector(2) + vector(3)).astype(bf16)
-
-    loop(norms)
+    def loop(body, steps=tiles):
+        lax.fori_loop(0, steps, lambda index, carry: (body(rows_of(index)), carry)[1], 0)
+
+    def scaled_rows(rows):
+        return centred(hid[rows])[0]
+
+    def norm_two(rows):
+        norm[rows] = (scaled_rows(rows) * vector(2) + vector(3)).astype(bf16)
+
+    def norm_one(rows):
+        norm[rows] = (scaled_rows(rows) * vector(0) + vector(1)).astype(bf16)
+
+    def emit(steps, compute, dst, size):
+        def write(index):
+            slot = lax.rem(index, 2)
+            return pltpu.make_async_copy(
+                stage.at[slot, :, :size], dst.at[rows_of(index)], local_sems.at[slot]
+            )
+
+        def body(index, carry):
+            @pl.when(index >= 2)
+            def _():
+                write(index - 2).wait()
+
+            stage[lax.rem(index, 2), :, :size] = compute(index).astype(bf16)
+            write(index).start()
+            return carry
+
+        lax.fori_loop(0, steps, body, 0)
+        write(steps - 2).wait()
+        write(steps - 1).wait()
+
+    loop(norm_two)
     up_square.arrived()
     down_square.forward()
-    qkv_square.start()
     gra_line.land(1)
 
-    row_size = vec.shape[2]
     bias_start = ctx * columns
     bias_row = 9 + bias_start // row_size
     bias_column = pl.multiple_of(lax.rem(bias_start, row_size), columns)
-    bias = jnp.concatenate(
+    up_bias = jnp.concatenate(
         [vec[index, pl.ds(bias_row, 1), pl.ds(bias_column, columns)] for index in range(shards)],
         axis=1,
     )
 
-    def forward(rows):
-        value = dot(n2[rows], w_up[...]) + bias
+    def feed_forward(rows):
+        value = dot(norm[rows], w_up[...]) + up_bias
         cdf = 0.5 * (1.0 + lax.erf(value * (0.5**0.5)))
         density = jnp.exp(-0.5 * value * value) * ((2.0 * math.pi) ** -0.5)
         act[rows] = (value * cdf).astype(bf16)
-        slope[rows] = cdf + value * density
-
-    loop(forward)
+        wide_f[rows] = cdf + value * density
+
+    loop(feed_forward)
     gra_line.land(2)
     down_square.arrived()
-    qkv_square.forward()
-    tree.start()
-
-    def output(rows):
-        ff[rows] = dot(act[rows], w_down[...]).astype(bf16)
-
-    loop(output)
     gra_line.land(3)
     gra_line.arrived()
 
-    def backward(rows):
-        d_up[rows] = (dot_cols(gra[rows], w_down[...]) * slope[rows]).astype(bf16)
-
-    loop(backward)
+    def fc2_grad(index, carry):
+        owner = shard ^ (3 - index)
+        rows = rows_of(owner)
+        stage[0] = dot_rows(act[:, rows], gra[...]).astype(bf16)
+        write = pltpu.make_async_copy(stage.at[0], down_parts.at[rows], local_sems.at[0])
+        write.start()
+        write.wait()
+        for step, slot in ((0, 1), (1, 2), (2, 0)):
+
+            @pl.when(index == step)
+            def _(slot=slot):
+                down_fold.send(slot)
+
+        return carry
+
+    lax.fori_loop(0, shards, fc2_grad, 0)
+
+    def feed_back(rows):
+        d_up[rows] = (dot_cols(gra[rows], w_down[...]) * wide_f[rows]).astype(bf16)
+
+    loop(feed_back)
+    down_fold.middle(0)
+    down_fold.send(3)
+    emit(
+        width // TILE,
+        lambda index: dot_rows(norm[:, rows_of(index)], d_up[...]),
+        up_parts,
+        ff_units,
+    )
+    down_fold.finish(0)
+    down_lines[0].start()
+    qkv_square.start()
+    loop(norm_one)
+    down_fold.middle(1)
+    down_lines[0].land(1)
+    qkv_square.forward()
+    for slot in (1, 2, 0):
+        up_fold.send(slot)
+    tree.start()
+    down_lines[0].land(2)
+    down_fold.finish(1)
+    down_lines[1].start()
+
+    per = 3 * HEADS // shards
+    bias_parts = []
+    for index in range(3):
+        at = index * HEADS + ctx
+        rest = lax.rem(at, per) * head_dim
+        bias_parts.append(
+            vec[
+                at // per,
+                pl.ds(6 + rest // row_size, 1),
+                pl.ds(pl.multiple_of(lax.rem(rest, row_size), head_dim), head_dim),
+            ]
+        )
+    rotary = table.shape[2]
+
+    def turn(entries, rows, way):
+        first = entries[:, :rotary]
+        first = (
+            first * table[0, rows]
+            + way * (pltpu.roll(first, ROT // 2, 1) * table[1, rows])
+            + way * (pltpu.roll(first, rotary - ROT // 2, 1) * table[2, rows])
+        )
+        return jnp.concatenate([first, entries[:, rotary:]], axis=1)
+
+    def project(rows):
+        joined = dot(norm[rows], w_qkv[...])
+        parts = [
+            joined[:, index * head_dim : (index + 1) * head_dim] + bias_parts[index]
+            for index in range(3)
+        ]
+        queries[rows] = turn(parts[0], rows, 1.0).astype(bf16)
+        keys[rows] = turn(parts[1], rows, 1.0).astype(bf16)
+        values[rows] = parts[2].astype(bf16)
+
+    seg_row = jnp.concatenate(
+        [seg[index * seg_rows : index * seg_rows + 1] for index in range(count)], axis=1
+    )
+    side = segs.shape[1]
+    for index in range(count):
+        block = seg[index * seg_rows : index * seg_rows + 1].astype(f32)
+        seg_col[index * side : (index + 1) * side] = jnp.broadcast_to(block, (side, side)).T
+
+    qkv_square.arrived()
+    loop(project)
+    down_lines[0].land(3)
+    down_lines[1].land(1)
+    up_fold.middle(0)
+    up_fold.send(3)
     tree.forward()
 
-    def fc2_grad(rows):
-        down_grad[rows] = dot_rows(act[:, rows], gra[...]).astype(bf16)
-
-    lax.fori_loop(
-        0, ff_units // TILE, lambda index, carry: (fc2_grad(rows_of(index)), carry)[1], 0
-    )
-
-    def fc1_grad(rows):
-        up_grad[rows] = dot_rows(n2[:, rows], d_up[...]).astype(bf16)
-
-    lax.fori_loop(0, width // TILE, lambda index, carry: (fc1_grad(rows_of(index)), carry)[1], 0)
+    def attend(index):
+        rows = pl.ds(index * TILE, TILE)
+        size = (index + 1) * TILE
+        scores = dot_cols(queries[rows], keys[:size]) * factor
+        query_place = index * TILE + lax.broadcasted_iota(jnp.int32, (TILE, size), 0)
+        key_place = lax.broadcasted_iota(jnp.int32, (TILE, size), 1)
+        same = seg_col[rows][:, :1] == seg_row[:, :size].astype(f32)
+        allowed = (key_place <= query_place) & same
+        scores = jnp.where(allowed, scores, -1e30)
+        terms = jnp.where(
+            allowed, jnp.exp(scores - jnp.max(scores, axis=-1, keepdims=True)), 0.0
+        )
+        probs = terms / jnp.sum(terms, axis=-1, keepdims=True)
+        wide_f[rows, :size] = probs
+        result = dot(probs.astype(bf16), values[:size])
+        att_f[rows] = result
+        att[rows] = result.astype(bf16)
+
+    attend(0)
+    attend(1)
+    down_lines[1].land(2)
+    up_fold.finish(0)
+    up_lines[0].start()
+    attend(2)
+    attend(3)
+    up_fold.middle(1)
+    tree.arrived()
+
+    def output(index):
+        rows = rows_of(index)
+        return dot(att[rows], w_dense[...]) + dot(act[rows], w_down[...])
+
+    emit(tiles, output, out_parts, width)
+    out_sink.start()
+    down_lines[1].land(3)
+    up_lines[0].land(1)
+    up_fold.finish(1)
+    up_lines[1].start()
+
+    dense_size = width // shards
+
+    def dense_grad(index):
+        start = pl.multiple_of(index * dense_size, dense_size)
+        return dot_rows(att[...], gra[:, pl.ds(start, dense_size)])
+
+    emit(shards, dense_grad, dense_parts, dense_size)
+    for slot in (1, 2, 0, 3):
+        dense_fold.send(slot)
+    out_sink.swap()
+    out_sink.step(1)
+
+    d_keys[...] = jnp.zeros_like(d_keys)
+    d_values[...] = jnp.zeros_like(d_values)
+
+    def attend_back(index):
+        rows = pl.ds(index * TILE, TILE)
+        size = (index + 1) * TILE
+        d_att = dot_cols(gra[rows], w_dense[...]).astype(bf16)
+        delta = jnp.sum(d_att.astype(f32) * att_f[rows], axis=-1, keepdims=True)
+        probs = wide_f[rows, :size]
+        d_scores = (probs * (dot_cols(d_att, values[:size]) - delta)).astype(bf16)
+        d_queries = dot(d_scores, keys[:size]) * factor
+        d_joined[rows, :head_dim] = turn(d_queries, rows, -1.0).astype(bf16)
+        d_keys[:size] += dot_rows(d_scores, queries[rows])
+        d_values[:size] += dot_rows(probs.astype(bf16), d_att)
+
+    attend_back(0)
+    attend_back(1)
+    up_lines[0].land(2)
+    dense_fold.middle(0)
+    dense_fold.middle(1)
+    attend_back(2)
+    attend_back(3)
+    up_lines[1].land(1)
+
+    def join(rows):
+        d_joined[rows, head_dim : 2 * head_dim] = turn(d_keys[rows] * factor, rows, -1.0).astype(bf16)
+        d_joined[rows, 2 * head_dim :] = d_values[rows].astype(bf16)
+
+    loop(join)
+    emit(
+        width // TILE,
+        lambda index: dot_rows(norm[:, rows_of(index)], d_joined[...]),
+        qkv_parts,
+        3 * head_dim,
+    )
+    for slot in (1, 2, 0, 3):
+        qkv_fold.send(slot)
+    out_sink.step(2)
+    dense_fold.finish(0)
+    dense_fold.finish(1)
+    dense_line.start()
+    up_lines[0].land(3)
+    up_lines[1].land(2)
+    qkv_fold.middle(0)
+    qkv_fold.middle(1)
+
     sums[...] = jnp.zeros_like(sums)
 
-    def inputs(rows):
+    def inputs(index):
+        rows = rows_of(index)
+        d_one = dot_cols(d_joined[rows], w_qkv[...])
         d_two = dot_cols(d_up[rows], w_up[...])
-        sums[0:1] += jnp.sum(d_two * centred(rows), axis=0, keepdims=True)
-        sums[1:2] += jnp.sum(d_two, axis=0, keepdims=True)
-        sums[2:3] += jnp.sum(gra[rows].astype(f32), axis=0, keepdims=True)
-        sums[3:4, :ff_units] += jnp.sum(d_up[rows].astype(f32), axis=0, keepdims=True)
-        e_two[rows] = (d_two * vector(2)).astype(bf16)
-
-    loop(inputs)
-
-    pairs = (
-        (hid, hidden_out), (n1, n1_out), (gra, grad_out), (vec, vec_out), (down_grad, down_grad_out),
-        (up_grad, up_grad_out), (ff, ff_out), (e_two, e_out), (sums, sums_out),
-    )
-    writes = [
-        pltpu.make_async_copy(src, dst, out_sems.at[index]) for index, (src, dst) in enumerate(pairs)
+        scaled = scaled_rows(rows)
+
+        def gather(row, entries):
+            sums[row : row + 1, : entries.shape[1]] += jnp.sum(
+                entries.astype(f32), axis=0, keepdims=True
+            )
+
+        gather(0, d_two * scaled)
+        gather(1, d_two)
+        gather(2, gra[rows])
+        gather(3, d_up[rows])
+        gather(4, d_one * scaled)
+        gather(5, d_one)
+        gather(6, d_joined[rows])
+        return d_one * vector(0) + d_two * vector(2)
+
+    emit(tiles, inputs, in_parts, width)
+    in_sink.start()
+    sums_sent = []
+    for bit in (1, 2, 3):
+        slot = take(1)
+        copy = remote(sums, sums_got.at[shard], sems, slot, (ctx, shard ^ bit))
+        copy.start()
+        sums_sent.append((copy, sums_got.at[shard ^ bit], slot))
+    sums_got[shard] = sums[...]
+    dense_line.land(1)
+    out_sink.step(3)
+    up_lines[1].land(3)
+    qkv_fold.finish(0)
+    qkv_lines[0].start()
+    qkv_fold.finish(1)
+    qkv_lines[1].start()
+    in_sink.swap()
+    in_sink.step(1)
+    dense_line.land(2)
+    for copy, landing, slot in sums_sent:
+        remote(landing, landing, sems, slot, (ctx ^ 1, shard)).wait_recv()
+    total = sums_got[0]
+    for index in range(1, shards):
+        total = total + sums_got[index]
+    sums_tot[...] = total
+    sums_line.start()
+    dense_line.land(3)
+    qkv_lines[0].land(1)
+    in_sink.step(2)
+    sums_line.land(1)
+    qkv_lines[1].land(1)
+    dense_line.arrived()
+    dense_block = dense_size
+    exchanged = []
+    for bit in (1, 2, 3):
+        slot = take(1)
+        peer = shard ^ bit
+        rows = pl.ds(pl.multiple_of(peer * dense_block, dense_block), dense_block)
+        own_rows = pl.ds(pl.multiple_of(shard * dense_block, dense_block), dense_block)
+        copy = remote(dense_lines.at[rows], dense_all.at[own_rows], sems, slot, (ctx, peer))
+        copy.start()
+        exchanged.append((copy, dense_all.at[rows], slot))
+    own_dense = pltpu.make_async_copy(
+        dense_lines.at[own_rows], dense_all.at[own_rows], local_sems.at[2]
+    )
+    own_dense.start()
+    out_sink.finish(output_out, local_sems.at[3])
+    qkv_lines[0].land(2)
+    in_sink.step(3)
+    sums_line.land(2)
+    qkv_lines[1].land(2)
+    qkv_lines[0].land(3)
+    sums_line.land(3)
+    qkv_lines[1].land(3)
+    in_sink.finish(input_out, local_sems.at[3])
+
+    write_vec = pltpu.make_async_copy(vec, vec_out, local_sems.at[8])
+    write_vec.start()
+    lines = down_lines + up_lines + qkv_lines + [sums_line]
+    for item in lines:
+        item.arrived()
+    for copy, landing, slot in exchanged:
+        remote(landing, landing, sems, slot, (ctx ^ 1, shard)).wait_recv()
+    own_dense.wait()
+    for item in [hid_line, gra_line, dense_line] + lines + squares + [tree]:
+        item.sent()
+    for item in (down_fold, up_fold, qkv_fold, dense_fold):
+        item.sent()
+    for copy, _, _ in small + sums_sent + exchanged:
+        copy.wait_send()
+    write_vec.wait()
+
+
+def rotary_table(length, lanes):
+    half = ROT // 2
+    freqs = (10000.0 ** (-2.0 * np.arange(half, dtype=np.float32) / ROT)).astype(np.float32)
+    angles = np.arange(length, dtype=np.float32)[:, None] * freqs[None]
+    cosine, sine = np.cos(angles), np.sin(angles)
+    table = np.zeros((3, length, lanes), np.float32)
+    table[0] = 1.0
+    table[0, :, :half], table[0, :, half:ROT] = cosine, cosine
+    table[1, :, half:ROT] = sine
+    table[2, :, :half] = -sine
+    return table
+
+
+def whole_block(hidden, grad, fc1, fc2, qkv, dense, vectors, segs):
+    chips, shards = lax.axis_size("ctx") // CORES, lax.axis_size("fsdp")
+    count = chips * CORES
+    tokens, width = hidden.shape
+    length = tokens * count
+    units = fc1.shape[1] // count
+    head_dim = width // HEADS
+    part = units // shards
+    rows = width // shards
+    bf16, f32 = jnp.bfloat16, jnp.float32
+    wide, joint = (length, width), 3 * head_dim
+    vec_shape = (shards,) + vectors.shape
+    seg_shape = (segs.shape[0] * count, segs.shape[1])
+    line = (tokens, width)
+    hops = (2 * (chips - 1) * tokens, width)
+    outs = [
+        (vec_shape, f32), (line, f32), (line, f32), ((count * part, width), bf16), ((count * rows, units), bf16),
+        ((count * rows, joint), bf16), ((width, rows), bf16), ((count * 8, width), f32),
+        ((units, width), bf16), ((width, units), bf16), ((width, joint), bf16), ((shards * head_dim, rows), bf16),
+        ((3 * part, width), bf16), ((3 * rows, units), bf16), ((3 * rows, joint), bf16), ((3 * head_dim, rows), bf16),
+        (wide, bf16), ((chips * tokens, width), bf16), (hops, bf16),
+        (wide, bf16), ((chips * tokens, width), bf16), (hops, bf16), ((count * head_dim, rows), bf16),
     ]
-    for write in writes:
-        write.start()
-    qkv_square.arrived()
-    tree.arrived()
-    for item in lines + squares + [tree]:
-        item.sent()
-    for copy, _ in small:
-        copy.wait_send()
-    for write in writes:
-        write.wait()
-
-
-def gather_and_feed_forward(hidden, grad, fc1, fc2, qkv, dense, vectors, segs):
-    chips, shards = lax.axis_size("ctx") // CORES, lax.axis_size("fsdp")
-    tokens, width = hidden.shape
-    length = tokens * chips * CORES
-    units = fc1.shape[1] // (chips * CORES)
-    head_dim = width // HEADS
-    bf16, f32 = jnp.bfloat16, jnp.float32
-    wide = (length, width)
-    shapes = [
-        (wide, bf16), (wide, bf16), (wide, bf16), ((width, 3 * head_dim), bf16), ((head_dim, width), bf16),
-        ((shards,) + vectors.shape, f32), ((segs.shape[0] * chips * CORES, segs.shape[1]), segs.dtype),
-        ((units, width), bf16), ((width, units), bf16), (wide, bf16), (wide, bf16), ((8, width), f32),
+    table = rotary_table(length, 128)
+    halves = [(part // 2, width), (rows // 2, units), (rows // 2, joint), (head_dim // 2, rows)]
+    scratch = [
+        (wide, bf16), (wide, bf16), (wide, bf16), ((width, units), bf16), ((units, width), bf16),
+        ((width, joint), bf16), ((head_dim, width), bf16), (vec_shape, f32), (seg_shape, segs.dtype),
+        ((length, segs.shape[1]), f32), (table.shape, f32),
+        ((length, units), bf16), ((length, max(units, length)), f32), ((length, units), bf16),
+        ((length, head_dim), bf16), ((length, head_dim), bf16), ((length, head_dim), bf16),
+        ((length, head_dim), f32), ((length, head_dim), bf16), ((length, head_dim), f32), ((length, head_dim), f32),
+        ((length, joint), bf16), ((8, width), f32), ((shards, 8, width), f32), ((8, width), f32),
+        ((2, TILE, width), bf16),
     ]
-    scratch = [
-        (wide, bf16), (wide, bf16), (wide, bf16), (wide, bf16), ((width, units), bf16), ((units, width), bf16),
-        ((shards,) + vectors.shape, f32), ((length, units), bf16), ((length, units), f32), ((length, units), bf16),
-        ((units, width), bf16), ((width, units), bf16), (wide, bf16), (wide, bf16), ((8, width), f32),
-    ]
-    count = 2 * Line.slots(chips) + 3 * Square.SLOTS + Tree.SLOTS + 3 + CORES * chips - 1
-    return pl.pallas_call(
-        functools.partial(gather_kernel, (chips, shards, units)),
-        out_shape=[jax.ShapeDtypeStruct(shape, kind) for shape, kind in shapes],
-        in_specs=[pl.BlockSpec(memory_space=pl.ANY)] * 8,
-        out_specs=[pl.BlockSpec(memory_space=pl.ANY)] * len(shapes),
+    scratch += [((3,) + half, bf16) for half in halves[:2]]
+    scratch += [((2,) + half, bf16) for half in halves]
+    scratch += [((2 * half[0], half[1]), bf16) for half in halves]
+    scratch += [((2, tokens, width), bf16), ((2, tokens, width), bf16), (line, f32)]
+    slots = (
+        10 * Line.slots(chips) + 3 * Square.SLOTS + Tree.SLOTS + 4 * Fold.SLOTS + 2 * Sink.slots(chips)
+        + 9 + count - 1
+    )
+    outputs = pl.pallas_call(
+        functools.partial(block_kernel, (chips, shards, part)),
+        out_shape=[jax.ShapeDtypeStruct(shape, kind) for shape, kind in outs],
+        in_specs=[pl.BlockSpec(memory_space=pl.ANY)] * 9,
+        out_specs=[pl.BlockSpec(memory_space=pl.ANY)] * len(outs),
         scratch_shapes=[pltpu.VMEM(shape, kind) for shape, kind in scratch]
         + [
-            pltpu.SemaphoreType.DMA((count,)),
-            pltpu.SemaphoreType.DMA((count,)),
-            pltpu.SemaphoreType.DMA((9,)),
+            pltpu.SemaphoreType.DMA((slots,)),
+            pltpu.SemaphoreType.DMA((slots,)),
+            pltpu.SemaphoreType.DMA((11,)),
         ],
         compiler_params=pltpu.CompilerParams(
-            collective_id=0, has_side_effects=True, vmem_limit_bytes=60 * 2**20
+            collective_id=0, has_side_effects=True, vmem_limit_bytes=62 * 2**20
         ),
-        name="gather_and_feed_forward",
-    )(hidden, grad, fc1, fc2, qkv, dense, vectors, segs)
+        name="whole_block",
+    )(hidden, grad, fc1, fc2, qkv, dense, vectors, segs, jnp.asarray(table))
+    return outputs[:8]
+
+
+def widen(blocks, groups, pieces):
+    rows, size = blocks.shape[0] // groups, blocks.shape[1] // pieces
+
+    def body(src, dst):
+        dst[...] = src[...].astype(jnp.float32)
+
+    return pl.pallas_call(
+        body,
+        grid=(groups, pieces),
+        in_specs=[pl.BlockSpec((rows, size), lambda group, piece: (group, piece))],
+        out_specs=pl.BlockSpec((rows, size), lambda group, piece: (0, piece * groups + group)),
+        out_shape=jax.ShapeDtypeStruct((rows, pieces * groups * size), jnp.float32),
+        name="widen",
+    )(blocks)
+
+
+def one_kernel(
+    hidden, qkv_weight, dense_weight, fc1_weight, fc2_weight, segments, out_grad, vectors
+):
+    shards, count = lax.axis_size("fsdp"), lax.axis_size("ctx")
+    shard = lax.axis_index("fsdp")
+    tokens, width = hidden.shape[1], hidden.shape[2]
+    rows = width // shards
+    head_dim = width // HEADS
+    f32, bf16 = jnp.float32, jnp.bfloat16
+    vec, branch, back, down_all, up_all, qkv_all, dense_all, sums_all = whole_block(
+        hidden[0], out_grad[0], fc1_weight, fc2_weight, qkv_weight, dense_weight, vectors,
+        jnp.broadcast_to(segments, (8, tokens)),
+    )
+    own = hidden[0].astype(f32)
+    shift = vec[:, 4].reshape(-1) + vec[:, 5].reshape(-1)
+    layer_output = (own + branch + shift).astype(bf16)
+    scaled, spread = centred(own)
+    input_part = spread * (
+        back
+        - jnp.mean(back, axis=-1, keepdims=True)
+        - scaled * jnp.mean(back * scaled, axis=-1, keepdims=True)
+    )
+    input_grad = (out_grad[0].astype(f32) + input_part).astype(bf16)
+    sums = sums_all.reshape(count, 8, width)
+    mine = lax.dynamic_slice_in_dim(sums, shard * rows, rows, 2)
+    totals = jnp.sum(mine, axis=0)
+    part = fc1_weight.shape[1] // count // shards
+    up_sum = lax.dynamic_slice_in_dim(sums[:, 3], shard * part, part, 1).reshape(-1)
+    joined = sums[:, 6, : 3 * head_dim].reshape(count, 3, head_dim).transpose(1, 0, 2).reshape(-1)
+    joined = lax.dynamic_slice_in_dim(joined, shard * 3 * rows, 3 * rows, 0)
+    columns = mine[0, 2]
+    return (
+        layer_output[None],
+        input_grad[None],
+        totals[4],
+        totals[5],
+        widen(qkv_all, count, 3),
+        joined,
+        widen(dense_all, shards, 1),
+        columns,
+        totals[0],
+        totals[1],
+        widen(up_all, count, shards),
+        up_sum,
+        widen(down_all, 1, 8),
+        columns,
+    )
 
 
 def per_device(
@@ -637,54 +1250,46 @@
     ).reshape(-1, rows)
     vectors = jnp.pad(vectors, ((0, -vectors.shape[0] % 8), (0, 0)))
     if ctx_count == HEADS and shards == 4:
-        (
-            hidden_all, normed_one, grad_all, qkv_w, dense_w, vec, seg_all,
-            down_part_grad, up_part_grad, ff_part, e_two, sums,
-        ) = gather_and_feed_forward(
-            hidden[0], out_grad[0], fc1_weight, fc2_weight, qkv_weight, dense_weight, vectors,
-            jnp.broadcast_to(segments, (8, tokens)),
+        return one_kernel(
+            hidden, qkv_weight, dense_weight, fc1_weight, fc2_weight, segments, out_grad, vectors
         )
-        query_seg = seg_all.reshape(ctx_count, 8, tokens)[:, 0].reshape(-1)
-        gain_two_sum, shift_two_sum, columns = sums[0], sums[1], sums[2]
-        up_sum = sums[3, : shards * units]
-    else:
-        vec = lax.all_gather(vectors, "fsdp", axis=0)
-        query_seg = lax.all_gather(segments[0], "ctx", axis=0, tiled=True)
-        up_part = lax.dynamic_index_in_dim(
-            fc1_weight.reshape(rows, shards, ctx_count, units), ctx, 2, keepdims=False
-        ).reshape(rows, shards * units)
-        down_part = lax.dynamic_slice_in_dim(fc2_weight, ctx * units, units, 0)
-        qkv_part = lax.dynamic_index_in_dim(
-            qkv_weight.reshape(rows, 3, HEADS, head_dim), head, 2, keepdims=False
-        ).reshape(rows, 3 * head_dim)
-        dense_cols = lax.all_to_all(
-            dense_weight, "fsdp", split_axis=1, concat_axis=0, tiled=True
-        )
-        dense_part = lax.dynamic_slice_in_dim(dense_cols, head * head_dim, head_dim, 0)
-        up_w = gather_fsdp(up_part)
-        down_w = gather_fsdp(down_part)
-        qkv_w = gather_fsdp(qkv_part)
-        dense_w = gather_fsdp(dense_part, axis=1)
-        hidden_all = line_gather(hidden[0]).reshape(length, width)
-        grad_all = line_gather(out_grad[0]).reshape(length, width)
-        normed_one = (centred(hidden_all)[0] * vec[:, 0].reshape(-1) + vec[:, 1].reshape(-1)).astype(bf16)
-        scaled = centred(hidden_all)[0]
-        gain_two = vec[:, 2].reshape(-1)
-        normed_two = (scaled * gain_two + vec[:, 3].reshape(-1)).astype(bf16)
-        up_shift = lax.dynamic_index_in_dim(
-            vec[:, 9 : 9 + ff // width].reshape(shards, ctx_count, units), ctx, 1, keepdims=False
-        ).reshape(-1)
-        act_f, slope = gelu_and_slope(dot(normed_two, up_w) + up_shift)
-        act = act_f.astype(bf16)
-        d_up = (dot_cols(grad_all, down_w) * slope).astype(bf16)
-        down_part_grad = dot_rows(act, grad_all).astype(bf16)
-        up_part_grad = dot_rows(normed_two, d_up).astype(bf16)
-        ff_part = dot(act, down_w).astype(bf16)
-        d_two = dot_cols(d_up, up_w)
-        e_two = (d_two * gain_two).astype(bf16)
-        gain_two_sum, shift_two_sum = jnp.sum(d_two * scaled, axis=0), jnp.sum(d_two, axis=0)
-        columns = jnp.sum(grad_all.astype(f32), axis=0)
-        up_sum = jnp.sum(d_up.astype(f32), axis=0)
+    vec = lax.all_gather(vectors, "fsdp", axis=0)
+    query_seg = lax.all_gather(segments[0], "ctx", axis=0, tiled=True)
+    up_part = lax.dynamic_index_in_dim(
+        fc1_weight.reshape(rows, shards, ctx_count, units), ctx, 2, keepdims=False
+    ).reshape(rows, shards * units)
+    down_part = lax.dynamic_slice_in_dim(fc2_weight, ctx * units, units, 0)
+    qkv_part = lax.dynamic_index_in_dim(
+        qkv_weight.reshape(rows, 3, HEADS, head_dim), head, 2, keepdims=False
+    ).reshape(rows, 3 * head_dim)
+    dense_cols = lax.all_to_all(
+        dense_weight, "fsdp", split_axis=1, concat_axis=0, tiled=True
+    )
+    dense_part = lax.dynamic_slice_in_dim(dense_cols, head * head_dim, head_dim, 0)
+    up_w = gather_fsdp(up_part)
+    down_w = gather_fsdp(down_part)
+    qkv_w = gather_fsdp(qkv_part)
+    dense_w = gather_fsdp(dense_part, axis=1)
+    hidden_all = line_gather(hidden[0]).reshape(length, width)
+    grad_all = line_gather(out_grad[0]).reshape(length, width)
+    normed_one = (centred(hidden_all)[0] * vec[:, 0].reshape(-1) + vec[:, 1].reshape(-1)).astype(bf16)
+    scaled = centred(hidden_all)[0]
+    gain_two = vec[:, 2].reshape(-1)
+    normed_two = (scaled * gain_two + vec[:, 3].reshape(-1)).astype(bf16)
+    up_shift = lax.dynamic_index_in_dim(
+        vec[:, 9 : 9 + ff // width].reshape(shards, ctx_count, units), ctx, 1, keepdims=False
+    ).reshape(-1)
+    act_f, slope = gelu_and_slope(dot(normed_two, up_w) + up_shift)
+    act = act_f.astype(bf16)
+    d_up = (dot_cols(grad_all, down_w) * slope).astype(bf16)
+    down_part_grad = dot_rows(act, grad_all).astype(bf16)
+    up_part_grad = dot_rows(normed_two, d_up).astype(bf16)
+    ff_part = dot(act, down_w).astype(bf16)
+    d_two = dot_cols(d_up, up_w)
+    e_two = (d_two * gain_two).astype(bf16)
+    gain_two_sum, shift_two_sum = jnp.sum(d_two * scaled, axis=0), jnp.sum(d_two, axis=0)
+    columns = jnp.sum(grad_all.astype(f32), axis=0)
+    up_sum = jnp.sum(d_up.astype(f32), axis=0)
     gain_one = vec[:, 0].reshape(-1)
     dense_shift, down_shift = vec[:, 4].reshape(-1), vec[:, 5].reshape(-1)
     qkv_shift = vec[:, 6:9].reshape(-1)

time: 758 us -> 441 us (0.58)
  waiting for transfers between devices: 303 us -> 0 us
  Pallas kernels: 125 us -> 414 us
  local copies, waits for them, and re-layouts: 143 us -> 12.8 us
  other arithmetic: 67.9 us -> 6.97 us
  starting transfers between devices: 56.8 us -> 0 us
  matrix products: 40.3 us -> 0 us
  between operations: 15.4 us -> 0.73 us
    pallas_call x1 -> x5, Pallas kernels: 125 us -> 414 us  [the longest x1 363 us: whole_block(): pl.pallas_call(functools.partial(block_kernel, (chips, shards, part)), ou...]
    ppermute x28 -> x0, waiting for transfers between devices: 189 us -> none  [the longest x12 169 us: line_gather(): lax.ppermute(down, 'ctx', [(i * CORES + k, (i - 1) * CORES + k) for i in...]
    reduce_scatter x6 -> x0, waiting for transfers between devices: 112 us -> none  [the longest x4 112 us: scatter_fsdp(): return lax.psum_scatter(values, 'fsdp', scatter_dimension=0, tiled=True)]
    unnamed x120 -> x16, local copies, waits for them, and re-layouts: 62 us -> 5.43 us
    ppermute x28 -> x0, starting transfers between devices: 51.9 us -> none  [the longest x12 36.4 us: line_gather(): lax.ppermute(up, 'ctx', [(i * CORES + k, (i + 1) * CORES + k) for i in ra...]
    dot_general x12 -> x0, matrix products: 40.3 us -> none  [the longest x4 15.8 us: dot(): return jnp.dot(left, right, preferred_element_type=jnp.float32)]
    reshape x6 -> x0, local copies, waits for them, and re-layouts: 20.2 us -> none  [the longest x1 11.6 us: per_device(): qkv_all.reshape(HEADS, rows, 3, head_dim).transpose(1, 2, 0, 3)]
    dynamic_slice x7 -> x2, local copies, waits for them, and re-layouts: 19.8 us -> 1.29 us  [the longest x1 0.68 us: one_kernel(): joined = lax.dynamic_slice_in_dim(joined, shard * 3 * rows, 3 * rows, 0)]
  transfers between devices with their start and end apart: 35 -> 0, of which waited for: 14 -> 0; matrix products, arithmetic and copies ran while one was open for 27% -> 0% of each run, Pallas kernels for 0% -> 0%
where the time goes in v3:
time: 441 us; the launch traced here: 434 us
  Pallas kernels  414 us (94%)
  local copies, waits for them, and re-layouts  12.8 us (3%)
  other arithmetic  6.97 us (2%)
    pallas_call x1, Pallas kernels, whole_block(): pl.pallas_call(functools.partial(block_kernel, (chips, shards, part)), ou...  363 us
    pallas_call x4, Pallas kernels, widen(): pl.pallas_call(body, grid=(groups, pieces), in_specs=[pl.BlockSpec((rows,...  50.5 us

profile of v3, /device:TPU:0, one launch (start us, length us, event | category | flops | bytes accessed | tf_op | source)
XLA Modules:
  0.0 434.0 jit_solution(3140231679009394029)
XLA Ops:
  0.7 0.7 constant_dynamic-update-slice_fusion.7
  1.3 0.7 constant_dynamic-update-slice_fusion.6
  2.0 0.7 constant_dynamic-update-slice_fusion.5
  2.7 0.7 constant_dynamic-update-slice_fusion.4
  3.4 0.7 constant_dynamic-update-slice_fusion.3
  4.1 0.7 constant_dynamic-update-slice_fusion.2
  4.8 0.7 constant_dynamic-update-slice_fusion.1
  5.5 0.7 constant_dynamic-update-slice_fusion
  6.2 0.6 pad.4.vectors
  6.8 1.2 broadcast_in_dim.9.segs
  8.1 363.0 %whole_block.1 = (f32[4,16,512]{2,1,0:T(8,128)}, f32[128,2048]{1,0:T(8,128)}, f32[128,2048]{1,0:T(8,128)}, bf16[2048,2048]{1,0:T(8,128)(2,1)}, bf16[4096,1024]{1...) custom-call(bf16[128,2048]{1,0:T(8,128)(2,1)} %bitcast.28, ...), custom_call_target="tpu_custom_call" | custom-call | tf_op jit(solution)/shard_map/whole_block/pallas_call | solution.py:1133
  371.5 1.6 fusion.14
  373.1 0.9 slice_add_fusion
  374.1 3.1 fusion.13
  377.2 0.9 dynamic-slice_reduce_fusion
  378.7 0.8 constant_dynamic-slice_fusion
  379.5 1.0 slice.38
  380.5 0.7 dynamic_slice.10
  381.2 1.1 slice.41
  382.3 0.6 constant_dynamic-slice_fusion.1
  382.9 20.4 %widen.6 = f32[512,8192]{1,0:T(8,128)} custom-call(bf16[4096,1024]{1,0:T(8,128)(2,1)} %get-tuple-element.28.src), custom_call_target="tpu_custom_call" | custom-call | tf_op jit(solution)/shard_map/widen/pallas_call | solution.py:1158
  403.2 10.4 %widen.7 = f32[2048,2048]{1,0:T(8,128)} custom-call(bf16[2048,2048]{1,0:T(8,128)(2,1)} %get-tuple-element.29.src), custom_call_target="tpu_custom_call" | custom-call | tf_op jit(solution)/shard_map/widen/pallas_call | solution.py:1158
  413.6 15.6 %widen.4 = f32[512,6144]{1,0:T(8,128)} custom-call(bf16[4096,768]{1,0:T(8,128)(2,1)} %get-tuple-element.26.src), custom_call_target="tpu_custom_call" | custom-call | tf_op jit(solution)/shard_map/widen/pallas_call | solution.py:1158
  429.2 4.2 widen.5
  (19 shorter events, 1.7 us)
Async XLA Ops:
  8.1 363.0 %copy-start = (bf16[1,128,2048]{2,1,0:T(8,128)(2,1)S(1)}, bf16[1,128,2048]{2,1,0:T(8,128)(2,1)}, u32[]{:S(2)}) copy-start(bf16[1,128,2048]{2,1,0:T(8,128)(2,1)} %param.16) | copy-start | bytes 1572868
  8.1 366.0 %copy-start.1 = (bf16[1,128,2048]{2,1,0:T(8,128)(2,1)S(1)}, bf16[1,128,2048]{2,1,0:T(8,128)(2,1)}, u32[]{:S(2)}) copy-start(bf16[1,128,2048]{2,1,0:T(8,128)(2,1)} %param.30) | copy-start | bytes 1572868
  379.5 53.9 %copy-start.2 = (f32[1,1,512]{2,1,0:T(1,128)}, f32[1,1,512]{2,1,0:T(1,128)S(1)}, u32[]{:S(2)}) copy-start(f32[1,1,512]{2,1,0:T(1,128)S(1)} %constant_dynamic-slice_fusion) | copy-start | bytes 6148

commit v4 on v3

--- a/solution.py
+++ b/solution.py
@@ -113,13 +113,15 @@
 
 
 class Line:
-    def __init__(self, source, blocks, sems, base, place, chips, stride=None, offset=0):
+    def __init__(self, source, blocks, sems, base, place, chips, stride=None, offset=0, columns=slice(None)):
         self.source, self.sems, self.base, self.chips = source, sems, base, chips
         self.ctx, self.shard = place
         self.chip = self.ctx // CORES
         rows = source.shape[0]
         stride = stride or rows
-        self.block = lambda index: blocks.at[pl.ds(pl.multiple_of(index * stride + offset, rows), rows)]
+        self.block = lambda index: blocks.at[
+            pl.ds(pl.multiple_of(index * stride + offset, rows), rows), columns
+        ]
         self.swap_base = base + 2 * (chips - 1)
         self.own_slot = base + 4 * (chips - 1)
 
@@ -569,7 +571,8 @@
 
 def block_kernel(
     sizes,
-    hidden, grad, fc1, fc2, qkv, dense, vectors, segs, tables,
+    hidden, grad, fc1, fc2, qkv, dense, segs, tables,
+    ln1_gain, ln1_bias, ln2_gain, ln2_bias, dense_bias, fc2_bias, qkv_bias, fc1_bias,
     vec_out, output_out, input_out, down_all, up_all, qkv_all, dense_all, sums_all,
     down_parts, up_parts, qkv_parts, dense_parts, down_land, up_land, qkv_land, dense_land,
     out_parts, out_swap, out_land, in_parts, in_swap, in_land, dense_lines,
@@ -588,7 +591,7 @@
     width, length = hidden.shape[1], hid.shape[0]
     ff_units = w_down.shape[0]
     head_dim = w_dense.shape[0]
-    row_size = vec.shape[2]
+    row_size = vec.shape[3]
     tiles = length // TILE
     f32, bf16 = jnp.float32, jnp.bfloat16
     factor = head_dim ** (-0.5)
@@ -607,15 +610,8 @@
         base += slots
         return base - slots
 
-    def line(source, blocks, stride=None, offset=0):
-        return Line(source, blocks, sems, take(Line.slots(chips)), place, chips, stride, offset)
-
-    def line_pair(final, blocks):
-        half = final.shape[0] // 2
-        return [
-            line(final.at[pl.ds(which * half, half)], blocks, final.shape[0], which * half)
-            for which in (0, 1)
-        ]
+    def line(source, blocks, stride=None, offset=0, cut=slice(None)):
+        return Line(source, blocks, sems, take(Line.slots(chips)), place, chips, stride, offset, cut)
 
     def fold(parts, landing, stage, carry, final):
         return Fold(
@@ -667,67 +663,80 @@
         pl.ds(pl.multiple_of(lax.rem(ctx, heads_here) * head_dim, head_dim), head_dim)
     ]
     tree = Tree(dense_rows, w_dense, sems, take(Tree.SLOTS), place, ctx // heads_here)
-    down_fold = fold(down_parts, down_land, down_stage, down_carry, down_final)
-    up_fold = fold(up_parts, up_land, up_stage, up_carry, up_final)
-    qkv_fold = fold(
-        qkv_parts, qkv_land, up_stage.at[:, :, : 3 * head_dim], qkv_carry, qkv_final
-    )
-    dense_fold = fold(
-        dense_parts, dense_land, down_stage.at[:, :, : width // shards], dense_carry, dense_final
-    )
-    down_lines = line_pair(down_final, down_all)
-    up_lines = line_pair(up_final, up_all)
-    qkv_lines = line_pair(qkv_final, qkv_all)
-    dense_line = line(dense_final, dense_lines)
-    sums_line = line(sums_tot, sums_all)
+    named = {"hid": hid_line, "gra": gra_line, "wu": up_square, "wd": down_square, "wq": qkv_square, "wt": tree}
+    folds, lines = [], []
+
+    def gradient(letter, cuts, parts, landing, stage, carry, final, gathered):
+        start, half = 0, final.shape[0] // 2
+        for index, (size, split) in enumerate(cuts):
+            cut = pl.ds(start, size)
+            item = fold(
+                parts.at[:, cut], landing.at[:, cut], stage.at[:, :, :size], carry.at[:, :, cut], final.at[:, cut]
+            )
+            folds.append(item)
+            named[f"f{letter}{index}"] = item
+            for which in range(2 if split else 1):
+                rows = half if split else 2 * half
+                item = line(
+                    final.at[pl.ds(which * rows, rows), cut], gathered, final.shape[0], which * rows, cut
+                )
+                lines.append(item)
+                named[f"l{letter}{index}{which}"] = item
+            start += size
+
+    gradient("d", DOWN_CUTS, down_parts, down_land, down_stage, down_carry, down_final, down_all)
+    gradient("u", UP_CUTS, up_parts, up_land, up_stage, up_carry, up_final, up_all)
+    gradient("q", QKV_CUTS, qkv_parts, qkv_land, up_stage, qkv_carry, qkv_final, qkv_all)
+    gradient("e", DENSE_CUTS, dense_parts, dense_land, down_stage, dense_carry, dense_final, dense_lines)
+    named["ls"] = line(sums_tot, sums_all)
+    lines.append(named["ls"])
     out_sink = sink(out_parts, out_swap, out_land, out_carry)
     in_sink = sink(in_parts, in_swap, in_land, in_carry)
+    named["so"], named["si"] = out_sink, in_sink
 
     small = []
 
     def send_small(src, dst, landing, device):
         slot = take(1)
         small.append((remote(src, dst, sems, slot, device), landing, slot))
-
-    seg_rows = segs.shape[0]
-
-    def seg_block(index):
-        return seg.at[pl.ds(pl.multiple_of(index * seg_rows, seg_rows), seg_rows)]
-
-    for bit in (1, 2, 3):
-        send_small(vectors, vec.at[shard], vec.at[shard ^ bit], (ctx, shard ^ bit))
-    for step in range(1, count):
-        send_small(
-            segs, seg_block(ctx), seg_block(lax.rem(ctx + count - step, count)),
-            (lax.rem(ctx + step, count), shard),
-        )
-    for copy, _, _ in small:
-        copy.start()
+        small[-1][0].start()
+
+    def wait_small(items):
+        for _, landing, slot in items:
+            remote(landing, landing, sems, slot, (ctx ^ 1, shard)).wait_recv()
+
+    vectors = (
+        ln1_gain, ln1_bias, ln2_gain, ln2_bias, dense_bias, fc2_bias, qkv_bias, fc1_bias
+    )
+    at, pairs = 0, [(segs, seg.at[ctx]), (tables, table)]
+    for vector in vectors:
+        size = vec.shape[3]
+        for start in range(0, vector.shape[1], size):
+            pairs.append((vector.at[:, pl.ds(start, size)], vec.at[shard, at]))
+            at += 1
     locals_in = [
         pltpu.make_async_copy(src, dst, local_sems.at[8 + index])
-        for index, (src, dst) in enumerate(
-            ((vectors, vec.at[shard]), (segs, seg_block(ctx)), (tables, table))
-        )
+        for index, (src, dst) in enumerate(pairs)
     ]
     for copy in locals_in:
         copy.start()
 
-    hid_line.start()
-    up_square.start()
-    hid_line.land(1)
-    up_square.forward()
-    down_square.start()
-    hid_line.land(2)
-    gra_line.start()
-    hid_line.land(3)
-    for _, landing, slot in small:
-        remote(landing, landing, sems, slot, (ctx ^ 1, shard)).wait_recv()
-    for copy in locals_in:
-        copy.wait()
-    hid_line.arrived()
+    def small_start():
+        for copy in locals_in:
+            copy.wait()
+        for bit in (1, 2, 3):
+            send_small(vec.at[shard], vec.at[shard], vec.at[shard ^ bit], (ctx, shard ^ bit))
+        for step in range(1, count):
+            send_small(
+                segs, seg.at[ctx], seg.at[lax.rem(ctx + count - step, count)],
+                (lax.rem(ctx + step, count), shard),
+            )
+
+    def small_land():
+        wait_small(small)
 
     def vector(row):
-        return jnp.concatenate([vec[index, row : row + 1] for index in range(shards)], axis=1)
+        return jnp.concatenate([vec[index, row] for index in range(shards)], axis=1)
 
     def rows_of(index):
         return pl.ds(pl.multiple_of(index * TILE, TILE), TILE)
@@ -744,11 +753,12 @@
     def norm_one(rows):
         norm[rows] = (scaled_rows(rows) * vector(0) + vector(1)).astype(bf16)
 
-    def emit(steps, compute, dst, size):
+    def emit(steps, compute, dst, size, start=0):
         def write(index):
-            slot = lax.rem(index, 2)
             return pltpu.make_async_copy(
-                stage.at[slot, :, :size], dst.at[rows_of(index)], local_sems.at[slot]
+                stage.at[lax.rem(index, 2), :, :size],
+                dst.at[rows_of(index), pl.ds(start, size)],
+                local_sems.at[lax.rem(index, 2)],
             )
 
         def body(index, carry):
@@ -764,87 +774,62 @@
         write(steps - 2).wait()
         write(steps - 1).wait()
 
-    loop(norm_two)
-    up_square.arrived()
-    down_square.forward()
-    gra_line.land(1)
-
-    bias_start = ctx * columns
-    bias_row = 9 + bias_start // row_size
-    bias_column = pl.multiple_of(lax.rem(bias_start, row_size), columns)
-    up_bias = jnp.concatenate(
-        [vec[index, pl.ds(bias_row, 1), pl.ds(bias_column, columns)] for index in range(shards)],
-        axis=1,
-    )
-
-    def feed_forward(rows):
-        value = dot(norm[rows], w_up[...]) + up_bias
-        cdf = 0.5 * (1.0 + lax.erf(value * (0.5**0.5)))
-        density = jnp.exp(-0.5 * value * value) * ((2.0 * math.pi) ** -0.5)
-        act[rows] = (value * cdf).astype(bf16)
-        wide_f[rows] = cdf + value * density
-
-    loop(feed_forward)
-    gra_line.land(2)
-    down_square.arrived()
-    gra_line.land(3)
-    gra_line.arrived()
-
-    def fc2_grad(index, carry):
-        owner = shard ^ (3 - index)
-        rows = rows_of(owner)
-        stage[0] = dot_rows(act[:, rows], gra[...]).astype(bf16)
-        write = pltpu.make_async_copy(stage.at[0], down_parts.at[rows], local_sems.at[0])
-        write.start()
-        write.wait()
-        for step, slot in ((0, 1), (1, 2), (2, 0)):
-
-            @pl.when(index == step)
-            def _(slot=slot):
-                down_fold.send(slot)
-
-        return carry
-
-    lax.fori_loop(0, shards, fc2_grad, 0)
-
-    def feed_back(rows):
-        d_up[rows] = (dot_cols(gra[rows], w_down[...]) * wide_f[rows]).astype(bf16)
-
-    loop(feed_back)
-    down_fold.middle(0)
-    down_fold.send(3)
-    emit(
-        width // TILE,
-        lambda index: dot_rows(norm[:, rows_of(index)], d_up[...]),
-        up_parts,
-        ff_units,
-    )
-    down_fold.finish(0)
-    down_lines[0].start()
-    qkv_square.start()
-    loop(norm_one)
-    down_fold.middle(1)
-    down_lines[0].land(1)
-    qkv_square.forward()
-    for slot in (1, 2, 0):
-        up_fold.send(slot)
-    tree.start()
-    down_lines[0].land(2)
-    down_fold.finish(1)
-    down_lines[1].start()
-
-    per = 3 * HEADS // shards
-    bias_parts = []
-    for index in range(3):
-        at = index * HEADS + ctx
-        rest = lax.rem(at, per) * head_dim
-        bias_parts.append(
-            vec[
-                at // per,
-                pl.ds(6 + rest // row_size, 1),
-                pl.ds(pl.multiple_of(lax.rem(rest, row_size), head_dim), head_dim),
-            ]
-        )
+    def feed_forward():
+        bias_start = ctx * columns
+        bias_row = 9 + bias_start // row_size
+        bias_column = pl.multiple_of(lax.rem(bias_start, row_size), columns)
+        up_bias = jnp.concatenate(
+            [vec[index, bias_row, :, pl.ds(bias_column, columns)] for index in range(shards)],
+            axis=1,
+        )
+
+        def body(rows):
+            value = dot(norm[rows], w_up[...]) + up_bias
+            cdf = 0.5 * (1.0 + lax.erf(value * (0.5**0.5)))
+            density = jnp.exp(-0.5 * value * value) * ((2.0 * math.pi) ** -0.5)
+            act[rows] = (value * cdf).astype(bf16)
+            wide_f[rows] = cdf + value * density
+
+        loop(body)
+
+    def down_grad(index):
+        start, size = sum(cut[0] for cut in DOWN_CUTS[:index]), DOWN_CUTS[index][0]
+
+        def body(step, carry):
+            rows = rows_of(shard ^ (3 - step))
+            cut = pl.ds(start, size)
+            stage[0, :, :size] = dot_rows(act[:, rows], gra[:, cut]).astype(bf16)
+            write = pltpu.make_async_copy(
+                stage.at[0, :, :size], down_parts.at[rows, cut], local_sems.at[0]
+            )
+            write.start()
+            write.wait()
+            for number, slot in ((0, 1), (1, 2), (2, 0)):
+
+                @pl.when(step == number)
+                def _(slot=slot):
+                    named[f"fd{index}"].send(slot)
+
+            return carry
+
+        lax.fori_loop(0, shards, body, 0)
+
+    def feed_back():
+        def body(rows):
+            d_up[rows] = (dot_cols(gra[rows], w_down[...]) * wide_f[rows]).astype(bf16)
+
+        loop(body)
+
+    def up_grad(index):
+        start, size = sum(cut[0] for cut in UP_CUTS[:index]), UP_CUTS[index][0]
+        emit(
+            width // TILE,
+            lambda step: dot_rows(norm[:, rows_of(step)], d_up[:, pl.ds(start, size)]),
+            up_parts,
+            size,
+            start,
+        )
+
     rotary = table.shape[2]
 
     def turn(entries, rows, way):
@@ -856,35 +841,41 @@
         )
         return jnp.concatenate([first, entries[:, rotary:]], axis=1)
 
-    def project(rows):
-        joined = dot(norm[rows], w_qkv[...])
-        parts = [
-            joined[:, index * head_dim : (index + 1) * head_dim] + bias_parts[index]
-            for index in range(3)
-        ]
-        queries[rows] = turn(parts[0], rows, 1.0).astype(bf16)
-        keys[rows] = turn(parts[1], rows, 1.0).astype(bf16)
-        values[rows] = parts[2].astype(bf16)
-
-    seg_row = jnp.concatenate(
-        [seg[index * seg_rows : index * seg_rows + 1] for index in range(count)], axis=1
-    )
-    side = segs.shape[1]
-    for index in range(count):
-        block = seg[index * seg_rows : index * seg_rows + 1].astype(f32)
-        seg_col[index * side : (index + 1) * side] = jnp.broadcast_to(block, (side, side)).T
-
-    qkv_square.arrived()
-    loop(project)
-    down_lines[0].land(3)
-    down_lines[1].land(1)
-    up_fold.middle(0)
-    up_fold.send(3)
-    tree.forward()
+    def project():
+        per = 3 * HEADS // shards
+        bias_parts = []
+        for index in range(3):
+            place = index * HEADS + ctx
+            rest = lax.rem(place, per) * head_dim
+            bias_parts.append(
+                vec[
+                    place // per,
+                    6 + rest // row_size,
+                    :,
+                    pl.ds(pl.multiple_of(lax.rem(rest, row_size), head_dim), head_dim),
+                ]
+            )
+
+        def body(rows):
+            joined = dot(norm[rows], w_qkv[...])
+            parts = [
+                joined[:, index * head_dim : (index + 1) * head_dim] + bias_parts[index]
+                for index in range(3)
+            ]
+            queries[rows] = turn(parts[0], rows, 1.0).astype(bf16)
+            keys[rows] = turn(parts[1], rows, 1.0).astype(bf16)
+            values[rows] = parts[2].astype(bf16)
+
+        loop(body)
+        side = segs.shape[1]
+        for index in range(count):
+            block = seg[index].astype(f32)
+            seg_col[index * side : (index + 1) * side] = jnp.broadcast_to(block, (side, side)).T
 
     def attend(index):
         rows = pl.ds(index * TILE, TILE)
         size = (index + 1) * TILE
+        seg_row = jnp.concatenate([seg[block] for block in range(count)], axis=1)
         scores = dot_cols(queries[rows], keys[:size]) * factor
         query_place = index * TILE + lax.broadcasted_iota(jnp.int32, (TILE, size), 0)
         key_place = lax.broadcasted_iota(jnp.int32, (TILE, size), 1)
@@ -900,41 +891,25 @@
         att_f[rows] = result
         att[rows] = result.astype(bf16)
 
-    attend(0)
-    attend(1)
-    down_lines[1].land(2)
-    up_fold.finish(0)
-    up_lines[0].start()
-    attend(2)
-    attend(3)
-    up_fold.middle(1)
-    tree.arrived()
-
-    def output(index):
-        rows = rows_of(index)
-        return dot(att[rows], w_dense[...]) + dot(act[rows], w_down[...])
-
-    emit(tiles, output, out_parts, width)
-    out_sink.start()
-    down_lines[1].land(3)
-    up_lines[0].land(1)
-    up_fold.finish(1)
-    up_lines[1].start()
+    def attend_all():
+        for index in range(tiles):
+            attend(index)
+
+    def output():
+        def body(index):
+            rows = rows_of(index)
+            return dot(att[rows], w_dense[...]) + dot(act[rows], w_down[...])
+
+        emit(tiles, body, out_parts, width)
 
     dense_size = width // shards
 
-    def dense_grad(index):
-        start = pl.multiple_of(index * dense_size, dense_size)
-        return dot_rows(att[...], gra[:, pl.ds(start, dense_size)])
-
-    emit(shards, dense_grad, dense_parts, dense_size)
-    for slot in (1, 2, 0, 3):
-        dense_fold.send(slot)
-    out_sink.swap()
-    out_sink.step(1)
-
-    d_keys[...] = jnp.zeros_like(d_keys)
-    d_values[...] = jnp.zeros_like(d_values)
+    def dense_grad():
+        def body(index):
+            start = pl.multiple_of(index * dense_size, dense_size)
+            return dot_rows(att[...], gra[:, pl.ds(start, dense_size)])
+
+        emit(shards, body, dense_parts, dense_size)
 
     def attend_back(index):
         rows = pl.ds(index * TILE, TILE)
@@ -948,130 +923,146 @@
         d_keys[:size] += dot_rows(d_scores, queries[rows])
         d_values[:size] += dot_rows(probs.astype(bf16), d_att)
 
-    attend_back(0)
-    attend_back(1)
-    up_lines[0].land(2)
-    dense_fold.middle(0)
-    dense_fold.middle(1)
-    attend_back(2)
-    attend_back(3)
-    up_lines[1].land(1)
-
-    def join(rows):
-        d_joined[rows, head_dim : 2 * head_dim] = turn(d_keys[rows] * factor, rows, -1.0).astype(bf16)
-        d_joined[rows, 2 * head_dim :] = d_values[rows].astype(bf16)
-
-    loop(join)
-    emit(
-        width // TILE,
-        lambda index: dot_rows(norm[:, rows_of(index)], d_joined[...]),
-        qkv_parts,
-        3 * head_dim,
-    )
-    for slot in (1, 2, 0, 3):
-        qkv_fold.send(slot)
-    out_sink.step(2)
-    dense_fold.finish(0)
-    dense_fold.finish(1)
-    dense_line.start()
-    up_lines[0].land(3)
-    up_lines[1].land(2)
-    qkv_fold.middle(0)
-    qkv_fold.middle(1)
-
-    sums[...] = jnp.zeros_like(sums)
-
-    def inputs(index):
-        rows = rows_of(index)
-        d_one = dot_cols(d_joined[rows], w_qkv[...])
-        d_two = dot_cols(d_up[rows], w_up[...])
-        scaled = scaled_rows(rows)
-
-        def gather(row, entries):
-            sums[row : row + 1, : entries.shape[1]] += jnp.sum(
-                entries.astype(f32), axis=0, keepdims=True
+    def attend_back_all():
+        d_keys[...] = jnp.zeros_like(d_keys)
+        d_values[...] = jnp.zeros_like(d_values)
+        for index in range(tiles):
+            attend_back(index)
+
+        def join(rows):
+            d_joined[rows, head_dim : 2 * head_dim] = turn(d_keys[rows] * factor, rows, -1.0).astype(bf16)
+            d_joined[rows, 2 * head_dim :] = d_values[rows].astype(bf16)
+
+        loop(join)
+
+    def qkv_grad(index):
+        start, size = sum(cut[0] for cut in QKV_CUTS[:index]), QKV_CUTS[index][0]
+        emit(
+            width // TILE,
+            lambda step: dot_rows(norm[:, rows_of(step)], d_joined[:, pl.ds(start, size)]),
+            qkv_parts,
+            size,
+            start,
+        )
+
+    def inputs():
+        sums[...] = jnp.zeros_like(sums)
+
+        def body(index):
+            rows = rows_of(index)
+            d_one = dot_cols(d_joined[rows], w_qkv[...])
+            d_two = dot_cols(d_up[rows], w_up[...])
+            scaled = scaled_rows(rows)
+
+            def gather(row, entries):
+                sums[row : row + 1, : entries.shape[1]] += jnp.sum(
+                    entries.astype(f32), axis=0, keepdims=True
+                )
+
+            gather(0, d_two * scaled)
+            gather(1, d_two)
+            gather(2, gra[rows])
+            gather(3, d_up[rows])
+            gather(4, d_one * scaled)
+            gather(5, d_one)
+            gather(6, d_joined[rows])
+            return d_one * vector(0) + d_two * vector(2)
+
+        emit(tiles, body, in_parts, width)
+
+    sums_items = []
+
+    def sums_start():
+        for bit in (1, 2, 3):
+            send_small(sums, sums_got.at[shard], sums_got.at[shard ^ bit], (ctx, shard ^ bit))
+            sums_items.append(small[-1])
+        sums_got[shard] = sums[...]
+
+    def sums_land():
+        wait_small(sums_items)
+        total = sums_got[0]
+        for index in range(1, shards):
+            total = total + sums_got[index]
+        sums_tot[...] = total
+
+    exchanged = []
+
+    def dense_block(owner):
+        return pl.ds(pl.multiple_of(owner * dense_size, dense_size), dense_size)
+
+    def own_dense():
+        return pltpu.make_async_copy(
+            dense_lines.at[dense_block(shard)], dense_all.at[dense_block(shard)], local_sems.at[2]
+        )
+
+    def exchange():
+        for bit in (1, 2, 3):
+            peer = shard ^ bit
+            send_small(
+                dense_lines.at[dense_block(peer)], dense_all.at[dense_block(shard)],
+                dense_all.at[dense_block(peer)], (ctx, peer),
             )
-
-        gather(0, d_two * scaled)
-        gather(1, d_two)
-        gather(2, gra[rows])
-        gather(3, d_up[rows])
-        gather(4, d_one * scaled)
-        gather(5, d_one)
-        gather(6, d_joined[rows])
-        return d_one * vector(0) + d_two * vector(2)
-
-    emit(tiles, inputs, in_parts, width)
-    in_sink.start()
-    sums_sent = []
-    for bit in (1, 2, 3):
-        slot = take(1)
-        copy = remote(sums, sums_got.at[shard], sems, slot, (ctx, shard ^ bit))
-        copy.start()
-        sums_sent.append((copy, sums_got.at[shard ^ bit], slot))
-    sums_got[shard] = sums[...]
-    dense_line.land(1)
-    out_sink.step(3)
-    up_lines[1].land(3)
-    qkv_fold.finish(0)
-    qkv_lines[0].start()
-    qkv_fold.finish(1)
-    qkv_lines[1].start()
-    in_sink.swap()
-    in_sink.step(1)
-    dense_line.land(2)
-    for copy, landing, slot in sums_sent:
-        remote(landing, landing, sems, slot, (ctx ^ 1, shard)).wait_recv()
-    total = sums_got[0]
-    for index in range(1, shards):
-        total = total + sums_got[index]
-    sums_tot[...] = total
-    sums_line.start()
-    dense_line.land(3)
-    qkv_lines[0].land(1)
-    in_sink.step(2)
-    sums_line.land(1)
-    qkv_lines[1].land(1)
-    dense_line.arrived()
-    dense_block = dense_size
-    exchanged = []
-    for bit in (1, 2, 3):
-        slot = take(1)
-        peer = shard ^ bit
-        rows = pl.ds(pl.multiple_of(peer * dense_block, dense_block), dense_block)
-        own_rows = pl.ds(pl.multiple_of(shard * dense_block, dense_block), dense_block)
-        copy = remote(dense_lines.at[rows], dense_all.at[own_rows], sems, slot, (ctx, peer))
-        copy.start()
-        exchanged.append((copy, dense_all.at[rows], slot))
-    own_dense = pltpu.make_async_copy(
-        dense_lines.at[own_rows], dense_all.at[own_rows], local_sems.at[2]
-    )
-    own_dense.start()
-    out_sink.finish(output_out, local_sems.at[3])
-    qkv_lines[0].land(2)
-    in_sink.step(3)
-    sums_line.land(2)
-    qkv_lines[1].land(2)
-    qkv_lines[0].land(3)
-    sums_line.land(3)
-    qkv_lines[1].land(3)
-    in_sink.finish(input_out, local_sems.at[3])
+            exchanged.append(small[-1])
+        own_dense().start()
+
+    steps = {
+        "small_start": small_start, "small_land": small_land, "norm_two": lambda: loop(norm_two),
+        "norm_one": lambda: loop(norm_one), "feed_forward": feed_forward, "down_grad": down_grad,
+        "feed_back": feed_back, "up_grad": up_grad, "project": project, "attend": attend_all, "output": output,
+        "dense_grad": dense_grad, "attend_back": attend_back_all, "qkv_grad": qkv_grad, "inputs": inputs,
+        "sums_start": sums_start, "sums_land": sums_land, "exchange": exchange,
+        "output_done": lambda: out_sink.finish(output_out, local_sems.at[3]),
+        "input_done": lambda: in_sink.finish(input_out, local_sems.at[3]),
+    }
+    for step in ORDER:
+        name, *rest = step.split(".")
+        if name in steps:
+            steps[name](*[int(number) for number in rest])
+        else:
+            getattr(named[name], rest[0])(*[int(number) for number in rest[1:]])
 
     write_vec = pltpu.make_async_copy(vec, vec_out, local_sems.at[8])
     write_vec.start()
-    lines = down_lines + up_lines + qkv_lines + [sums_line]
     for item in lines:
-        item.arrived()
-    for copy, landing, slot in exchanged:
-        remote(landing, landing, sems, slot, (ctx ^ 1, shard)).wait_recv()
-    own_dense.wait()
-    for item in [hid_line, gra_line, dense_line] + lines + squares + [tree]:
+        if item is not named["le00"]:
+            item.arrived()
+    wait_small(exchanged)
+    own_dense().wait()
+    for item in [hid_line, gra_line] + lines + squares + [tree] + folds:
         item.sent()
-    for item in (down_fold, up_fold, qkv_fold, dense_fold):
-        item.sent()
-    for copy, _, _ in small + sums_sent + exchanged:
+    for copy, _, _ in small:
         copy.wait_send()
     write_vec.wait()
+
+
+DOWN_CUTS = ((512, False), (512, False), (1024, True))
+UP_CUTS = ((512, True), (512, True))
+QKV_CUTS = ((768, True),)
+DENSE_CUTS = ((512, False),)
+
+ORDER = (
+    "wu.start", "hid.start", "gra.start", "small_start", "hid.land.1", "wu.forward", "gra.land.1", "wd.start",
+    "hid.land.2", "hid.land.3", "small_land", "wd.forward", "wu.arrived", "hid.arrived", "norm_two", "gra.land.2",
+    "feed_forward", "gra.land.3", "gra.arrived", "down_grad.2", "fd2.send.3", "wd.arrived", "feed_back", "up_grad.0",
+    "fu0.send.3", "fd2.middle.1", "fd2.middle.0", "fu0.send.2", "down_grad.1", "fd2.finish.1", "ld21.start",
+    "fu0.middle.1", "fd2.finish.0", "fu0.send.1", "ld20.start", "fd1.middle.0", "fu0.finish.1", "lu01.start",
+    "fu0.send.0", "ld21.land.1", "fd1.send.3", "down_grad.0", "ld20.land.1", "fd0.send.3", "fd1.middle.1",
+    "fu0.middle.0", "wq.start", "lu01.land.1", "fu0.finish.0", "ld20.land.2", "lu00.start", "ld20.land.3",
+    "wq.forward", "fd1.finish.0", "fd0.middle.1", "fd0.middle.0", "wt.start", "lu01.land.2", "lu00.land.1",
+    "up_grad.1", "fu1.send.3", "lu00.land.2", "fd1.finish.1", "ld10.start", "fd0.finish.1", "fd0.finish.0",
+    "ld00.start", "ld10.land.1", "norm_one", "wq.arrived", "wt.forward", "project", "ld00.land.1", "attend",
+    "ld21.land.2", "fu1.send.1", "fu1.send.0", "ld10.land.2", "fu1.send.2", "dense_grad", "ld00.land.2",
+    "wt.arrived", "attend_back", "fe0.send.1", "fu1.middle.1", "fu1.middle.0", "qkv_grad.0", "fq0.send.1",
+    "fq0.send.3", "fu1.finish.0", "lu10.start", "fq0.send.0", "ld21.land.3", "fq0.send.2", "fu1.finish.1",
+    "lu11.start", "output", "so.start", "lu10.land.1", "fq0.middle.0", "fq0.middle.1", "lu11.land.1", "lu01.land.3",
+    "lu10.land.2", "so.swap", "so.step.1", "fq0.finish.0", "lq00.start", "fq0.finish.1", "lq01.start", "lu11.land.2",
+    "fe0.send.3", "inputs", "sums_start", "ld00.land.3", "lq00.land.1", "so.step.2", "fe0.send.2", "si.start",
+    "sums_land", "ls.start", "fe0.middle.1", "lu11.land.3", "lu00.land.3", "fe0.send.0", "fe0.middle.0",
+    "lq01.land.1", "fe0.finish.1", "fe0.finish.0", "le00.start", "si.swap", "ls.land.1", "lu10.land.3", "si.step.1",
+    "lq00.land.2", "le00.land.1", "si.step.2", "ls.land.2", "ls.land.3", "le00.land.2", "so.step.3", "ld10.land.3",
+    "si.step.3", "lq00.land.3", "le00.land.3", "lq01.land.2", "le00.arrived", "exchange", "output_done",
+    "input_done", "lq01.land.3",
+)
 
 
 def rotary_table(length, lanes):
@@ -1087,7 +1078,7 @@
     return table
 
 
-def whole_block(hidden, grad, fc1, fc2, qkv, dense, vectors, segs):
+def whole_block(hidden, grad, fc1, fc2, qkv, dense, segs, vectors):
     chips, shards = lax.axis_size("ctx") // CORES, lax.axis_size("fsdp")
     count = chips * CORES
     tokens, width = hidden.shape
@@ -1098,8 +1089,9 @@
     rows = width // shards
     bf16, f32 = jnp.bfloat16, jnp.float32
     wide, joint = (length, width), 3 * head_dim
-    vec_shape = (shards,) + vectors.shape
-    seg_shape = (segs.shape[0] * count, segs.shape[1])
+    vectors = [vector.reshape(1, -1) for vector in vectors]
+    vec_shape = (shards, sum(vector.shape[1] for vector in vectors) // rows, 1, rows)
+    seg_shape = (count,) + segs.shape
     line = (tokens, width)
     hops = (2 * (chips - 1) * tokens, width)
     outs = [
@@ -1111,6 +1103,7 @@
         (wide, bf16), ((chips * tokens, width), bf16), (hops, bf16), ((count * head_dim, rows), bf16),
     ]
     table = rotary_table(length, 128)
+    cuts = DOWN_CUTS + UP_CUTS + QKV_CUTS + DENSE_CUTS
     halves = [(part // 2, width), (rows // 2, units), (rows // 2, joint), (head_dim // 2, rows)]
     scratch = [
         (wide, bf16), (wide, bf16), (wide, bf16), ((width, units), bf16), ((units, width), bf16),
@@ -1127,91 +1120,141 @@
     scratch += [((2 * half[0], half[1]), bf16) for half in halves]
     scratch += [((2, tokens, width), bf16), ((2, tokens, width), bf16), (line, f32)]
     slots = (
-        10 * Line.slots(chips) + 3 * Square.SLOTS + Tree.SLOTS + 4 * Fold.SLOTS + 2 * Sink.slots(chips)
-        + 9 + count - 1
+        (3 + sum(1 + split for _, split in cuts)) * Line.slots(chips)
+        + 3 * Square.SLOTS + Tree.SLOTS + len(cuts) * Fold.SLOTS + 2 * Sink.slots(chips) + 9 + count - 1
     )
     outputs = pl.pallas_call(
         functools.partial(block_kernel, (chips, shards, part)),
         out_shape=[jax.ShapeDtypeStruct(shape, kind) for shape, kind in outs],
-        in_specs=[pl.BlockSpec(memory_space=pl.ANY)] * 9,
+        in_specs=[pl.BlockSpec(memory_space=pl.ANY)] * 16,
         out_specs=[pl.BlockSpec(memory_space=pl.ANY)] * len(outs),
         scratch_shapes=[pltpu.VMEM(shape, kind) for shape, kind in scratch]
         + [
             pltpu.SemaphoreType.DMA((slots,)),
             pltpu.SemaphoreType.DMA((slots,)),
-            pltpu.SemaphoreType.DMA((11,)),
+            pltpu.SemaphoreType.DMA((24,)),
         ],
         compiler_params=pltpu.CompilerParams(
             collective_id=0, has_side_effects=True, vmem_limit_bytes=62 * 2**20
         ),
         name="whole_block",
-    )(hidden, grad, fc1, fc2, qkv, dense, vectors, segs, jnp.asarray(table))
+    )(hidden, grad, fc1, fc2, qkv, dense, segs, jnp.asarray(table), *vectors)
     return outputs[:8]
 
 
-def widen(blocks, groups, pieces):
-    rows, size = blocks.shape[0] // groups, blocks.shape[1] // pieces
-
-    def body(src, dst):
-        dst[...] = src[...].astype(jnp.float32)
-
+FINISH_STEPS = 16
+
+
+def finish_kernel(
+    sizes,
+    up_all, qkv_all, dense_all, down_all, vec, branch, back, hidden, grad, sums,
+    output, input_grad, gain_one, shift_one, qkv, qkv_bias, dense, columns_one, gain_two, shift_two, up, up_bias,
+    down, columns_two,
+):
+    count, shards = sizes
+    f32 = jnp.float32
+
+    def spread(src, dst, pieces):
+        groups, size = src.shape[0], src.shape[2] // pieces
+        for piece in range(pieces):
+            for group in range(groups):
+                start = (piece * groups + group) * size
+                dst[:, start : start + size] = src[group, :, piece * size : (piece + 1) * size].astype(f32)
+
+    spread(up_all, up, shards)
+    spread(qkv_all, qkv, 3)
+    spread(dense_all, dense, 1)
+    down[...] = down_all[...].astype(f32)
+
+    @pl.when(pl.program_id(0) == 0)
+    def _():
+        own = hidden[...].astype(f32)
+        shift = jnp.concatenate([vec[index, 4] + vec[index, 5] for index in range(shards)], axis=1)
+        output[...] = (own + branch[...] + shift).astype(output.dtype)
+        scaled, spread_own = centred(own)
+        e = back[...]
+        part = spread_own * (
+            e
+            - jnp.mean(e, axis=-1, keepdims=True)
+            - scaled * jnp.mean(e * scaled, axis=-1, keepdims=True)
+        )
+        input_grad[...] = (grad[...].astype(f32) + part).astype(input_grad.dtype)
+
+        shard = lax.axis_index("fsdp")
+        rows = gain_one.shape[1]
+        mine = pl.ds(pl.multiple_of(shard * rows, rows), rows)
+        for row, dst in ((0, gain_two), (1, shift_two), (4, gain_one), (5, shift_one)):
+            total = sums[0, row : row + 1, mine]
+            for index in range(1, count):
+                total = total + sums[index, row : row + 1, mine]
+            dst[...] = total
+        columns_one[...] = sums[0, 2:3, mine]
+        columns_two[...] = sums[0, 2:3, mine]
+        part = up_bias.shape[1] // count
+        here = pl.ds(pl.multiple_of(shard * part, part), part)
+        for index in range(count):
+            up_bias[:, index * part : (index + 1) * part] = sums[index, 3:4, here]
+        size = 3 * hidden.shape[1] // (3 * count)
+        chunks = qkv_bias.shape[1] // size
+        for chunk in range(chunks):
+            place = shard * chunks + chunk
+            start = pl.multiple_of(place // count * size, size)
+            qkv_bias[:, chunk * size : (chunk + 1) * size] = sums[
+                lax.rem(place, count), 6:7, pl.ds(start, size)
+            ]
+
+
+def finish(up_all, qkv_all, dense_all, down_all, vec, branch, back, hidden, grad, sums):
+    count, shards = lax.axis_size("ctx"), lax.axis_size("fsdp")
+    tokens, width = hidden.shape
+    rows = width // shards
+    f32 = jnp.float32
+    steps = FINISH_STEPS
+
+    def sliced(shape):
+        block = shape[:-2] + (shape[-2] // steps, shape[-1])
+        return pl.BlockSpec(block, lambda index: (0,) * (len(shape) - 2) + (index, 0))
+
+    def entire(shape):
+        return pl.BlockSpec(shape, lambda index: (0,) * len(shape))
+
+    grads = [
+        up_all.reshape(count, rows, -1), qkv_all.reshape(count, rows, -1), dense_all.reshape(shards, rows, rows),
+        down_all,
+    ]
+    units = up_all.shape[1] * count
+    sums = sums.reshape(count, 8, width)
+    others = [vec, branch, back, hidden, grad, sums]
+    vector = (1, rows)
+    outs = [
+        ((tokens, width), hidden.dtype, entire), ((tokens, width), hidden.dtype, entire),
+        (vector, f32, entire), (vector, f32, entire), ((rows, 3 * width), f32, sliced),
+        ((1, 3 * rows), f32, entire), ((rows, width), f32, sliced), (vector, f32, entire),
+        (vector, f32, entire), (vector, f32, entire), ((rows, units), f32, sliced),
+        ((1, units // shards), f32, entire), (down_all.shape, f32, sliced), (vector, f32, entire),
+    ]
     return pl.pallas_call(
-        body,
-        grid=(groups, pieces),
-        in_specs=[pl.BlockSpec((rows, size), lambda group, piece: (group, piece))],
-        out_specs=pl.BlockSpec((rows, size), lambda group, piece: (0, piece * groups + group)),
-        out_shape=jax.ShapeDtypeStruct((rows, pieces * groups * size), jnp.float32),
-        name="widen",
-    )(blocks)
+        functools.partial(finish_kernel, (count, shards)),
+        grid=(steps,),
+        in_specs=[sliced(array.shape) for array in grads] + [entire(array.shape) for array in others],
+        out_specs=[kind(shape) for shape, _, kind in outs],
+        out_shape=[jax.ShapeDtypeStruct(shape, dtype) for shape, dtype, _ in outs],
+        compiler_params=pltpu.CompilerParams(vmem_limit_bytes=62 * 2**20),
+        name="finish",
+    )(*grads, *others)
 
 
 def one_kernel(
     hidden, qkv_weight, dense_weight, fc1_weight, fc2_weight, segments, out_grad, vectors
 ):
-    shards, count = lax.axis_size("fsdp"), lax.axis_size("ctx")
-    shard = lax.axis_index("fsdp")
-    tokens, width = hidden.shape[1], hidden.shape[2]
-    rows = width // shards
-    head_dim = width // HEADS
-    f32, bf16 = jnp.float32, jnp.bfloat16
     vec, branch, back, down_all, up_all, qkv_all, dense_all, sums_all = whole_block(
-        hidden[0], out_grad[0], fc1_weight, fc2_weight, qkv_weight, dense_weight, vectors,
-        jnp.broadcast_to(segments, (8, tokens)),
-    )
-    own = hidden[0].astype(f32)
-    shift = vec[:, 4].reshape(-1) + vec[:, 5].reshape(-1)
-    layer_output = (own + branch + shift).astype(bf16)
-    scaled, spread = centred(own)
-    input_part = spread * (
-        back
-        - jnp.mean(back, axis=-1, keepdims=True)
-        - scaled * jnp.mean(back * scaled, axis=-1, keepdims=True)
-    )
-    input_grad = (out_grad[0].astype(f32) + input_part).astype(bf16)
-    sums = sums_all.reshape(count, 8, width)
-    mine = lax.dynamic_slice_in_dim(sums, shard * rows, rows, 2)
-    totals = jnp.sum(mine, axis=0)
-    part = fc1_weight.shape[1] // count // shards
-    up_sum = lax.dynamic_slice_in_dim(sums[:, 3], shard * part, part, 1).reshape(-1)
-    joined = sums[:, 6, : 3 * head_dim].reshape(count, 3, head_dim).transpose(1, 0, 2).reshape(-1)
-    joined = lax.dynamic_slice_in_dim(joined, shard * 3 * rows, 3 * rows, 0)
-    columns = mine[0, 2]
-    return (
-        layer_output[None],
-        input_grad[None],
-        totals[4],
-        totals[5],
-        widen(qkv_all, count, 3),
-        joined,
-        widen(dense_all, shards, 1),
-        columns,
-        totals[0],
-        totals[1],
-        widen(up_all, count, shards),
-        up_sum,
-        widen(down_all, 1, 8),
-        columns,
-    )
+        hidden[0], out_grad[0], fc1_weight, fc2_weight, qkv_weight, dense_weight, segments, vectors
+    )
+    outs = finish(
+        up_all, qkv_all, dense_all, down_all, vec, branch, back, hidden[0], out_grad[0], sums_all
+    )
+    outs = [out.reshape(-1) if out.shape[0] == 1 else out for out in outs]
+    return (outs[0][None], outs[1][None], *outs[2:])
 
 
 def per_device(
@@ -1245,14 +1288,12 @@
     units = ff // shards // ctx_count
     bf16, f32 = jnp.bfloat16, jnp.float32
 
-    vectors = jnp.concatenate(
-        [ln1_gain, ln1_bias, ln2_gain, ln2_bias, dense_bias, fc2_bias, qkv_bias, fc1_bias]
-    ).reshape(-1, rows)
-    vectors = jnp.pad(vectors, ((0, -vectors.shape[0] % 8), (0, 0)))
+    vectors = [ln1_gain, ln1_bias, ln2_gain, ln2_bias, dense_bias, fc2_bias, qkv_bias, fc1_bias]
     if ctx_count == HEADS and shards == 4:
         return one_kernel(
             hidden, qkv_weight, dense_weight, fc1_weight, fc2_weight, segments, out_grad, vectors
         )
+    vectors = jnp.concatenate(vectors).reshape(-1, rows)
     vec = lax.all_gather(vectors, "fsdp", axis=0)
     query_seg = lax.all_gather(segments[0], "ctx", axis=0, tiled=True)
     up_part = lax.dynamic_index_in_dim(

time: 441 us -> 369 us (0.84); the launches traced: 434 us -> 367 us
  Pallas kernels: 414 us -> 364 us
  local copies, waits for them, and re-layouts: 12.8 us -> 1.29 us
  other arithmetic: 6.97 us -> 1.31 us
    pallas_call x1, Pallas kernels: 363 us -> 335 us  [whole_block(): pl.pallas_call(functools.partial(block_kernel, (chips, shards, part)), ou...]
    pallas_call x4 -> x1, Pallas kernels: 50.5 us -> 29.1 us  [finish(): pl.pallas_call(functools.partial(finish_kernel, (count, shards)), grid=(s...]
    unnamed x16 -> x0, local copies, waits for them, and re-layouts: 5.43 us -> none
where the time goes in v4:
time: 369 us; the launch traced here: 367 us
  Pallas kernels  364 us (99%)
    pallas_call x1, Pallas kernels, whole_block(): pl.pallas_call(functools.partial(block_kernel, (chips, shards, part)), ou...  335 us
    pallas_call x1, Pallas kernels, finish(): pl.pallas_call(functools.partial(finish_kernel, (count, shards)), grid=(s...  29.1 us

profile of v4, /device:TPU:0, one launch (start us, length us, event | category | flops | bytes accessed | tf_op | source)
XLA Modules:
  0.0 367.0 jit_solution(14441725456579324899)
XLA Ops:
  0.6 1.3 reshape.94.qkv_bias
  1.9 334.7 %whole_block.1 = (f32[4,13,1,512]{3,2,1,0:T(1,128)}, f32[128,2048]{1,0:T(8,128)}, f32[128,2048]{1,0:T(8,128)}, bf16[2048,2048]{1,0:T(8,128)(2,1)}, bf16[4096,102...) custom-call(bf16[128,2048]{1,0:T(8,128)(2,1)} %bitcast.25, ...), custom_call_target="tpu_custom_call" | custom-call | tf_op jit(solution)/shard_map/whole_block/pallas_call | solution.py:1126
  336.6 29.1 %finish.1 = (bf16[128,2048]{1,0:T(8,128)(2,1)}, bf16[128,2048]{1,0:T(8,128)(2,1)}, f32[1,512]{1,0:T(1,128)}, f32[1,512]{1,0:T(1,128)}, f32[512,6144]{1,0:T(8,128...) custom-call(bf16[8,512,1024]{2,1,0:T(8,128)(2,1)} %bitcast.22, ...), custom_call_target="tpu_custom_call" | custom-call | tf_op jit(solution)/shard_map/finish/pallas_call | solution.py:1236
  365.7 1.3 reduce

commit v5 on v4

--- a/solution.py
+++ b/solution.py
@@ -129,20 +129,16 @@
     def slots(chips):
         return 4 * (chips - 1) + 2
 
-    def hop(self, up, number):
-        step = 1 if up else -1
-        slot = (0 if up else self.chips - 1) + number - 1
-        origin = self.ctx - step * (number - 1) * CORES
-        if up:
-            sends = (self.chip >= number - 1) & (self.chip < self.chips - 1)
-            gets = self.chip >= number
-        else:
-            sends = (self.chip <= self.chips - number) & (self.chip > 0)
-            gets = self.chip <= self.chips - 1 - number
-        return slot, step, origin, sends, gets
-
-    def send(self, up, number):
-        slot, step, origin, sends, _ = self.hop(up, number)
+    def hop(self, out, number):
+        up = (self.chip >= self.chips // 2) == out
+        place = jnp.where(up, self.chip, self.chips - 1 - self.chip)
+        step = jnp.where(up, CORES, -CORES)
+        slot = jnp.where(up, 0, self.chips - 1) + number - 1
+        sends = (place >= number - 1) & (place < self.chips - 1)
+        return slot, step, self.ctx - step * (number - 1), sends, place >= number
+
+    def send(self, out, number):
+        slot, step, origin, sends, _ = self.hop(out, number)
 
         @pl.when(sends)
         def _():
@@ -151,7 +147,7 @@
                 self.block(origin),
                 self.sems,
                 self.base + slot,
-                (self.ctx + step * CORES, self.shard),
+                (self.ctx + step, self.shard),
             ).start()
 
     def start(self):
@@ -165,34 +161,39 @@
         )
         self.local.start()
 
-    def land(self, number):
-        for up in (True, False):
-            slot, step, origin, _, gets = self.hop(up, number)
-            block = self.block(origin - step * CORES)
-
-            @pl.when(gets)
-            def _(block=block, slot=slot):
-                remote(
-                    block, block, self.sems, self.base + slot, (self.ctx ^ 1, self.shard)
-                ).wait_recv()
-
-            if number < self.chips - 1:
-                self.send(up, number + 1)
-
-            @pl.when(gets)
-            def _(block=block, slot=slot):
-                remote(
-                    block, block, self.sems, self.swap_base + slot, (self.ctx ^ 1, self.shard)
-                ).start()
+    def land(self, out, number):
+        slot, step, origin, _, gets = self.hop(out, number)
+        block = self.block(origin - step)
+
+        @pl.when(gets)
+        def _():
+            remote(
+                block, block, self.sems, self.base + slot, (self.ctx ^ 1, self.shard)
+            ).wait_recv()
+
+        if number < self.chips - 1:
+            self.send(out, number + 1)
+
+        @pl.when(gets)
+        def _():
+            remote(
+                block, block, self.sems, self.swap_base + slot, (self.ctx ^ 1, self.shard)
+            ).start()
+
+    def out(self, number):
+        self.land(True, number)
+
+    def inward(self, number):
+        self.land(False, number)
 
     def arrived(self):
         other = self.block(self.ctx ^ 1)
         remote(other, other, self.sems, self.own_slot, (self.ctx ^ 1, self.shard)).wait_recv()
         self.local.wait()
-        for up in (True, False):
+        for out in (True, False):
             for number in range(1, self.chips):
-                slot, step, origin, _, gets = self.hop(up, number)
-                block = self.block((origin - step * CORES) ^ 1)
+                slot, step, origin, _, gets = self.hop(out, number)
+                block = self.block((origin - step) ^ 1)
 
                 @pl.when(gets)
                 def _(block=block, slot=slot):
@@ -204,9 +205,9 @@
         source = self.source
         peer = (self.ctx ^ 1, self.shard)
         remote(source, source, self.sems, self.own_slot, peer).wait_send()
-        for up in (True, False):
+        for out in (True, False):
             for number in range(1, self.chips):
-                slot, _, _, sends, gets = self.hop(up, number)
+                slot, _, _, sends, gets = self.hop(out, number)
 
                 @pl.when(sends)
                 def _(slot=slot):
@@ -244,11 +245,11 @@
                 self.to(bit),
             ).start()
 
-    def start(self):
-        self.own(1, 0)
-        self.own(2, 1)
-        self.own(1, 1)
-        self.own(2, 0)
+    def start(self, part):
+        self.own(1, part)
+        self.own(2, 1 - part)
+        if part == 1:
+            return
         for which in (0, 1):
             for source, columns in self.pieces(which):
                 pltpu.make_async_copy(
@@ -285,7 +286,7 @@
 
 
 class Tree:
-    SLOTS = 8
+    SLOTS = 7
 
     def __init__(self, source, block, sems, base, place, owner):
         self.source, self.block, self.sems, self.base = source, block, sems, base
@@ -296,61 +297,61 @@
     def rows(self, ref, which):
         return ref.at[pl.ds(which * self.half, self.half)]
 
-    def copy(self, ref, which, slot, bit):
+    def copy(self, slot, ref=None):
+        which = slot % 2
+        bit = 1 if slot in (0, 3, 4) else 2
         return remote(
-            self.rows(ref, which),
+            self.rows(self.block if ref is None else ref, which),
             self.rows(self.block, which),
             self.sems,
             self.base + slot,
             (self.ctx, self.shard ^ bit),
         )
 
+    def at(self, turn, body):
+        pl.when(self.turn == turn)(body)
+
     def start(self):
-        @pl.when(self.turn == 0)
-        def _():
-            self.copy(self.source, 0, 0, 1).start()
-            self.copy(self.source, 1, 3, 2).start()
-            self.copy(self.source, 1, 1, 1).start()
-            self.copy(self.source, 0, 2, 2).start()
+        def body():
+            self.copy(0, self.source).start()
+            self.copy(1, self.source).start()
             pltpu.make_async_copy(self.source, self.block, self.sems[0].at[self.base + 6]).start()
 
+        self.at(0, body)
+
     def forward(self):
-        for bit in (1, 2):
-            which = bit - 1
-
-            @pl.when(self.turn == bit)
-            def _(bit=bit, which=which):
-                self.copy(self.block, which, 2 * (bit - 1) + which, bit).wait_recv()
-                self.copy(self.block, which, 4 + which, 3 - bit).start()
+        for turn, slot in ((1, 0), (2, 1)):
+
+            def body(slot=slot):
+                self.copy(slot).wait_recv()
+                self.copy(slot + 2).start()
+
+            self.at(turn, body)
+
+    def back(self):
+        def body():
+            for slot in (2, 3):
+                self.copy(slot).wait_recv()
+                self.copy(slot + 2).start()
+
+        self.at(3, body)
 
     def arrived(self):
-        @pl.when(self.turn == 0)
-        def _():
+        def body():
             pltpu.make_async_copy(self.source, self.block, self.sems[0].at[self.base + 6]).wait()
 
-        for bit in (1, 2):
-
-            @pl.when(self.turn == bit)
-            def _(bit=bit):
-                which = 2 - bit
-                self.copy(self.block, which, 2 * (bit - 1) + which, bit).wait_recv()
-
-        @pl.when(self.turn == 3)
-        def _():
-            self.copy(self.block, 0, 4, 2).wait_recv()
-            self.copy(self.block, 1, 5, 1).wait_recv()
+        self.at(0, body)
+        self.at(1, lambda: self.copy(5).wait_recv())
+        self.at(2, lambda: self.copy(4).wait_recv())
 
     def sent(self):
-        @pl.when(self.turn == 0)
-        def _():
-            for slot in range(4):
-                self.copy(self.block, 0, slot, 1).wait_send()
-
-        for bit in (1, 2):
-
-            @pl.when(self.turn == bit)
-            def _(bit=bit):
-                self.copy(self.block, bit - 1, 3 + bit, 3 - bit).wait_send()
+        for turn, slots in ((0, (0, 1)), (1, (2,)), (2, (3,)), (3, (4, 5))):
+
+            def body(slots=slots):
+                for slot in slots:
+                    self.copy(slot).wait_send()
+
+            self.at(turn, body)
 
 
 def add_rows(dst, sources):
@@ -458,26 +459,27 @@
         swapped = self.swapped
         remote(swapped, swapped, self.sems, self.base, (self.ctx ^ 1, self.shard)).wait_recv()
 
-    def hop(self, up, step):
-        place = self.chip if up else self.chips - 1 - self.chip
+    def hop(self, out, step):
+        up = (self.chip >= self.chips // 2) == out
+        place = jnp.where(up, self.chip, self.chips - 1 - self.chip)
         target = place + self.chips - step
-        target = target if up else self.chips - 1 - target
-        slot = (0 if up else self.chips - 1) + step - 1
+        target = jnp.where(up, target, self.chips - 1 - target)
+        slot = jnp.where(up, 0, self.chips - 1) + step - 1
         sends = (place + 1 <= step) & (place < self.chips - 1)
         gets = (place <= step) & (place > 0)
         return slot, target, sends, gets, place > 0
 
     def landed(self, slot):
-        return self.landing.at[pl.ds(slot * self.rows, self.rows)]
-
-    def copy(self, up, slot):
-        way = CORES if up else -CORES
+        return self.landing.at[pl.ds(pl.multiple_of(slot * self.rows, self.rows), self.rows)]
+
+    def copy(self, out, slot):
+        up = (self.chip >= self.chips // 2) == out
         return remote(
-            self.carry.at[0 if up else 1],
+            self.carry.at[0 if out else 1],
             self.landed(slot),
             self.sems,
             self.base + 1 + slot,
-            (self.ctx + way, self.shard),
+            (self.ctx + jnp.where(up, CORES, -CORES), self.shard),
         )
 
     def load(self, index, source):
@@ -489,81 +491,107 @@
             self.load(1, self.block(self.swapped, target)),
         ]
 
-    def step(self, number):
-        for up in (True, False):
-            slot, target, sends, _, passes = self.hop(up, number)
+    def step(self, out, number):
+        slot, target, sends, _, passes = self.hop(out, number)
+        if number > 1:
+            before, _, sent, gets, _ = self.hop(out, number - 1)
+
+            @pl.when(gets)
+            def _():
+                remote(
+                    self.landed(before), self.landed(before), self.sems, self.base + 1 + before,
+                    (self.ctx ^ 1, self.shard),
+                ).wait_recv()
+
+            @pl.when(sent)
+            def _():
+                self.copy(out, before).wait_send()
+
+        @pl.when(sends)
+        def _():
+            loads = self.own(target)
+            for load in loads:
+                load.start()
+            carry = self.carry.at[0 if out else 1]
+            stage = self.stage
             if number > 1:
-                before, _, sent, gets, _ = self.hop(up, number - 1)
-
-                @pl.when(gets)
-                def _(before=before, up=up):
-                    remote(
-                        self.landed(before), self.landed(before), self.sems, self.base + 1 + before,
-                        (self.ctx ^ 1, self.shard),
-                    ).wait_recv()
-
-                @pl.when(sent)
-                def _(before=before, up=up):
-                    self.copy(up, before).wait_send()
+
+                @pl.when(passes)
+                def _():
+                    more = self.load(2, self.landed(slot - 1))
+                    more.start()
+                    for load in loads + [more]:
+                        load.wait()
+                    add_rows(carry, [stage.at[0], stage.at[1], stage.at[2]])
+
+                @pl.when(jnp.logical_not(passes))
+                def _():
+                    for load in loads:
+                        load.wait()
+                    add_rows(carry, [stage.at[0], stage.at[1]])
+            else:
+                for load in loads:
+                    load.wait()
+                add_rows(carry, [stage.at[0], stage.at[1]])
+            self.copy(out, slot).start()
+
+    def inward(self, number):
+        self.step(False, number)
+
+    def last(self, handed, first, own, sem):
+        number = self.chips - 1
+        for out in (True, False):
+            slot, target, sends, _, passes = self.hop(out, number)
+            before, _, sent, gets, _ = self.hop(out, number - 1)
+
+            @pl.when(gets)
+            def _(before=before):
+                remote(
+                    self.landed(before), self.landed(before), self.sems, self.base + 1 + before,
+                    (self.ctx ^ 1, self.shard),
+                ).wait_recv()
+
+            @pl.when(sent)
+            def _(out=out, before=before):
+                self.copy(out, before).wait_send()
 
             @pl.when(sends)
-            def _(up=up, slot=slot, target=target, passes=passes):
+            def _(out=out, slot=slot, target=target, passes=passes):
                 loads = self.own(target)
                 for load in loads:
                     load.start()
-                carry = self.carry.at[0 if up else 1]
-                stage = self.stage
-                if number > 1:
-
-                    @pl.when(passes)
-                    def _():
-                        more = self.load(2, self.landed(slot - 1))
-                        more.start()
-                        for load in loads + [more]:
-                            load.wait()
-                        add_rows(carry, [stage.at[0], stage.at[1], stage.at[2]])
-
-                    @pl.when(jnp.logical_not(passes))
-                    def _():
-                        for load in loads:
-                            load.wait()
-                        add_rows(carry, [stage.at[0], stage.at[1]])
-                else:
-                    for load in loads:
-                        load.wait()
-                    add_rows(carry, [stage.at[0], stage.at[1]])
-                self.copy(up, slot).start()
-
-    def finish(self, dst, sem):
+                for load in loads:
+                    load.wait()
+                carry = self.carry.at[0 if out else 1]
+                add_rows(carry, [self.stage.at[0], self.stage.at[1]])
+
+                @pl.when(passes)
+                def _():
+                    more = self.load(2, self.landed(slot - 1))
+                    more.start()
+                    more.wait()
+                    add_rows(carry, [self.stage.at[0], self.stage.at[1], self.stage.at[2]])
+
+                up = (self.chip >= self.chips // 2) == out
+                for way, dst in ((True, handed[0]), (False, handed[1])):
+
+                    @pl.when(up == way)
+                    def _(dst=dst):
+                        write = pltpu.make_async_copy(carry, dst.at[pl.ds(first, self.rows)], sem)
+                        write.start()
+                        write.wait()
+
         loads = self.own(self.chip)
         for load in loads:
             load.start()
         for load in loads:
             load.wait()
         add_rows(self.final, [self.stage.at[0], self.stage.at[1]])
-        for up in (True, False):
-            slot, _, sends, gets, _ = self.hop(up, self.chips - 1)
-
-            @pl.when(gets)
-            def _(slot=slot):
-                landed = self.landed(slot)
-                remote(
-                    landed, landed, self.sems, self.base + 1 + slot, (self.ctx ^ 1, self.shard)
-                ).wait_recv()
-                load = self.load(2, landed)
-                load.start()
-                load.wait()
-                add_rows(self.final, [self.final, self.stage.at[2]])
-
-            @pl.when(sends)
-            def _(up=up, slot=slot):
-                self.copy(up, slot).wait_send()
-
         swapped = self.swapped
         remote(swapped, swapped, self.sems, self.base, (self.ctx ^ 1, self.shard)).wait_send()
-        copy = pltpu.make_async_copy(self.final, dst, sem)
-        copy.start()
-        copy.wait()
+        write = pltpu.make_async_copy(self.final, own, sem)
+        write.start()
+        write.wait()
 
 
 TILE = 256
@@ -573,7 +601,7 @@
     sizes,
     hidden, grad, fc1, fc2, qkv, dense, segs, tables,
     ln1_gain, ln1_bias, ln2_gain, ln2_bias, dense_bias, fc2_bias, qkv_bias, fc1_bias,
-    vec_out, output_out, input_out, down_all, up_all, qkv_all, dense_all, sums_all,
+    vec_out, output_out, input_out, up_out, down_out, down_all, up_all, qkv_all, dense_all, sums_all,
     down_parts, up_parts, qkv_parts, dense_parts, down_land, up_land, qkv_land, dense_land,
     out_parts, out_swap, out_land, in_parts, in_swap, in_land, dense_lines,
     hid, gra, norm, w_up, w_down, w_qkv, w_dense, vec, seg, seg_col, table,
@@ -804,7 +832,7 @@
             )
             write.start()
             write.wait()
-            for number, slot in ((0, 1), (1, 2), (2, 0)):
+            for number, slot in ((0, 1), (0, 3), (1, 2), (2, 0)):
 
                 @pl.when(step == number)
                 def _(slot=slot):
@@ -995,44 +1023,66 @@
             dense_lines.at[dense_block(shard)], dense_all.at[dense_block(shard)], local_sems.at[2]
         )
 
+    def dense_part(owner, side):
+        size = dense_size // CORES
+        return pl.ds(pl.multiple_of(owner * dense_size + side * size, size), size)
+
     def exchange():
         for bit in (1, 2, 3):
             peer = shard ^ bit
             send_small(
-                dense_lines.at[dense_block(peer)], dense_all.at[dense_block(shard)],
-                dense_all.at[dense_block(peer)], (ctx, peer),
+                dense_lines.at[dense_part(peer, core)], dense_all.at[dense_part(shard, core)],
+                dense_all.at[dense_part(peer, core)], (ctx, peer),
             )
             exchanged.append(small[-1])
         own_dense().start()
+
+    relayed = []
+
+    def relay():
+        wait_small(exchanged)
+        for bit in (1, 2, 3):
+            rows = dense_part(shard ^ bit, core)
+            send_small(
+                dense_all.at[rows], dense_all.at[rows], dense_all.at[dense_part(shard ^ bit, 1 - core)],
+                (ctx ^ 1, shard),
+            )
+            relayed.append(small[-1])
+
+    def relay_done():
+        wait_small(relayed)
+        own_dense().wait()
 
     steps = {
         "small_start": small_start, "small_land": small_land, "norm_two": lambda: loop(norm_two),
         "norm_one": lambda: loop(norm_one), "feed_forward": feed_forward, "down_grad": down_grad,
         "feed_back": feed_back, "up_grad": up_grad, "project": project, "attend": attend_all, "output": output,
         "dense_grad": dense_grad, "attend_back": attend_back_all, "qkv_grad": qkv_grad, "inputs": inputs,
-        "sums_start": sums_start, "sums_land": sums_land, "exchange": exchange,
-        "output_done": lambda: out_sink.finish(output_out, local_sems.at[3]),
-        "input_done": lambda: in_sink.finish(input_out, local_sems.at[3]),
+        "sums_start": sums_start, "sums_land": sums_land, "exchange": exchange, "relay": relay,
+        "relay_done": relay_done,
+        "output_done": lambda: out_sink.last((up_out, down_out), 0, output_out, local_sems.at[3]),
+        "input_done": lambda: in_sink.last(
+            (up_out, down_out), hidden.shape[0], input_out, local_sems.at[3]
+        ),
     }
     for step in ORDER:
         name, *rest = step.split(".")
         if name in steps:
             steps[name](*[int(number) for number in rest])
         else:
-            getattr(named[name], rest[0])(*[int(number) for number in rest[1:]])
-
-    write_vec = pltpu.make_async_copy(vec, vec_out, local_sems.at[8])
-    write_vec.start()
-    for item in lines:
-        if item is not named["le00"]:
+            method = {"in": "inward"}.get(rest[0], rest[0])
+            getattr(named[name], method)(*[int(number) for number in rest[1:]])
+
+    pltpu.make_async_copy(vec, vec_out, local_sems.at[8]).start()
+    for name, item in named.items():
+        if isinstance(item, Line) and name + ".arrived" not in ORDER:
             item.arrived()
-    wait_small(exchanged)
-    own_dense().wait()
-    for item in [hid_line, gra_line] + lines + squares + [tree] + folds:
-        item.sent()
+    for name, item in named.items():
+        if not isinstance(item, Sink) and name + ".sent" not in ORDER:
+            item.sent()
     for copy, _, _ in small:
         copy.wait_send()
-    write_vec.wait()
+    pltpu.make_async_copy(vec, vec_out, local_sems.at[8]).wait()
 
 
 DOWN_CUTS = ((512, False), (512, False), (1024, True))
@@ -1041,27 +1091,32 @@
 DENSE_CUTS = ((512, False),)
 
 ORDER = (
-    "wu.start", "hid.start", "gra.start", "small_start", "hid.land.1", "wu.forward", "gra.land.1", "wd.start",
-    "hid.land.2", "hid.land.3", "small_land", "wd.forward", "wu.arrived", "hid.arrived", "norm_two", "gra.land.2",
-    "feed_forward", "gra.land.3", "gra.arrived", "down_grad.2", "fd2.send.3", "wd.arrived", "feed_back", "up_grad.0",
-    "fu0.send.3", "fd2.middle.1", "fd2.middle.0", "fu0.send.2", "down_grad.1", "fd2.finish.1", "ld21.start",
-    "fu0.middle.1", "fd2.finish.0", "fu0.send.1", "ld20.start", "fd1.middle.0", "fu0.finish.1", "lu01.start",
-    "fu0.send.0", "ld21.land.1", "fd1.send.3", "down_grad.0", "ld20.land.1", "fd0.send.3", "fd1.middle.1",
-    "fu0.middle.0", "wq.start", "lu01.land.1", "fu0.finish.0", "ld20.land.2", "lu00.start", "ld20.land.3",
-    "wq.forward", "fd1.finish.0", "fd0.middle.1", "fd0.middle.0", "wt.start", "lu01.land.2", "lu00.land.1",
-    "up_grad.1", "fu1.send.3", "lu00.land.2", "fd1.finish.1", "ld10.start", "fd0.finish.1", "fd0.finish.0",
-    "ld00.start", "ld10.land.1", "norm_one", "wq.arrived", "wt.forward", "project", "ld00.land.1", "attend",
-    "ld21.land.2", "fu1.send.1", "fu1.send.0", "ld10.land.2", "fu1.send.2", "dense_grad", "ld00.land.2",
-    "wt.arrived", "attend_back", "fe0.send.1", "fu1.middle.1", "fu1.middle.0", "qkv_grad.0", "fq0.send.1",
-    "fq0.send.3", "fu1.finish.0", "lu10.start", "fq0.send.0", "ld21.land.3", "fq0.send.2", "fu1.finish.1",
-    "lu11.start", "output", "so.start", "lu10.land.1", "fq0.middle.0", "fq0.middle.1", "lu11.land.1", "lu01.land.3",
-    "lu10.land.2", "so.swap", "so.step.1", "fq0.finish.0", "lq00.start", "fq0.finish.1", "lq01.start", "lu11.land.2",
-    "fe0.send.3", "inputs", "sums_start", "ld00.land.3", "lq00.land.1", "so.step.2", "fe0.send.2", "si.start",
-    "sums_land", "ls.start", "fe0.middle.1", "lu11.land.3", "lu00.land.3", "fe0.send.0", "fe0.middle.0",
-    "lq01.land.1", "fe0.finish.1", "fe0.finish.0", "le00.start", "si.swap", "ls.land.1", "lu10.land.3", "si.step.1",
-    "lq00.land.2", "le00.land.1", "si.step.2", "ls.land.2", "ls.land.3", "le00.land.2", "so.step.3", "ld10.land.3",
-    "si.step.3", "lq00.land.3", "le00.land.3", "lq01.land.2", "le00.arrived", "exchange", "output_done",
-    "input_done", "lq01.land.3",
+    "wd.start.0", "hid.start", "wu.start.0", "gra.start", "wu.start.1", "hid.out.1", "small_start", "wu.forward",
+    "gra.out.1", "wd.forward", "hid.in.1", "gra.in.1", "wd.start.1", "hid.out.2", "hid.out.3", "gra.out.2",
+    "small_land", "hid.arrived", "norm_two", "wu.arrived", "feed_forward", "gra.out.3", "gra.arrived", "down_grad.2",
+    "fd2.middle.1", "wd.arrived", "down_grad.1", "fd2.middle.0", "fd1.middle.1", "wq.start.0", "fd2.finish.1",
+    "ld21.start", "fd1.middle.0", "fd2.finish.0", "ld20.start", "down_grad.0", "ld21.out.1", "fd1.finish.1",
+    "ld21.in.1", "ld20.out.1", "fd1.finish.0", "ld10.start", "wq.start.1", "feed_back", "up_grad.0", "fu0.send.1",
+    "fu0.send.3", "ld21.out.2", "ld10.out.1", "ld20.in.1", "wd.sent", "fd0.middle.0", "fd0.middle.1", "fu0.send.2",
+    "ld21.out.3", "fu0.middle.1", "wq.forward", "ld20.out.2", "ld10.in.1", "fd0.finish.0", "fd2.sent",
+    "fd0.finish.1", "ld00.start", "wt.start", "fu0.finish.1", "lu01.start", "fu0.send.0", "up_grad.1", "fu1.send.1",
+    "fu1.send.3", "norm_one", "fu0.middle.0", "ld10.out.2", "lu01.out.1", "wq.arrived", "ld00.in.1", "ld00.out.1",
+    "project", "attend", "wt.forward", "dense_grad", "fe0.send.3", "lu01.in.1", "fu1.send.2", "fe0.send.1",
+    "fu1.middle.1", "ld00.out.2", "ld21.arrived", "fu0.finish.0", "lu00.start", "wt.back", "fe0.send.0",
+    "fu1.middle.0", "ld00.out.3", "fe0.middle.1", "hid.sent", "fe0.middle.0", "lu00.out.1", "lu01.out.2",
+    "fu1.send.0", "wq.sent", "fu1.finish.1", "lu11.start", "fe0.send.2", "wt.arrived", "attend_back", "qkv_grad.0",
+    "fq0.send.3", "fq0.send.1", "lu11.out.1", "lu00.in.1", "fe0.finish.1", "fe0.finish.0", "le00.start",
+    "fq0.send.0", "fq0.send.2", "fu1.finish.0", "lu10.start", "fq0.middle.0", "output", "so.start", "lu10.out.1",
+    "fq0.middle.1", "le00.in.1", "fd0.sent", "ld10.out.3", "lu10.in.1", "le00.out.1", "so.swap", "so.in.1",
+    "fq0.finish.0", "lu11.in.1", "lq00.start", "le00.out.2", "fq0.finish.1", "lu10.out.2", "lq01.start", "fu1.sent",
+    "inputs", "sums_start", "sums_land", "ld00.arrived", "ls.start", "lu01.out.3", "si.start", "ld20.out.3",
+    "so.in.2", "gra.sent", "fe0.sent", "le00.out.3", "wu.sent", "ld10.arrived", "ld10.sent", "lu00.out.2",
+    "ld20.arrived", "lu11.out.2", "lq01.in.1", "le00.arrived", "ls.in.1", "le00.sent", "lu01.arrived", "si.swap",
+    "fd1.sent", "lu10.out.3", "exchange", "lu10.arrived", "lu10.sent", "lq01.out.1", "lu00.out.3", "si.in.1",
+    "lu11.out.3", "ld00.sent", "ls.out.1", "lq00.out.1", "lu00.arrived", "lq00.in.1", "lu00.sent", "fu0.sent",
+    "output_done", "lu01.sent", "si.in.2", "ld21.sent", "ls.out.2", "lu11.arrived", "lq01.out.2", "ld20.sent",
+    "lu11.sent", "ls.out.3", "relay", "ls.arrived", "wt.sent", "ls.sent", "lq00.out.2", "input_done", "relay_done",
+    "lq01.out.3", "lq01.arrived", "lq00.out.3", "lq01.sent", "fq0.sent", "lq00.arrived", "lq00.sent",
 )
 
 
@@ -1095,7 +1150,8 @@
     line = (tokens, width)
     hops = (2 * (chips - 1) * tokens, width)
     outs = [
-        (vec_shape, f32), (line, f32), (line, f32), ((count * part, width), bf16), ((count * rows, units), bf16),
+        (vec_shape, f32), (line, f32), (line, f32), ((2 * tokens, width), bf16), ((2 * tokens, width), bf16),
+        ((count * part, width), bf16), ((count * rows, units), bf16),
         ((count * rows, joint), bf16), ((width, rows), bf16), ((count * 8, width), f32),
         ((units, width), bf16), ((width, units), bf16), ((width, joint), bf16), ((shards * head_dim, rows), bf16),
         ((3 * part, width), bf16), ((3 * rows, units), bf16), ((3 * rows, joint), bf16), ((3 * head_dim, rows), bf16),
@@ -1121,7 +1177,7 @@
     scratch += [((2, tokens, width), bf16), ((2, tokens, width), bf16), (line, f32)]
     slots = (
         (3 + sum(1 + split for _, split in cuts)) * Line.slots(chips)
-        + 3 * Square.SLOTS + Tree.SLOTS + len(cuts) * Fold.SLOTS + 2 * Sink.slots(chips) + 9 + count - 1
+        + 3 * Square.SLOTS + Tree.SLOTS + len(cuts) * Fold.SLOTS + 2 * Sink.slots(chips) + 12 + count - 1
     )
     outputs = pl.pallas_call(
         functools.partial(block_kernel, (chips, shards, part)),
@@ -1139,19 +1195,18 @@
         ),
         name="whole_block",
     )(hidden, grad, fc1, fc2, qkv, dense, segs, jnp.asarray(table), *vectors)
-    return outputs[:8]
-
-
-FINISH_STEPS = 16
-
-
-def finish_kernel(
+    return outputs[:10]
+
+
+FINISH_STEPS = 8
+
+
+def widen_kernel(
     sizes,
-    up_all, qkv_all, dense_all, down_all, vec, branch, back, hidden, grad, sums,
-    output, input_grad, gain_one, shift_one, qkv, qkv_bias, dense, columns_one, gain_two, shift_two, up, up_bias,
-    down, columns_two,
+    up_all, qkv_all, dense_all, down_all, sums,
+    gain_one, shift_one, qkv, qkv_bias, dense, columns_one, gain_two, shift_two, up, up_bias, down, columns_two,
 ):
-    count, shards = sizes
+    count, shards, width = sizes
     f32 = jnp.float32
 
     def spread(src, dst, pieces):
@@ -1168,18 +1223,6 @@
 
     @pl.when(pl.program_id(0) == 0)
     def _():
-        own = hidden[...].astype(f32)
-        shift = jnp.concatenate([vec[index, 4] + vec[index, 5] for index in range(shards)], axis=1)
-        output[...] = (own + branch[...] + shift).astype(output.dtype)
-        scaled, spread_own = centred(own)
-        e = back[...]
-        part = spread_own * (
-            e
-            - jnp.mean(e, axis=-1, keepdims=True)
-            - scaled * jnp.mean(e * scaled, axis=-1, keepdims=True)
-        )
-        input_grad[...] = (grad[...].astype(f32) + part).astype(input_grad.dtype)
-
         shard = lax.axis_index("fsdp")
         rows = gain_one.shape[1]
         mine = pl.ds(pl.multiple_of(shard * rows, rows), rows)
@@ -1194,7 +1237,7 @@
         here = pl.ds(pl.multiple_of(shard * part, part), part)
         for index in range(count):
             up_bias[:, index * part : (index + 1) * part] = sums[index, 3:4, here]
-        size = 3 * hidden.shape[1] // (3 * count)
+        size = width // count
         chunks = qkv_bias.shape[1] // size
         for chunk in range(chunks):
             place = shard * chunks + chunk
@@ -1204,57 +1247,93 @@
             ]
 
 
-def finish(up_all, qkv_all, dense_all, down_all, vec, branch, back, hidden, grad, sums):
+def sliced(shape, steps):
+    block = shape[:-2] + (shape[-2] // steps, shape[-1])
+    return pl.BlockSpec(block, lambda index: (0,) * (len(shape) - 2) + (index, 0))
+
+
+def entire(shape, _=None):
+    return pl.BlockSpec(shape, lambda index: (0,) * len(shape))
+
+
+def widen(up_all, qkv_all, dense_all, down_all, sums, width):
     count, shards = lax.axis_size("ctx"), lax.axis_size("fsdp")
-    tokens, width = hidden.shape
     rows = width // shards
     f32 = jnp.float32
     steps = FINISH_STEPS
-
-    def sliced(shape):
-        block = shape[:-2] + (shape[-2] // steps, shape[-1])
-        return pl.BlockSpec(block, lambda index: (0,) * (len(shape) - 2) + (index, 0))
-
-    def entire(shape):
-        return pl.BlockSpec(shape, lambda index: (0,) * len(shape))
-
     grads = [
         up_all.reshape(count, rows, -1), qkv_all.reshape(count, rows, -1), dense_all.reshape(shards, rows, rows),
         down_all,
     ]
     units = up_all.shape[1] * count
     sums = sums.reshape(count, 8, width)
-    others = [vec, branch, back, hidden, grad, sums]
     vector = (1, rows)
     outs = [
-        ((tokens, width), hidden.dtype, entire), ((tokens, width), hidden.dtype, entire),
-        (vector, f32, entire), (vector, f32, entire), ((rows, 3 * width), f32, sliced),
-        ((1, 3 * rows), f32, entire), ((rows, width), f32, sliced), (vector, f32, entire),
-        (vector, f32, entire), (vector, f32, entire), ((rows, units), f32, sliced),
-        ((1, units // shards), f32, entire), (down_all.shape, f32, sliced), (vector, f32, entire),
+        (vector, entire), (vector, entire), ((rows, 3 * width), sliced), ((1, 3 * rows), entire),
+        ((rows, width), sliced), (vector, entire), (vector, entire), (vector, entire), ((rows, units), sliced),
+        ((1, units // shards), entire), (down_all.shape, sliced), (vector, entire),
     ]
+    size = sum(math.prod(shape) for shape, _ in outs)
     return pl.pallas_call(
-        functools.partial(finish_kernel, (count, shards)),
+        functools.partial(widen_kernel, (count, shards, width)),
         grid=(steps,),
-        in_specs=[sliced(array.shape) for array in grads] + [entire(array.shape) for array in others],
-        out_specs=[kind(shape) for shape, _, kind in outs],
-        out_shape=[jax.ShapeDtypeStruct(shape, dtype) for shape, dtype, _ in outs],
+        in_specs=[sliced(array.shape, steps) for array in grads] + [entire(sums.shape)],
+        out_specs=[kind(shape, steps) for shape, kind in outs],
+        out_shape=[jax.ShapeDtypeStruct(shape, f32) for shape, _ in outs],
         compiler_params=pltpu.CompilerParams(vmem_limit_bytes=62 * 2**20),
-        name="finish",
-    )(*grads, *others)
+        cost_estimate=pl.CostEstimate(flops=size, bytes_accessed=6 * size, transcendentals=0),
+        name="widen",
+    )(*grads, sums)
+
+
+def close_kernel(shards, vec, branch, back, upward, downward, hidden, grad, output, input_grad):
+    f32 = jnp.float32
+    own = hidden[...].astype(f32)
+    shift = jnp.concatenate([vec[index, 4] + vec[index, 5] for index in range(shards)], axis=1)
+
+    def total(ref, index):
+        return ref[...] + upward[index].astype(f32) + downward[index].astype(f32)
+
+    output[...] = (own + total(branch, 0) + shift).astype(output.dtype)
+    scaled, spread = centred(own)
+    e = total(back, 1)
+    part = spread * (
+        e
+        - jnp.mean(e, axis=-1, keepdims=True)
+        - scaled * jnp.mean(e * scaled, axis=-1, keepdims=True)
+    )
+    input_grad[...] = (grad[...].astype(f32) + part).astype(input_grad.dtype)
+
+
+def close(vec, branch, back, upward, downward, hidden, grad):
+    steps = 4
+    shape = hidden.shape
+    both = (2,) + shape
+    wide = sliced(shape, steps)
+    return pl.pallas_call(
+        functools.partial(close_kernel, lax.axis_size("fsdp")),
+        grid=(steps,),
+        in_specs=[entire(vec.shape), wide, wide, sliced(both, steps), sliced(both, steps), wide, wide],
+        out_specs=[wide, wide],
+        out_shape=[jax.ShapeDtypeStruct(shape, hidden.dtype)] * 2,
+        compiler_params=pltpu.CompilerParams(vmem_limit_bytes=62 * 2**20),
+        name="close",
+    )(vec, branch, back, upward.reshape(both), downward.reshape(both), hidden, grad)
 
 
 def one_kernel(
     hidden, qkv_weight, dense_weight, fc1_weight, fc2_weight, segments, out_grad, vectors
 ):
-    vec, branch, back, down_all, up_all, qkv_all, dense_all, sums_all = whole_block(
+    vec, branch, back, up_out, down_out, down_all, up_all, qkv_all, dense_all, sums_all = whole_block(
         hidden[0], out_grad[0], fc1_weight, fc2_weight, qkv_weight, dense_weight, segments, vectors
     )
-    outs = finish(
-        up_all, qkv_all, dense_all, down_all, vec, branch, back, hidden[0], out_grad[0], sums_all
-    )
+    count = lax.axis_size("ctx")
+    upward = lax.ppermute(up_out, "ctx", [(index, index + CORES) for index in range(count - CORES)])
+    downward = lax.ppermute(down_out, "ctx", [(index + CORES, index) for index in range(count - CORES)])
+    outs = widen(up_all, qkv_all, dense_all, down_all, sums_all, hidden.shape[2])
     outs = [out.reshape(-1) if out.shape[0] == 1 else out for out in outs]
-    return (outs[0][None], outs[1][None], *outs[2:])
+    output, input_grad = close(vec, branch, back, upward, downward, hidden[0], out_grad[0])
+    return (output[None], input_grad[None], *outs)
 
 
 def per_device(

time: 369 us -> 349 us (0.946)
  Pallas kernels: 364 us -> 341 us
    pallas_call x1, Pallas kernels: 335 us -> 310 us  [whole_block(): pl.pallas_call(functools.partial(block_kernel, (chips, shards, part)), ou...]
    pallas_call x1 -> x2, Pallas kernels: 29.1 us -> 30.4 us  [the longest x1 25.7 us: widen(): pl.pallas_call(functools.partial(widen_kernel, (count, shards, width)), g...]
  transfers between devices with their start and end apart: 0 -> 2, of which waited for: 0 -> 0; matrix products, arithmetic and copies ran while one was open for 0% -> 0% of each run, Pallas kernels for 0% -> 7%
where the time goes in v5:
time: 349 us; the launch traced here: 347 us
  Pallas kernels  341 us (98%)
    pallas_call x1, Pallas kernels, whole_block(): pl.pallas_call(functools.partial(block_kernel, (chips, shards, part)), ou...  310 us
    pallas_call x1, Pallas kernels, widen(): pl.pallas_call(functools.partial(widen_kernel, (count, shards, width)), g...  25.7 us
  transfers between devices with their start and end apart: 2, of which 0 were waited for; matrix products, arithmetic and copies ran while one was open for 0% of the time, Pallas kernels for 7%

profile of v5, /device:TPU:0, one launch (start us, length us, event | category | flops | bytes accessed | tf_op | source)
XLA Modules:
  0.0 347.4 jit_solution(8328103840364379229)
XLA Ops:
  0.6 1.3 reshape.100.qkv_bias
  1.9 310.1 %whole_block.1 = (f32[4,13,1,512]{3,2,1,0:T(1,128)}, f32[128,2048]{1,0:T(8,128)}, f32[128,2048]{1,0:T(8,128)}, bf16[256,2048]{1,0:T(8,128)(2,1)}, bf16[256,2048]...) custom-call(bf16[128,2048]{1,0:T(8,128)(2,1)} %bitcast.27, ...), custom_call_target="tpu_custom_call" | custom-call | tf_op jit(solution)/shard_map/whole_block/pallas_call | solution.py:1182
  312.0 1.4 collective-permute-start
  313.4 1.3 collective-permute-start.1
  314.7 25.7 %widen.1 = (f32[1,512]{1,0:T(1,128)}, f32[1,512]{1,0:T(1,128)}, f32[512,6144]{1,0:T(8,128)}, f32[1,1536]{1,0:T(1,128)}, f32[512,2048]{1,0:T(8,128)}, /*index=5*/...) custom-call(bf16[8,512,1024]{2,1,0:T(8,128)(2,1)} %bitcast.24, ...), custom_call_target="tpu_custom_call" | custom-call | flops 12589568 | bytes 75537408 | tf_op jit(solution)/shard_map/widen/pallas_call | solution.py:1277
  340.4 1.3 reduce
  341.7 0.0 collective-permute-done
  341.7 0.0 copy-start
  341.7 0.0 collective-permute-done.1
  341.7 0.9 copy-done
  342.6 4.8 %close.1 = (bf16[128,2048]{1,0:T(8,128)(2,1)}, bf16[128,2048]{1,0:T(8,128)(2,1)}) custom-call(f32[4,13,1,512]{3,2,1,0:T(1,128)} %get-tuple-element.38.vec, f32[128,2048]{1,0:T(8,128)} %get-tuple-element.39.branch, f32[128,2048]{1,0:T(8,128)} %get-tuple-element.40.back, bf16[2,128,2048]{2,1,0:T(8,128)(2,1)} %bitcast.31, ...), custom_call_target="tpu_custom_call" | custom-call | tf_op jit(solution)/shard_map/close/pallas_call | solution.py:1313
Async XLA Ops:
  312.0 29.7 %collective-permute-start = (bf16[256,2048]{1,0:T(8,128)(2,1)}, bf16[256,2048]{1,0:T(8,128)(2,1)S(1)}, u32[]{:S(2)}, u32[]{:S(2)}) collective-permute-start(bf16[256,2048]{1,0:T(8,128)(2,1)} %get-tuple-element.41), channel_id=1, source_target_pairs={{0,8},{4,12},{8,16},{12,20},{16,24},{20,28},{1,9},{5,13},{9,17},{1... | collective-permute-start | bytes 3145736 | tf_op jit(solution)/shard_map/ppermute | solution.py:1331
  313.4 28.3 %collective-permute-start.1 = (bf16[256,2048]{1,0:T(8,128)(2,1)}, bf16[256,2048]{1,0:T(8,128)(2,1)}, u32[]{:S(2)}, u32[]{:S(2)}) collective-permute-start(bf16[256,2048]{1,0:T(8,128)(2,1)} %get-tuple-element.42), channel_id=1, source_target_pairs={{8,0},{12,4},{16,8},{20,12},{24,16},{28,20},{9,1},{13,5},{17,9},{2... | collective-permute-start | bytes 3145736 | tf_op jit(solution)/shard_map/ppermute | solution.py:1332
  341.7 0.9 copy-start

commit v6 on v3

--- a/solution.py
+++ b/solution.py
@@ -569,7 +569,8 @@
 
 def block_kernel(
     sizes,
-    hidden, grad, fc1, fc2, qkv, dense, vectors, segs, tables,
+    hidden, grad, fc1, fc2, qkv, dense, segs, tables,
+    ln1_gain, ln1_bias, ln2_gain, ln2_bias, dense_bias, fc2_bias, qkv_bias, fc1_bias,
     vec_out, output_out, input_out, down_all, up_all, qkv_all, dense_all, sums_all,
     down_parts, up_parts, qkv_parts, dense_parts, down_land, up_land, qkv_land, dense_land,
     out_parts, out_swap, out_land, in_parts, in_swap, in_land, dense_lines,
@@ -588,7 +589,7 @@
     width, length = hidden.shape[1], hid.shape[0]
     ff_units = w_down.shape[0]
     head_dim = w_dense.shape[0]
-    row_size = vec.shape[2]
+    row_size = vec.shape[3]
     tiles = length // TILE
     f32, bf16 = jnp.float32, jnp.bfloat16
     factor = head_dim ** (-0.5)
@@ -689,31 +690,33 @@
         slot = take(1)
         small.append((remote(src, dst, sems, slot, device), landing, slot))
 
-    seg_rows = segs.shape[0]
-
-    def seg_block(index):
-        return seg.at[pl.ds(pl.multiple_of(index * seg_rows, seg_rows), seg_rows)]
-
+    vectors = (
+        ln1_gain, ln1_bias, ln2_gain, ln2_bias, dense_bias, fc2_bias, qkv_bias, fc1_bias
+    )
+    at, pairs = 0, [(segs, seg.at[ctx]), (tables, table)]
+    for vector in vectors:
+        pairs.append((vector, vec.at[shard, pl.ds(at, vector.shape[0])]))
+        at += vector.shape[0]
+    locals_in = [
+        pltpu.make_async_copy(src, dst, local_sems.at[8 + index])
+        for index, (src, dst) in enumerate(pairs)
+    ]
+    for copy in locals_in:
+        copy.start()
+
+    hid_line.start()
+    up_square.start()
+    for copy in locals_in:
+        copy.wait()
     for bit in (1, 2, 3):
-        send_small(vectors, vec.at[shard], vec.at[shard ^ bit], (ctx, shard ^ bit))
+        send_small(vec.at[shard], vec.at[shard], vec.at[shard ^ bit], (ctx, shard ^ bit))
     for step in range(1, count):
         send_small(
-            segs, seg_block(ctx), seg_block(lax.rem(ctx + count - step, count)),
+            segs, seg.at[ctx], seg.at[lax.rem(ctx + count - step, count)],
             (lax.rem(ctx + step, count), shard),
         )
     for copy, _, _ in small:
         copy.start()
-    locals_in = [
-        pltpu.make_async_copy(src, dst, local_sems.at[8 + index])
-        for index, (src, dst) in enumerate(
-            ((vectors, vec.at[shard]), (segs, seg_block(ctx)), (tables, table))
-        )
-    ]
-    for copy in locals_in:
-        copy.start()
-
-    hid_line.start()
-    up_square.start()
     hid_line.land(1)
     up_square.forward()
     down_square.start()
@@ -722,12 +725,10 @@
     hid_line.land(3)
     for _, landing, slot in small:
         remote(landing, landing, sems, slot, (ctx ^ 1, shard)).wait_recv()
-    for copy in locals_in:
-        copy.wait()
     hid_line.arrived()
 
     def vector(row):
-        return jnp.concatenate([vec[index, row : row + 1] for index in range(shards)], axis=1)
+        return jnp.concatenate([vec[index, row] for index in range(shards)], axis=1)
 
     def rows_of(index):
         return pl.ds(pl.multiple_of(index * TILE, TILE), TILE)
@@ -773,7 +774,7 @@
     bias_row = 9 + bias_start // row_size
     bias_column = pl.multiple_of(lax.rem(bias_start, row_size), columns)
     up_bias = jnp.concatenate(
-        [vec[index, pl.ds(bias_row, 1), pl.ds(bias_column, columns)] for index in range(shards)],
+        [vec[index, bias_row, :, pl.ds(bias_column, columns)] for index in range(shards)],
         axis=1,
     )
 
@@ -841,7 +842,8 @@
         bias_parts.append(
             vec[
                 at // per,
-                pl.ds(6 + rest // row_size, 1),
+                6 + rest // row_size,
+                :,
                 pl.ds(pl.multiple_of(lax.rem(rest, row_size), head_dim), head_dim),
             ]
         )
@@ -866,12 +868,10 @@
         keys[rows] = turn(parts[1], rows, 1.0).astype(bf16)
         values[rows] = parts[2].astype(bf16)
 
-    seg_row = jnp.concatenate(
-        [seg[index * seg_rows : index * seg_rows + 1] for index in range(count)], axis=1
-    )
+    seg_row = jnp.concatenate([seg[index] for index in range(count)], axis=1)
     side = segs.shape[1]
     for index in range(count):
-        block = seg[index * seg_rows : index * seg_rows + 1].astype(f32)
+        block = seg[index].astype(f32)
         seg_col[index * side : (index + 1) * side] = jnp.broadcast_to(block, (side, side)).T
 
     qkv_square.arrived()
@@ -1087,7 +1087,7 @@
     return table
 
 
-def whole_block(hidden, grad, fc1, fc2, qkv, dense, vectors, segs):
+def whole_block(hidden, grad, fc1, fc2, qkv, dense, segs, vectors):
     chips, shards = lax.axis_size("ctx") // CORES, lax.axis_size("fsdp")
     count = chips * CORES
     tokens, width = hidden.shape
@@ -1098,8 +1098,9 @@
     rows = width // shards
     bf16, f32 = jnp.bfloat16, jnp.float32
     wide, joint = (length, width), 3 * head_dim
-    vec_shape = (shards,) + vectors.shape
-    seg_shape = (segs.shape[0] * count, segs.shape[1])
+    vectors = [vector.reshape(-1, 1, rows) for vector in vectors]
+    vec_shape = (shards, sum(vector.shape[0] for vector in vectors), 1, rows)
+    seg_shape = (count,) + segs.shape
     line = (tokens, width)
     hops = (2 * (chips - 1) * tokens, width)
     outs = [
@@ -1133,85 +1134,135 @@
     outputs = pl.pallas_call(
         functools.partial(block_kernel, (chips, shards, part)),
         out_shape=[jax.ShapeDtypeStruct(shape, kind) for shape, kind in outs],
-        in_specs=[pl.BlockSpec(memory_space=pl.ANY)] * 9,
+        in_specs=[pl.BlockSpec(memory_space=pl.ANY)] * 16,
         out_specs=[pl.BlockSpec(memory_space=pl.ANY)] * len(outs),
         scratch_shapes=[pltpu.VMEM(shape, kind) for shape, kind in scratch]
         + [
             pltpu.SemaphoreType.DMA((slots,)),
             pltpu.SemaphoreType.DMA((slots,)),
-            pltpu.SemaphoreType.DMA((11,)),
+            pltpu.SemaphoreType.DMA((18,)),
         ],
         compiler_params=pltpu.CompilerParams(
             collective_id=0, has_side_effects=True, vmem_limit_bytes=62 * 2**20
         ),
         name="whole_block",
-    )(hidden, grad, fc1, fc2, qkv, dense, vectors, segs, jnp.asarray(table))
+    )(hidden, grad, fc1, fc2, qkv, dense, segs, jnp.asarray(table), *vectors)
     return outputs[:8]
 
 
-def widen(blocks, groups, pieces):
-    rows, size = blocks.shape[0] // groups, blocks.shape[1] // pieces
-
-    def body(src, dst):
-        dst[...] = src[...].astype(jnp.float32)
-
+FINISH_STEPS = 16
+
+
+def finish_kernel(
+    sizes,
+    up_all, qkv_all, dense_all, down_all, vec, branch, back, hidden, grad, sums,
+    output, input_grad, gain_one, shift_one, qkv, qkv_bias, dense, columns_one, gain_two, shift_two, up, up_bias,
+    down, columns_two,
+):
+    count, shards = sizes
+    f32 = jnp.float32
+
+    def spread(src, dst, pieces):
+        groups, size = src.shape[0], src.shape[2] // pieces
+        for piece in range(pieces):
+            for group in range(groups):
+                start = (piece * groups + group) * size
+                dst[:, start : start + size] = src[group, :, piece * size : (piece + 1) * size].astype(f32)
+
+    spread(up_all, up, shards)
+    spread(qkv_all, qkv, 3)
+    spread(dense_all, dense, 1)
+    down[...] = down_all[...].astype(f32)
+
+    @pl.when(pl.program_id(0) == 0)
+    def _():
+        own = hidden[...].astype(f32)
+        shift = jnp.concatenate([vec[index, 4] + vec[index, 5] for index in range(shards)], axis=1)
+        output[...] = (own + branch[...] + shift).astype(output.dtype)
+        scaled, spread_own = centred(own)
+        e = back[...]
+        part = spread_own * (
+            e
+            - jnp.mean(e, axis=-1, keepdims=True)
+            - scaled * jnp.mean(e * scaled, axis=-1, keepdims=True)
+        )
+        input_grad[...] = (grad[...].astype(f32) + part).astype(input_grad.dtype)
+
+        shard = lax.axis_index("fsdp")
+        rows = gain_one.shape[1]
+        mine = pl.ds(pl.multiple_of(shard * rows, rows), rows)
+        for row, dst in ((0, gain_two), (1, shift_two), (4, gain_one), (5, shift_one)):
+            total = sums[0, row : row + 1, mine]
+            for index in range(1, count):
+                total = total + sums[index, row : row + 1, mine]
+            dst[...] = total
+        columns_one[...] = sums[0, 2:3, mine]
+        columns_two[...] = sums[0, 2:3, mine]
+        part = up_bias.shape[1] // count
+        here = pl.ds(pl.multiple_of(shard * part, part), part)
+        for index in range(count):
+            up_bias[:, index * part : (index + 1) * part] = sums[index, 3:4, here]
+        size = 3 * hidden.shape[1] // (3 * count)
+        chunks = qkv_bias.shape[1] // size
+        for chunk in range(chunks):
+            place = shard * chunks + chunk
+            start = pl.multiple_of(place // count * size, size)
+            qkv_bias[:, chunk * size : (chunk + 1) * size] = sums[
+                lax.rem(place, count), 6:7, pl.ds(start, size)
+            ]
+
+
+def finish(up_all, qkv_all, dense_all, down_all, vec, branch, back, hidden, grad, sums):
+    count, shards = lax.axis_size("ctx"), lax.axis_size("fsdp")
+    tokens, width = hidden.shape
+    rows = width // shards
+    f32 = jnp.float32
+    steps = FINISH_STEPS
+
+    def sliced(shape):
+        block = shape[:-2] + (shape[-2] // steps, shape[-1])
+        return pl.BlockSpec(block, lambda index: (0,) * (len(shape) - 2) + (index, 0))
+
+    def entire(shape):
+        return pl.BlockSpec(shape, lambda index: (0,) * len(shape))
+
+    grads = [
+        up_all.reshape(count, rows, -1), qkv_all.reshape(count, rows, -1), dense_all.reshape(shards, rows, rows),
+        down_all,
+    ]
+    units = up_all.shape[1] * count
+    sums = sums.reshape(count, 8, width)
+    others = [vec, branch, back, hidden, grad, sums]
+    vector = (1, rows)
+    outs = [
+        ((tokens, width), hidden.dtype, entire), ((tokens, width), hidden.dtype, entire),
+        (vector, f32, entire), (vector, f32, entire), ((rows, 3 * width), f32, sliced),
+        ((1, 3 * rows), f32, entire), ((rows, width), f32, sliced), (vector, f32, entire),
+        (vector, f32, entire), (vector, f32, entire), ((rows, units), f32, sliced),
+        ((1, units // shards), f32, entire), (down_all.shape, f32, sliced), (vector, f32, entire),
+    ]
     return pl.pallas_call(
-        body,
-        grid=(groups, pieces),
-        in_specs=[pl.BlockSpec((rows, size), lambda group, piece: (group, piece))],
-        out_specs=pl.BlockSpec((rows, size), lambda group, piece: (0, piece * groups + group)),
-        out_shape=jax.ShapeDtypeStruct((rows, pieces * groups * size), jnp.float32),
-        name="widen",
-    )(blocks)
+        functools.partial(finish_kernel, (count, shards)),
+        grid=(steps,),
+        in_specs=[sliced(array.shape) for array in grads] + [entire(array.shape) for array in others],
+        out_specs=[kind(shape) for shape, _, kind in outs],
+        out_shape=[jax.ShapeDtypeStruct(shape, dtype) for shape, dtype, _ in outs],
+        compiler_params=pltpu.CompilerParams(vmem_limit_bytes=48 * 2**20),
+        name="finish",
+    )(*grads, *others)
 
 
 def one_kernel(
     hidden, qkv_weight, dense_weight, fc1_weight, fc2_weight, segments, out_grad, vectors
 ):
-    shards, count = lax.axis_size("fsdp"), lax.axis_size("ctx")
-    shard = lax.axis_index("fsdp")
-    tokens, width = hidden.shape[1], hidden.shape[2]
-    rows = width // shards
-    head_dim = width // HEADS
-    f32, bf16 = jnp.float32, jnp.bfloat16
     vec, branch, back, down_all, up_all, qkv_all, dense_all, sums_all = whole_block(
-        hidden[0], out_grad[0], fc1_weight, fc2_weight, qkv_weight, dense_weight, vectors,
-        jnp.broadcast_to(segments, (8, tokens)),
-    )
-    own = hidden[0].astype(f32)
-    shift = vec[:, 4].reshape(-1) + vec[:, 5].reshape(-1)
-    layer_output = (own + branch + shift).astype(bf16)
-    scaled, spread = centred(own)
-    input_part = spread * (
-        back
-        - jnp.mean(back, axis=-1, keepdims=True)
-        - scaled * jnp.mean(back * scaled, axis=-1, keepdims=True)
-    )
-    input_grad = (out_grad[0].astype(f32) + input_part).astype(bf16)
-    sums = sums_all.reshape(count, 8, width)
-    mine = lax.dynamic_slice_in_dim(sums, shard * rows, rows, 2)
-    totals = jnp.sum(mine, axis=0)
-    part = fc1_weight.shape[1] // count // shards
-    up_sum = lax.dynamic_slice_in_dim(sums[:, 3], shard * part, part, 1).reshape(-1)
-    joined = sums[:, 6, : 3 * head_dim].reshape(count, 3, head_dim).transpose(1, 0, 2).reshape(-1)
-    joined = lax.dynamic_slice_in_dim(joined, shard * 3 * rows, 3 * rows, 0)
-    columns = mine[0, 2]
-    return (
-        layer_output[None],
-        input_grad[None],
-        totals[4],
-        totals[5],
-        widen(qkv_all, count, 3),
-        joined,
-        widen(dense_all, shards, 1),
-        columns,
-        totals[0],
-        totals[1],
-        widen(up_all, count, shards),
-        up_sum,
-        widen(down_all, 1, 8),
-        columns,
-    )
+        hidden[0], out_grad[0], fc1_weight, fc2_weight, qkv_weight, dense_weight, segments, vectors
+    )
+    outs = finish(
+        up_all, qkv_all, dense_all, down_all, vec, branch, back, hidden[0], out_grad[0], sums_all
+    )
+    outs = [out.reshape(-1) if out.shape[0] == 1 else out for out in outs]
+    return (outs[0][None], outs[1][None], *outs[2:])
 
 
 def per_device(
@@ -1245,14 +1296,12 @@
     units = ff // shards // ctx_count
     bf16, f32 = jnp.bfloat16, jnp.float32
 
-    vectors = jnp.concatenate(
-        [ln1_gain, ln1_bias, ln2_gain, ln2_bias, dense_bias, fc2_bias, qkv_bias, fc1_bias]
-    ).reshape(-1, rows)
-    vectors = jnp.pad(vectors, ((0, -vectors.shape[0] % 8), (0, 0)))
+    vectors = [ln1_gain, ln1_bias, ln2_gain, ln2_bias, dense_bias, fc2_bias, qkv_bias, fc1_bias]
     if ctx_count == HEADS and shards == 4:
         return one_kernel(
             hidden, qkv_weight, dense_weight, fc1_weight, fc2_weight, segments, out_grad, vectors
         )
+    vectors = jnp.concatenate(vectors).reshape(-1, rows)
     vec = lax.all_gather(vectors, "fsdp", axis=0)
     query_seg = lax.all_gather(segments[0], "ctx", axis=0, tiled=True)
     up_part = lax.dynamic_index_in_dim(

time: 441 us -> 403 us (0.914)
  Pallas kernels: 414 us -> 389 us
  other arithmetic: 6.97 us -> 0.62 us
  local copies, waits for them, and re-layouts: 12.8 us -> 7.28 us
    pallas_call x4 -> x1, Pallas kernels: 50.5 us -> 26.3 us  [finish(): pl.pallas_call(functools.partial(finish_kernel, (count, shards)), grid=(s...]
where the time goes in v6:
time: 403 us; the launch traced here: 397 us
  Pallas kernels  389 us (97%)
  local copies, waits for them, and re-layouts  7.28 us (2%)
    pallas_call x1, Pallas kernels, whole_block(): pl.pallas_call(functools.partial(block_kernel, (chips, shards, part)), ou...  363 us
    pallas_call x1, Pallas kernels, finish(): pl.pallas_call(functools.partial(finish_kernel, (count, shards)), grid=(s...  26.3 us

profile of v6, /device:TPU:0, one launch (start us, length us, event | category | flops | bytes accessed | tf_op | source)
XLA Modules:
  0.0 397.4 jit_solution(1122671523175420536)
XLA Ops:
  0.6 1.3 reshape.94.qkv_bias
  1.9 0.0 copy-start.1
  1.9 0.0 copy-start.2
  1.9 362.5 %whole_block.1 = (f32[4,13,1,512]{3,2,1,0:T(1,128)}, f32[128,2048]{1,0:T(8,128)}, f32[128,2048]{1,0:T(8,128)}, bf16[2048,2048]{1,0:T(8,128)(2,1)}, bf16[4096,102...) custom-call(bf16[128,2048]{1,0:T(8,128)(2,1)} %bitcast.23, ...), custom_call_target="tpu_custom_call" | custom-call | tf_op jit(solution)/shard_map/whole_block/pallas_call | solution.py:1134
  364.5 0.0 copy-done.1
  364.5 0.0 copy-done.2
  364.5 0.0 copy-start
  364.5 1.6 copy-done
  366.1 0.0 copy-start.3
  366.1 1.2 copy-done.3
  367.3 0.0 copy-start.4
  367.3 1.2 copy-done.4
  368.5 0.0 copy-start.5
  368.5 1.0 copy-done.5
  369.6 0.0 copy-start.6
  369.6 0.9 copy-done.6
  370.5 26.3 %finish.1 = (bf16[128,2048]{1,0:T(8,128)(2,1)}, bf16[128,2048]{1,0:T(8,128)(2,1)}, f32[1,512]{1,0:T(1,128)}, f32[1,512]{1,0:T(1,128)}, f32[512,6144]{1,0:T(8,128...) custom-call(bf16[8,512,1024]{2,1,0:T(8,128)(2,1)} %bitcast.28, ...), custom_call_target="tpu_custom_call" | custom-call | tf_op jit(solution)/shard_map/finish/pallas_call | solution.py:1244
  396.8 0.6 reduce
Async XLA Ops:
  1.9 362.5 %copy-start.1 = (bf16[1,128,2048]{2,1,0:T(8,128)(2,1)S(1)}, bf16[1,128,2048]{2,1,0:T(8,128)(2,1)}, u32[]{:S(2)}) copy-start(bf16[1,128,2048]{2,1,0:T(8,128)(2,1)} %param.16) | copy-start | bytes 1572868
  1.9 362.5 %copy-start.2 = (bf16[1,128,2048]{2,1,0:T(8,128)(2,1)S(1)}, bf16[1,128,2048]{2,1,0:T(8,128)(2,1)}, u32[]{:S(2)}) copy-start(bf16[1,128,2048]{2,1,0:T(8,128)(2,1)} %param.30) | copy-start | bytes 1572868
  364.5 1.6 copy-start
  366.1 1.2 copy-start.3
  367.3 1.2 copy-start.4
  368.5 1.0 copy-start.5
  369.6 0.9 copy-start.6

commit v7 on v5

--- a/solution.py
+++ b/solution.py
@@ -601,7 +601,7 @@
     sizes,
     hidden, grad, fc1, fc2, qkv, dense, segs, tables,
     ln1_gain, ln1_bias, ln2_gain, ln2_bias, dense_bias, fc2_bias, qkv_bias, fc1_bias,
-    vec_out, output_out, input_out, up_out, down_out, down_all, up_all, qkv_all, dense_all, sums_all,
+    output_out, input_out, up_out, down_out, down_all, up_all, qkv_all, dense_all, sums_all,
     down_parts, up_parts, qkv_parts, dense_parts, down_land, up_land, qkv_land, dense_land,
     out_parts, out_swap, out_land, in_parts, in_swap, in_land, dense_lines,
     hid, gra, norm, w_up, w_down, w_qkv, w_dense, vec, seg, seg_col, table,
@@ -739,8 +739,8 @@
     at, pairs = 0, [(segs, seg.at[ctx]), (tables, table)]
     for vector in vectors:
         size = vec.shape[3]
-        for start in range(0, vector.shape[1], size):
-            pairs.append((vector.at[:, pl.ds(start, size)], vec.at[shard, at]))
+        for start in range(0, vector.shape[0], size):
+            pairs.append((vector.at[pl.ds(start, size)], vec.at[shard, at, 0]))
             at += 1
     locals_in = [
         pltpu.make_async_copy(src, dst, local_sems.at[8 + index])
@@ -1012,6 +1012,7 @@
         for index in range(1, shards):
             total = total + sums_got[index]
         sums_tot[...] = total
+        sums_tot[7:8] = vector(4) + vector(5)
 
     exchanged = []
 
@@ -1070,10 +1071,15 @@
         if name in steps:
             steps[name](*[int(number) for number in rest])
         else:
-            method = {"in": "inward"}.get(rest[0], rest[0])
-            getattr(named[name], method)(*[int(number) for number in rest[1:]])
-
-    pltpu.make_async_copy(vec, vec_out, local_sems.at[8]).start()
+            method = getattr(named[name], {"in": "inward"}.get(rest[0], rest[0]))
+            numbers = [int(number) for number in rest[1:] if number.isdigit()]
+            if rest[-1] in WHERE:
+                pl.when(((chip == 0) | (chip == chips - 1)) == WHERE[rest[-1]])(
+                    functools.partial(method, *numbers)
+                )
+            else:
+                method(*numbers)
+
     for name, item in named.items():
         if isinstance(item, Line) and name + ".arrived" not in ORDER:
             item.arrived()
@@ -1082,7 +1088,6 @@
             item.sent()
     for copy, _, _ in small:
         copy.wait_send()
-    pltpu.make_async_copy(vec, vec_out, local_sems.at[8]).wait()
 
 
 DOWN_CUTS = ((512, False), (512, False), (1024, True))
@@ -1090,33 +1095,37 @@
 QKV_CUTS = ((768, True),)
 DENSE_CUTS = ((512, False),)
 
+WHERE = {"e": True, "m": False}
+
 ORDER = (
-    "wd.start.0", "hid.start", "wu.start.0", "gra.start", "wu.start.1", "hid.out.1", "small_start", "wu.forward",
-    "gra.out.1", "wd.forward", "hid.in.1", "gra.in.1", "wd.start.1", "hid.out.2", "hid.out.3", "gra.out.2",
-    "small_land", "hid.arrived", "norm_two", "wu.arrived", "feed_forward", "gra.out.3", "gra.arrived", "down_grad.2",
-    "fd2.middle.1", "wd.arrived", "down_grad.1", "fd2.middle.0", "fd1.middle.1", "wq.start.0", "fd2.finish.1",
-    "ld21.start", "fd1.middle.0", "fd2.finish.0", "ld20.start", "down_grad.0", "ld21.out.1", "fd1.finish.1",
-    "ld21.in.1", "ld20.out.1", "fd1.finish.0", "ld10.start", "wq.start.1", "feed_back", "up_grad.0", "fu0.send.1",
-    "fu0.send.3", "ld21.out.2", "ld10.out.1", "ld20.in.1", "wd.sent", "fd0.middle.0", "fd0.middle.1", "fu0.send.2",
-    "ld21.out.3", "fu0.middle.1", "wq.forward", "ld20.out.2", "ld10.in.1", "fd0.finish.0", "fd2.sent",
-    "fd0.finish.1", "ld00.start", "wt.start", "fu0.finish.1", "lu01.start", "fu0.send.0", "up_grad.1", "fu1.send.1",
-    "fu1.send.3", "norm_one", "fu0.middle.0", "ld10.out.2", "lu01.out.1", "wq.arrived", "ld00.in.1", "ld00.out.1",
-    "project", "attend", "wt.forward", "dense_grad", "fe0.send.3", "lu01.in.1", "fu1.send.2", "fe0.send.1",
-    "fu1.middle.1", "ld00.out.2", "ld21.arrived", "fu0.finish.0", "lu00.start", "wt.back", "fe0.send.0",
-    "fu1.middle.0", "ld00.out.3", "fe0.middle.1", "hid.sent", "fe0.middle.0", "lu00.out.1", "lu01.out.2",
-    "fu1.send.0", "wq.sent", "fu1.finish.1", "lu11.start", "fe0.send.2", "wt.arrived", "attend_back", "qkv_grad.0",
-    "fq0.send.3", "fq0.send.1", "lu11.out.1", "lu00.in.1", "fe0.finish.1", "fe0.finish.0", "le00.start",
-    "fq0.send.0", "fq0.send.2", "fu1.finish.0", "lu10.start", "fq0.middle.0", "output", "so.start", "lu10.out.1",
-    "fq0.middle.1", "le00.in.1", "fd0.sent", "ld10.out.3", "lu10.in.1", "le00.out.1", "so.swap", "so.in.1",
-    "fq0.finish.0", "lu11.in.1", "lq00.start", "le00.out.2", "fq0.finish.1", "lu10.out.2", "lq01.start", "fu1.sent",
-    "inputs", "sums_start", "sums_land", "ld00.arrived", "ls.start", "lu01.out.3", "si.start", "ld20.out.3",
-    "so.in.2", "gra.sent", "fe0.sent", "le00.out.3", "wu.sent", "ld10.arrived", "ld10.sent", "lu00.out.2",
-    "ld20.arrived", "lu11.out.2", "lq01.in.1", "le00.arrived", "ls.in.1", "le00.sent", "lu01.arrived", "si.swap",
-    "fd1.sent", "lu10.out.3", "exchange", "lu10.arrived", "lu10.sent", "lq01.out.1", "lu00.out.3", "si.in.1",
-    "lu11.out.3", "ld00.sent", "ls.out.1", "lq00.out.1", "lu00.arrived", "lq00.in.1", "lu00.sent", "fu0.sent",
-    "output_done", "lu01.sent", "si.in.2", "ld21.sent", "ls.out.2", "lu11.arrived", "lq01.out.2", "ld20.sent",
-    "lu11.sent", "ls.out.3", "relay", "ls.arrived", "wt.sent", "ls.sent", "lq00.out.2", "input_done", "relay_done",
-    "lq01.out.3", "lq01.arrived", "lq00.out.3", "lq01.sent", "fq0.sent", "lq00.arrived", "lq00.sent",
+    "wu.start.0", "wu.start.1", "hid.start", "small_start", "gra.start", "wd.start.0.m", "wu.forward", "hid.out.1",
+    "hid.in.1", "wd.start.0.e", "wq.start.0.e", "gra.in.1", "wd.forward.e", "gra.out.1", "hid.out.2", "hid.out.3",
+    "wq.start.1.e", "wd.forward.m", "hid.arrived", "small_land", "norm_two", "wu.arrived", "gra.out.2",
+    "feed_forward", "gra.out.3", "gra.arrived", "down_grad.0", "fd0.middle.1", "fd0.middle.0", "wd.start.1.e",
+    "wd.start.1.m", "fd0.finish.1", "fd0.finish.0", "ld00.start", "down_grad.2", "wd.arrived", "feed_back",
+    "fd2.middle.1", "fd2.middle.0", "up_grad.1", "fu1.send.0", "fu1.send.3", "ld00.out.1", "fu1.send.1",
+    "fu1.send.2", "fd2.finish.1", "ld21.start", "fd2.finish.0", "ld20.start", "down_grad.1", "ld21.out.1",
+    "fu1.middle.1", "ld00.in.1", "fu1.middle.0", "fd1.middle.1", "ld20.out.1", "fd1.middle.0", "wt.start",
+    "up_grad.0", "fu0.send.3", "fu0.send.1", "wq.forward.e", "ld00.out.2", "wq.start.0.m", "fd0.sent", "ld21.in.1",
+    "fu1.finish.0", "lu10.start", "fu1.finish.1", "lu11.start", "fd1.finish.1", "fd1.finish.0", "wt.forward",
+    "ld10.start", "lu10.out.1", "wq.start.1.m", "ld20.in.1", "wq.forward.m", "ld00.out.3", "norm_one", "lu11.out.1",
+    "lu10.in.1", "ld21.out.2", "fu0.middle.1", "fu0.send.2", "lu11.in.1", "ld20.out.2", "fu0.middle.0", "fu0.send.0",
+    "fd2.sent", "wu.sent", "ld10.in.1", "ld10.out.1", "hid.sent", "lu10.out.2", "lu11.out.2", "wt.back",
+    "wq.arrived", "project", "attend", "fu0.finish.1", "lu01.start", "dense_grad", "fu0.finish.0", "lu00.start",
+    "fe0.send.2", "fe0.send.1", "ld10.out.2", "wt.arrived", "attend_back", "fe0.send.0", "qkv_grad.0", "fq0.send.1",
+    "fe0.send.3", "lu01.out.1", "fq0.send.0", "lu00.in.1", "lu01.in.1", "inputs", "sums_start", "lu00.out.1",
+    "fe0.middle.0", "lu01.out.2", "fq0.middle.0", "fe0.middle.1", "sums_land", "ls.start", "fe0.finish.0",
+    "fe0.finish.1", "le00.start", "fu0.sent", "fq0.send.3", "si.start", "fq0.finish.0", "lq00.start", "fq0.send.2",
+    "lu01.out.3", "ld00.arrived", "si.swap", "si.in.1", "ls.out.1", "le00.out.1", "le00.in.1", "fq0.middle.1",
+    "output", "ls.in.1", "so.start", "lq00.in.1", "le00.out.2", "fq0.finish.1", "lq01.start", "ld10.out.3",
+    "ld10.arrived", "so.swap", "so.in.1", "le00.out.3", "le00.arrived", "exchange", "ls.out.2", "wt.sent",
+    "fd1.sent", "lu00.out.2", "fe0.sent", "fq0.sent", "ld20.out.3", "wd.sent", "lq01.in.1", "ld21.out.3",
+    "ld21.arrived", "ld21.sent", "lu10.out.3", "si.in.2", "lu11.out.3", "lu11.arrived", "lq01.out.1", "ls.out.3",
+    "lu00.out.3", "fu1.sent", "ld10.sent", "lu10.arrived", "lu11.sent", "lu00.arrived", "lu01.arrived", "lu01.sent",
+    "relay", "relay_done", "gra.sent", "lu00.sent", "ls.arrived", "ls.sent", "lq01.out.2", "le00.sent",
+    "ld20.arrived", "lq00.out.1", "wq.sent", "lu10.sent", "ld20.sent", "ld00.sent", "so.in.2", "input_done",
+    "lq01.out.3", "lq01.arrived", "lq00.out.2", "output_done", "lq00.out.3", "lq01.sent", "lq00.arrived",
+    "lq00.sent",
 )
 
 
@@ -1144,13 +1153,12 @@
     rows = width // shards
     bf16, f32 = jnp.bfloat16, jnp.float32
     wide, joint = (length, width), 3 * head_dim
-    vectors = [vector.reshape(1, -1) for vector in vectors]
-    vec_shape = (shards, sum(vector.shape[1] for vector in vectors) // rows, 1, rows)
+    vec_shape = (shards, sum(vector.shape[0] for vector in vectors) // rows, 1, rows)
     seg_shape = (count,) + segs.shape
     line = (tokens, width)
     hops = (2 * (chips - 1) * tokens, width)
     outs = [
-        (vec_shape, f32), (line, f32), (line, f32), ((2 * tokens, width), bf16), ((2 * tokens, width), bf16),
+        (line, f32), (line, f32), ((2 * tokens, width), bf16), ((2 * tokens, width), bf16),
         ((count * part, width), bf16), ((count * rows, units), bf16),
         ((count * rows, joint), bf16), ((width, rows), bf16), ((count * 8, width), f32),
         ((units, width), bf16), ((width, units), bf16), ((width, joint), bf16), ((shards * head_dim, rows), bf16),
@@ -1195,7 +1203,7 @@
         ),
         name="whole_block",
     )(hidden, grad, fc1, fc2, qkv, dense, segs, jnp.asarray(table), *vectors)
-    return outputs[:10]
+    return outputs[:9]
 
 
 FINISH_STEPS = 8
@@ -1238,12 +1246,12 @@
         for index in range(count):
             up_bias[:, index * part : (index + 1) * part] = sums[index, 3:4, here]
         size = width // count
-        chunks = qkv_bias.shape[1] // size
+        chunks = qkv_bias.shape[0] // size
         for chunk in range(chunks):
             place = shard * chunks + chunk
             start = pl.multiple_of(place // count * size, size)
-            qkv_bias[:, chunk * size : (chunk + 1) * size] = sums[
-                lax.rem(place, count), 6:7, pl.ds(start, size)
+            qkv_bias[chunk * size : (chunk + 1) * size] = sums[
+                lax.rem(place, count), 6, pl.ds(start, size)
             ]
 
 
@@ -1269,7 +1277,7 @@
     sums = sums.reshape(count, 8, width)
     vector = (1, rows)
     outs = [
-        (vector, entire), (vector, entire), ((rows, 3 * width), sliced), ((1, 3 * rows), entire),
+        (vector, entire), (vector, entire), ((rows, 3 * width), sliced), ((3 * rows,), entire),
         ((rows, width), sliced), (vector, entire), (vector, entire), (vector, entire), ((rows, units), sliced),
         ((1, units // shards), entire), (down_all.shape, sliced), (vector, entire),
     ]
@@ -1286,10 +1294,10 @@
     )(*grads, sums)
 
 
-def close_kernel(shards, vec, branch, back, upward, downward, hidden, grad, output, input_grad):
+def close_kernel(sums, branch, back, upward, downward, hidden, grad, output, input_grad):
     f32 = jnp.float32
     own = hidden[...].astype(f32)
-    shift = jnp.concatenate([vec[index, 4] + vec[index, 5] for index in range(shards)], axis=1)
+    shift = sums[7:8]
 
     def total(ref, index):
         return ref[...] + upward[index].astype(f32) + downward[index].astype(f32)
@@ -1305,26 +1313,26 @@
     input_grad[...] = (grad[...].astype(f32) + part).astype(input_grad.dtype)
 
 
-def close(vec, branch, back, upward, downward, hidden, grad):
-    steps = 4
+def close(sums, branch, back, upward, downward, hidden, grad):
+    steps = 2
     shape = hidden.shape
     both = (2,) + shape
     wide = sliced(shape, steps)
     return pl.pallas_call(
-        functools.partial(close_kernel, lax.axis_size("fsdp")),
+        close_kernel,
         grid=(steps,),
-        in_specs=[entire(vec.shape), wide, wide, sliced(both, steps), sliced(both, steps), wide, wide],
+        in_specs=[entire((8, shape[1])), wide, wide, sliced(both, steps), sliced(both, steps), wide, wide],
         out_specs=[wide, wide],
         out_shape=[jax.ShapeDtypeStruct(shape, hidden.dtype)] * 2,
         compiler_params=pltpu.CompilerParams(vmem_limit_bytes=62 * 2**20),
         name="close",
-    )(vec, branch, back, upward.reshape(both), downward.reshape(both), hidden, grad)
+    )(sums, branch, back, upward.reshape(both), downward.reshape(both), hidden, grad)
 
 
 def one_kernel(
     hidden, qkv_weight, dense_weight, fc1_weight, fc2_weight, segments, out_grad, vectors
 ):
-    vec, branch, back, up_out, down_out, down_all, up_all, qkv_all, dense_all, sums_all = whole_block(
+    branch, back, up_out, down_out, down_all, up_all, qkv_all, dense_all, sums_all = whole_block(
         hidden[0], out_grad[0], fc1_weight, fc2_weight, qkv_weight, dense_weight, segments, vectors
     )
     count = lax.axis_size("ctx")
@@ -1332,7 +1340,7 @@
     downward = lax.ppermute(down_out, "ctx", [(index + CORES, index) for index in range(count - CORES)])
     outs = widen(up_all, qkv_all, dense_all, down_all, sums_all, hidden.shape[2])
     outs = [out.reshape(-1) if out.shape[0] == 1 else out for out in outs]
-    output, input_grad = close(vec, branch, back, upward, downward, hidden[0], out_grad[0])
+    output, input_grad = close(sums_all, branch, back, upward, downward, hidden[0], out_grad[0])
     return (output[None], input_grad[None], *outs)
 
 

time: 349 us -> 344 us (0.986)
  Pallas kernels: 341 us -> 337 us
  transfers between devices with their start and end apart: 2 -> 2, of which waited for: 0 -> 1; matrix products, arithmetic and copies ran while one was open for 0% -> 0% of each run, Pallas kernels for 7% -> 8%
where the time goes in v7:
time: 344 us; the launch traced here: 342 us
  Pallas kernels  337 us (98%)
    pallas_call x1, Pallas kernels, whole_block(): pl.pallas_call(functools.partial(block_kernel, (chips, shards, part)), ou...  308 us
    pallas_call x1, Pallas kernels, widen(): pl.pallas_call(functools.partial(widen_kernel, (count, shards, width)), g...  25.7 us
  transfers between devices with their start and end apart: 2, of which 1 were waited for; matrix products, arithmetic and copies ran while one was open for 0% of the time, Pallas kernels for 8%

profile of v7, /device:TPU:0, one launch (start us, length us, event | category | flops | bytes accessed | tf_op | source)
XLA Modules:
  0.0 341.6 jit_solution(14343452285779733500)
XLA Ops:
  0.7 307.9 %whole_block.1 = (f32[128,2048]{1,0:T(8,128)}, f32[128,2048]{1,0:T(8,128)}, bf16[256,2048]{1,0:T(8,128)(2,1)}, bf16[256,2048]{1,0:T(8,128)(2,1)}, bf16[2048,2048...) custom-call(bf16[128,2048]{1,0:T(8,128)(2,1)} %bitcast.20, ...), custom_call_target="tpu_custom_call" | custom-call | tf_op jit(solution)/shard_map/whole_block/pallas_call | solution.py:1190
  308.6 1.4 collective-permute-start
  309.9 1.3 collective-permute-start.1
  311.2 25.7 %widen.1 = (f32[1,512]{1,0:T(1,128)}, f32[1,512]{1,0:T(1,128)}, f32[512,6144]{1,0:T(8,128)}, f32[1536]{0:T(1024)}, f32[512,2048]{1,0:T(8,128)}, /*index=5*/f32[1...) custom-call(bf16[8,512,1024]{2,1,0:T(8,128)(2,1)} %bitcast.17, ...), custom_call_target="tpu_custom_call" | custom-call | flops 12589568 | bytes 75537408 | tf_op jit(solution)/shard_map/widen/pallas_call | solution.py:1285
  336.9 0.0 collective-permute-done
  336.9 0.0 copy-start
  336.9 0.6 collective-permute-done.1
  337.6 0.3 copy-done
  337.9 3.7 %close.1 = (bf16[128,2048]{1,0:T(8,128)(2,1)}, bf16[128,2048]{1,0:T(8,128)(2,1)}) custom-call(f32[64,2048]{1,0:T(8,128)} %get-tuple-element.37.sums, f32[128,2048]{1,0:T(8,128)} %get-tuple-element.38.branch, f32[128,2048]{1,0:T(8,128)} %get-tuple-element.39.back, bf16[2,128,2048]{2,1,0:T(8,128)(2,1)} %bitcast.25, bf16[2,128,2048]{2,1,0:T(8,128)(2,1)} %bitcast.3.downward, ...), custom_call_target="tpu_custom_call" | custom-call | tf_op jit(solution)/shard_map/close/pallas_call | solution.py:1321
Async XLA Ops:
  308.6 28.4 %collective-permute-start = (bf16[256,2048]{1,0:T(8,128)(2,1)}, bf16[256,2048]{1,0:T(8,128)(2,1)S(1)}, u32[]{:S(2)}, u32[]{:S(2)}) collective-permute-start(bf16[256,2048]{1,0:T(8,128)(2,1)} %get-tuple-element.40), channel_id=1, source_target_pairs={{0,8},{4,12},{8,16},{12,20},{16,24},{20,28},{1,9},{5,13},{9,17},{1... | collective-permute-start | bytes 3145736 | tf_op jit(solution)/shard_map/ppermute | solution.py:1339
  309.9 27.7 %collective-permute-start.1 = (bf16[256,2048]{1,0:T(8,128)(2,1)}, bf16[256,2048]{1,0:T(8,128)(2,1)}, u32[]{:S(2)}, u32[]{:S(2)}) collective-permute-start(bf16[256,2048]{1,0:T(8,128)(2,1)} %get-tuple-element.41), channel_id=1, source_target_pairs={{8,0},{12,4},{16,8},{20,12},{24,16},{28,20},{9,1},{13,5},{17,9},{2... | collective-permute-start | bytes 3145736 | tf_op jit(solution)/shard_map/ppermute | solution.py:1340
  336.9 1.0 copy-start

commit v8 on v7

--- a/solution.py
+++ b/solution.py
@@ -1098,34 +1098,33 @@
 WHERE = {"e": True, "m": False}
 
 ORDER = (
-    "wu.start.0", "wu.start.1", "hid.start", "small_start", "gra.start", "wd.start.0.m", "wu.forward", "hid.out.1",
-    "hid.in.1", "wd.start.0.e", "wq.start.0.e", "gra.in.1", "wd.forward.e", "gra.out.1", "hid.out.2", "hid.out.3",
-    "wq.start.1.e", "wd.forward.m", "hid.arrived", "small_land", "norm_two", "wu.arrived", "gra.out.2",
-    "feed_forward", "gra.out.3", "gra.arrived", "down_grad.0", "fd0.middle.1", "fd0.middle.0", "wd.start.1.e",
-    "wd.start.1.m", "fd0.finish.1", "fd0.finish.0", "ld00.start", "down_grad.2", "wd.arrived", "feed_back",
-    "fd2.middle.1", "fd2.middle.0", "up_grad.1", "fu1.send.0", "fu1.send.3", "ld00.out.1", "fu1.send.1",
-    "fu1.send.2", "fd2.finish.1", "ld21.start", "fd2.finish.0", "ld20.start", "down_grad.1", "ld21.out.1",
-    "fu1.middle.1", "ld00.in.1", "fu1.middle.0", "fd1.middle.1", "ld20.out.1", "fd1.middle.0", "wt.start",
-    "up_grad.0", "fu0.send.3", "fu0.send.1", "wq.forward.e", "ld00.out.2", "wq.start.0.m", "fd0.sent", "ld21.in.1",
-    "fu1.finish.0", "lu10.start", "fu1.finish.1", "lu11.start", "fd1.finish.1", "fd1.finish.0", "wt.forward",
-    "ld10.start", "lu10.out.1", "wq.start.1.m", "ld20.in.1", "wq.forward.m", "ld00.out.3", "norm_one", "lu11.out.1",
-    "lu10.in.1", "ld21.out.2", "fu0.middle.1", "fu0.send.2", "lu11.in.1", "ld20.out.2", "fu0.middle.0", "fu0.send.0",
-    "fd2.sent", "wu.sent", "ld10.in.1", "ld10.out.1", "hid.sent", "lu10.out.2", "lu11.out.2", "wt.back",
-    "wq.arrived", "project", "attend", "fu0.finish.1", "lu01.start", "dense_grad", "fu0.finish.0", "lu00.start",
-    "fe0.send.2", "fe0.send.1", "ld10.out.2", "wt.arrived", "attend_back", "fe0.send.0", "qkv_grad.0", "fq0.send.1",
-    "fe0.send.3", "lu01.out.1", "fq0.send.0", "lu00.in.1", "lu01.in.1", "inputs", "sums_start", "lu00.out.1",
-    "fe0.middle.0", "lu01.out.2", "fq0.middle.0", "fe0.middle.1", "sums_land", "ls.start", "fe0.finish.0",
-    "fe0.finish.1", "le00.start", "fu0.sent", "fq0.send.3", "si.start", "fq0.finish.0", "lq00.start", "fq0.send.2",
-    "lu01.out.3", "ld00.arrived", "si.swap", "si.in.1", "ls.out.1", "le00.out.1", "le00.in.1", "fq0.middle.1",
-    "output", "ls.in.1", "so.start", "lq00.in.1", "le00.out.2", "fq0.finish.1", "lq01.start", "ld10.out.3",
-    "ld10.arrived", "so.swap", "so.in.1", "le00.out.3", "le00.arrived", "exchange", "ls.out.2", "wt.sent",
-    "fd1.sent", "lu00.out.2", "fe0.sent", "fq0.sent", "ld20.out.3", "wd.sent", "lq01.in.1", "ld21.out.3",
-    "ld21.arrived", "ld21.sent", "lu10.out.3", "si.in.2", "lu11.out.3", "lu11.arrived", "lq01.out.1", "ls.out.3",
-    "lu00.out.3", "fu1.sent", "ld10.sent", "lu10.arrived", "lu11.sent", "lu00.arrived", "lu01.arrived", "lu01.sent",
-    "relay", "relay_done", "gra.sent", "lu00.sent", "ls.arrived", "ls.sent", "lq01.out.2", "le00.sent",
-    "ld20.arrived", "lq00.out.1", "wq.sent", "lu10.sent", "ld20.sent", "ld00.sent", "so.in.2", "input_done",
-    "lq01.out.3", "lq01.arrived", "lq00.out.2", "output_done", "lq00.out.3", "lq01.sent", "lq00.arrived",
-    "lq00.sent",
+    "wu.start.0", "hid.start", "wu.start.1", "gra.start", "wd.start.0.e", "wu.forward", "wd.forward.e",
+    "small_start", "wq.start.0.e", "hid.out.1", "hid.in.1", "wd.start.0.m", "wd.start.1.m", "wq.start.1.e",
+    "gra.out.1", "gra.in.1", "hid.out.2", "hid.out.3", "small_land", "hid.arrived", "norm_two", "gra.out.2",
+    "wu.arrived", "feed_forward", "gra.out.3", "gra.arrived", "down_grad.0", "fd0.middle.1", "fd0.middle.0",
+    "wd.forward.m", "wd.start.1.e", "fd0.finish.1", "fd0.finish.0", "ld00.start", "down_grad.2", "wd.arrived",
+    "feed_back", "fd2.middle.1", "fd2.middle.0", "ld00.out.1", "up_grad.1", "fu1.send.3", "fu1.send.0", "fu1.send.2",
+    "fd2.finish.1", "ld21.start", "fu1.send.1", "ld00.in.1", "fd2.finish.0", "ld20.start", "fu1.middle.1",
+    "ld21.out.1", "down_grad.1", "fu1.middle.0", "wq.start.0.m", "ld00.out.2", "fu1.finish.1", "lu11.start",
+    "fd1.middle.0", "wt.start", "fd1.middle.1", "up_grad.0", "fu0.send.1", "ld21.in.1", "fu0.send.3", "ld20.out.1",
+    "wq.forward.e", "fu1.finish.0", "lu10.start", "fu1.sent", "wq.forward.m", "lu11.out.1", "ld20.in.1", "fd2.sent",
+    "wq.start.1.m", "fd1.finish.0", "fd1.finish.1", "ld10.start", "lu10.out.1", "lu11.in.1", "wt.forward",
+    "ld00.out.3", "ld10.out.1", "ld21.out.2", "fu0.send.2", "fu0.middle.1", "lu10.in.1", "norm_one", "ld20.out.2",
+    "fu0.send.0", "fu0.middle.0", "ld10.in.1", "lu10.out.2", "lu11.out.2", "wq.arrived", "project", "attend",
+    "wt.back", "dense_grad", "fe0.send.2", "fe0.send.3", "fe0.send.0", "fe0.send.1", "fu0.finish.1", "lu01.start",
+    "fu0.finish.0", "lu00.start", "wt.arrived", "attend_back", "qkv_grad.0", "fq0.send.1", "fq0.send.3",
+    "ld10.out.2", "fe0.middle.0", "lu00.out.1", "lu01.out.1", "lu00.in.1", "fe0.middle.1", "output", "fq0.middle.0",
+    "fq0.send.0", "fq0.send.2", "lu00.out.2", "lu01.in.1", "fe0.finish.1", "fe0.finish.0", "le00.start",
+    "fq0.middle.1", "so.start", "fq0.finish.0", "lq00.start", "lu00.out.3", "ld10.out.3", "so.swap", "le00.in.1",
+    "wu.sent", "so.in.1", "fd1.sent", "fq0.finish.1", "lq01.start", "le00.out.1", "inputs", "si.start", "sums_start",
+    "le00.out.2", "lq00.in.1", "sums_land", "ls.start", "si.swap", "si.in.1", "ld20.out.3", "lu01.out.2",
+    "le00.out.3", "ls.in.1", "ld21.out.3", "ld21.arrived", "lq01.in.1", "ld10.arrived", "ls.out.1", "fq0.sent",
+    "le00.arrived", "exchange", "fu0.sent", "le00.sent", "lq01.out.1", "ld21.sent", "lu10.out.3", "lu11.out.3",
+    "wq.sent", "lu00.arrived", "lu11.arrived", "lu11.sent", "lu01.out.3", "lu00.sent", "si.in.2", "ls.out.2",
+    "lu10.arrived", "lu10.sent", "fd0.sent", "ld20.arrived", "ld00.arrived", "lq01.out.2", "gra.sent", "ls.out.3",
+    "relay", "ld00.sent", "ls.arrived", "lu01.arrived", "so.in.2", "fe0.sent", "lu01.sent", "hid.sent", "relay_done",
+    "ld10.sent", "ld20.sent", "wd.sent", "ls.sent", "wt.sent", "lq00.out.1", "lq01.out.3", "input_done",
+    "lq01.arrived", "lq00.out.2", "output_done", "lq00.out.3", "lq01.sent", "lq00.arrived", "lq00.sent",
 )
 
 
@@ -1206,7 +1205,7 @@
     return outputs[:9]
 
 
-FINISH_STEPS = 8
+FINISH_STEPS = 4
 
 
 def widen_kernel(
@@ -1376,7 +1375,7 @@
     bf16, f32 = jnp.bfloat16, jnp.float32
 
     vectors = [ln1_gain, ln1_bias, ln2_gain, ln2_bias, dense_bias, fc2_bias, qkv_bias, fc1_bias]
-    if ctx_count == HEADS and shards == 4:
+    if ctx_count == HEADS and shards == 4 and width == sum(size for size, _ in DOWN_CUTS):
         return one_kernel(
             hidden, qkv_weight, dense_weight, fc1_weight, fc2_weight, segments, out_grad, vectors
         )

time: 344 us -> 341 us (level)
  Pallas kernels: 337 us -> 333 us
  transfers between devices with their start and end apart: 2 -> 2, of which waited for: 1 -> 1; matrix products, arithmetic and copies ran while one was open for 0% -> 0% of each run, Pallas kernels for 8% -> 7%
where the time goes in v8:
time: 341 us; the launch traced here: 339 us
  Pallas kernels  333 us (98%)
    pallas_call x1, Pallas kernels, whole_block(): pl.pallas_call(functools.partial(block_kernel, (chips, shards, part)), ou...  306 us
    pallas_call x1, Pallas kernels, widen(): pl.pallas_call(functools.partial(widen_kernel, (count, shards, width)), g...  23.6 us
  transfers between devices with their start and end apart: 2, of which 1 were waited for; matrix products, arithmetic and copies ran while one was open for 0% of the time, Pallas kernels for 7%

profile of v8, /device:TPU:0, one launch (start us, length us, event | category | flops | bytes accessed | tf_op | source)
XLA Modules:
  0.0 339.4 jit_solution(15634424888408825035)
XLA Ops:
  0.7 306.0 %whole_block.1 = (f32[128,2048]{1,0:T(8,128)}, f32[128,2048]{1,0:T(8,128)}, bf16[256,2048]{1,0:T(8,128)(2,1)}, bf16[256,2048]{1,0:T(8,128)(2,1)}, bf16[2048,2048...) custom-call(bf16[128,2048]{1,0:T(8,128)(2,1)} %bitcast.20, ...), custom_call_target="tpu_custom_call" | custom-call | tf_op jit(solution)/shard_map/whole_block/pallas_call | solution.py:1189
  306.7 1.4 collective-permute-start
  308.0 1.3 collective-permute-start.1
  309.3 23.6 %widen.1 = (f32[1,512]{1,0:T(1,128)}, f32[1,512]{1,0:T(1,128)}, f32[512,6144]{1,0:T(8,128)}, f32[1536]{0:T(1024)}, f32[512,2048]{1,0:T(8,128)}, /*index=5*/f32[1...) custom-call(bf16[8,512,1024]{2,1,0:T(8,128)(2,1)} %bitcast.17, ...), custom_call_target="tpu_custom_call" | custom-call | flops 12589568 | bytes 75537408 | tf_op jit(solution)/shard_map/widen/pallas_call | solution.py:1284
  332.9 0.0 collective-permute-done
  332.9 0.0 copy-start
  332.9 2.7 collective-permute-done.1
  335.7 0.0 copy-done
  335.7 3.7 %close.1 = (bf16[128,2048]{1,0:T(8,128)(2,1)}, bf16[128,2048]{1,0:T(8,128)(2,1)}) custom-call(f32[64,2048]{1,0:T(8,128)} %get-tuple-element.37.sums, f32[128,2048]{1,0:T(8,128)} %get-tuple-element.38.branch, f32[128,2048]{1,0:T(8,128)} %get-tuple-element.39.back, bf16[2,128,2048]{2,1,0:T(8,128)(2,1)} %bitcast.25, bf16[2,128,2048]{2,1,0:T(8,128)(2,1)} %bitcast.3.downward, ...), custom_call_target="tpu_custom_call" | custom-call | tf_op jit(solution)/shard_map/close/pallas_call | solution.py:1320
Async XLA Ops:
  306.7 26.3 %collective-permute-start = (bf16[256,2048]{1,0:T(8,128)(2,1)}, bf16[256,2048]{1,0:T(8,128)(2,1)S(1)}, u32[]{:S(2)}, u32[]{:S(2)}) collective-permute-start(bf16[256,2048]{1,0:T(8,128)(2,1)} %get-tuple-element.40), channel_id=1, source_target_pairs={{0,8},{4,12},{8,16},{12,20},{16,24},{20,28},{1,9},{5,13},{9,17},{1... | collective-permute-start | bytes 3145736 | tf_op jit(solution)/shard_map/ppermute | solution.py:1338
  308.0 27.7 %collective-permute-start.1 = (bf16[256,2048]{1,0:T(8,128)(2,1)}, bf16[256,2048]{1,0:T(8,128)(2,1)}, u32[]{:S(2)}, u32[]{:S(2)}) collective-permute-start(bf16[256,2048]{1,0:T(8,128)(2,1)} %get-tuple-element.41), channel_id=1, source_target_pairs={{8,0},{12,4},{16,8},{20,12},{24,16},{28,20},{9,1},{13,5},{17,9},{2... | collective-permute-start | bytes 3145736 | tf_op jit(solution)/shard_map/ppermute | solution.py:1339
  332.9 2.8 copy-start

commit v9 on v8

--- a/solution.py
+++ b/solution.py
@@ -394,16 +394,15 @@
         owner = self.shard ^ (3 if slot % 2 else bit)
         self.copy(self.part(owner, which), slot, bit).start()
 
-    def add(self, dst, sources):
-        copies = []
-        for index, source in enumerate(sources):
-            copies.append(
-                pltpu.make_async_copy(source, self.stage.at[index], self.local.at[index])
-            )
-            copies[-1].start()
+    def load(self, index, source):
+        copy = pltpu.make_async_copy(source, self.stage.at[index], self.local.at[index])
+        copy.start()
+        return copy
+
+    def add(self, dst, copies):
         for copy in copies:
             copy.wait()
-        add_rows(dst, [self.stage.at[index] for index in range(len(sources))])
+        add_rows(dst, [self.stage.at[index] for index in range(len(copies))])
 
     def wait(self, slot, bit):
         self.copy(self.landed(slot), slot, bit).wait_recv()
@@ -411,19 +410,20 @@
     def middle(self, which):
         first, second = (1, 2) if which == 0 else (2, 1)
         slot = 1 + 2 * which
+        own = self.load(0, self.part(self.shard ^ second, which))
         self.wait(slot, first)
         carry = self.carry.at[which]
-        self.add(carry, [self.part(self.shard ^ second, which), self.landed(slot)])
+        self.add(carry, [own, self.load(1, self.landed(slot))])
         self.copy(carry, 4 + which, second).start()
 
     def finish(self, which):
         first, second = (1, 2) if which == 0 else (2, 1)
+        copies = [self.load(0, self.part(self.shard, which))]
         self.wait(2 * which, first)
+        copies.append(self.load(1, self.landed(2 * which)))
         self.wait(4 + which, second)
-        self.add(
-            self.final.at[pl.ds(which * self.half, self.half)],
-            [self.part(self.shard, which), self.landed(2 * which), self.landed(4 + which)],
-        )
+        copies.append(self.load(2, self.landed(4 + which)))
+        self.add(self.final.at[pl.ds(which * self.half, self.half)], copies)
 
     def sent(self):
         for slot in range(6):

time: 341 us -> 340 us (level)
  no operation moved by 1% of the time
where the time goes in v9:
time: 340 us; the launch traced here: 339 us
  Pallas kernels  333 us (98%)
    pallas_call x1, Pallas kernels, whole_block(): pl.pallas_call(functools.partial(block_kernel, (chips, shards, part)), ou...  306 us
    pallas_call x1, Pallas kernels, widen(): pl.pallas_call(functools.partial(widen_kernel, (count, shards, width)), g...  23.6 us
  transfers between devices with their start and end apart: 2, of which 1 were waited for; matrix products, arithmetic and copies ran while one was open for 0% of the time, Pallas kernels for 7%

profile of v9, /device:TPU:0, one launch (start us, length us, event | category | flops | bytes accessed | tf_op | source)
XLA Modules:
  0.0 339.2 jit_solution(4239626261105071378)
XLA Ops:
  0.7 305.8 %whole_block.1 = (f32[128,2048]{1,0:T(8,128)}, f32[128,2048]{1,0:T(8,128)}, bf16[256,2048]{1,0:T(8,128)(2,1)}, bf16[256,2048]{1,0:T(8,128)(2,1)}, bf16[2048,2048...) custom-call(bf16[128,2048]{1,0:T(8,128)(2,1)} %bitcast.20, ...), custom_call_target="tpu_custom_call" | custom-call | tf_op jit(solution)/shard_map/whole_block/pallas_call | solution.py:1189
  306.4 1.4 collective-permute-start
  307.8 1.3 collective-permute-start.1
  309.1 23.6 %widen.1 = (f32[1,512]{1,0:T(1,128)}, f32[1,512]{1,0:T(1,128)}, f32[512,6144]{1,0:T(8,128)}, f32[1536]{0:T(1024)}, f32[512,2048]{1,0:T(8,128)}, /*index=5*/f32[1...) custom-call(bf16[8,512,1024]{2,1,0:T(8,128)(2,1)} %bitcast.17, ...), custom_call_target="tpu_custom_call" | custom-call | flops 12589568 | bytes 75537408 | tf_op jit(solution)/shard_map/widen/pallas_call | solution.py:1284
  332.7 0.0 collective-permute-done
  332.7 0.0 copy-start
  332.7 2.7 collective-permute-done.1
  335.5 0.0 copy-done
  335.5 3.7 %close.1 = (bf16[128,2048]{1,0:T(8,128)(2,1)}, bf16[128,2048]{1,0:T(8,128)(2,1)}) custom-call(f32[64,2048]{1,0:T(8,128)} %get-tuple-element.37.sums, f32[128,2048]{1,0:T(8,128)} %get-tuple-element.38.branch, f32[128,2048]{1,0:T(8,128)} %get-tuple-element.39.back, bf16[2,128,2048]{2,1,0:T(8,128)(2,1)} %bitcast.25, bf16[2,128,2048]{2,1,0:T(8,128)(2,1)} %bitcast.3.downward, ...), custom_call_target="tpu_custom_call" | custom-call | tf_op jit(solution)/shard_map/close/pallas_call | solution.py:1320
Async XLA Ops:
  306.4 26.3 %collective-permute-start = (bf16[256,2048]{1,0:T(8,128)(2,1)}, bf16[256,2048]{1,0:T(8,128)(2,1)S(1)}, u32[]{:S(2)}, u32[]{:S(2)}) collective-permute-start(bf16[256,2048]{1,0:T(8,128)(2,1)} %get-tuple-element.40), channel_id=1, source_target_pairs={{0,8},{4,12},{8,16},{12,20},{16,24},{20,28},{1,9},{5,13},{9,17},{1... | collective-permute-start | bytes 3145736 | tf_op jit(solution)/shard_map/ppermute | solution.py:1338
  307.8 27.7 %collective-permute-start.1 = (bf16[256,2048]{1,0:T(8,128)(2,1)}, bf16[256,2048]{1,0:T(8,128)(2,1)}, u32[]{:S(2)}, u32[]{:S(2)}) collective-permute-start(bf16[256,2048]{1,0:T(8,128)(2,1)} %get-tuple-element.41), channel_id=1, source_target_pairs={{8,0},{12,4},{16,8},{20,12},{24,16},{28,20},{9,1},{13,5},{17,9},{2... | collective-permute-start | bytes 3145736 | tf_op jit(solution)/shard_map/ppermute | solution.py:1339
  332.7 2.8 copy-start
